TPU v7x, 256 devices: a whole 4x4x8 slice. The times are simulated.
256 devices in a mesh: depth: 4 (over y_hi, core), row: 8 (over z), col: 8 (over y_lo, x).
Axes of the slice: x: 4, y: 4 (y_hi: 2, y_lo: 2; y = y_hi * 2 + y_lo), z: 8, core: 2. Of those that a mesh axis runs over, the one named last changes fastest.
Arguments:
- activations: bfloat16 [20480, 2048], P(('depth', 'row'), 'col'), may hold values from -6 to 6
- weight_in: bfloat16 [2048, 8192], P('row', 'col'), may hold values from -0.125 to 0.125
- weight_out: bfloat16 [8192, 2048], P('col', 'row'), may hold values from -0.0625 to 0.0625
- upstream: bfloat16 [20480, 2048], P(('depth', 'row'), 'col'), may hold values from -0.59765625 to 0.59765625
Outputs:
- grad_input: bfloat16 [20480, 2048], P(('depth', 'row'), 'col')
- grad_weight_in: float32 [2048, 8192], P('row', 'col')
- grad_weight_out: float32 [8192, 2048], P('col', 'row')
All inputs are finite; a program needn't handle non-finite values.
Results may differ from a plain program's by a relative error of at most 0.022.
Values may be sent and summed in bfloat16 or wider, within the bound.
No kernel may reach another device: no remote copies, remote signals or barrier semaphores. Data moves between devices by JAX's collectives and lax.ppermute only.
A program may use at most 128 MiB of HBM per device.

v0:
```python
import jax
import jax.numpy as jnp
from jax import lax
from jax.sharding import PartitionSpec as P


def gelu_tanh(values):
    return jax.nn.gelu(values, approximate=True)


def reorder(matrix, row_count, depth_count):
    tokens_here, width = matrix.shape
    share = width // (row_count * depth_count)
    return (
        matrix.reshape(tokens_here, row_count, depth_count, share)
        .transpose(0, 2, 1, 3)
        .reshape(tokens_here, width)
    )


def on_device(activations, weight_in, weight_out, upstream):
    inputs_full, grads_full = (
        lax.all_gather(activations, "col", axis=1, tiled=True),
        lax.all_gather(upstream, "col", axis=1, tiled=True),
    )
    weight_cols, weight_rows = (
        lax.all_gather(weight_in, "row", axis=0, tiled=True),
        lax.all_gather(weight_out, "row", axis=1, tiled=True),
    )
    pre = jnp.dot(inputs_full, weight_cols, preferred_element_type=jnp.float32)
    back = lax.dot_general(
        grads_full, weight_rows, (((1,), (1,)), ((), ())), preferred_element_type=jnp.float32
    )
    act_full, pull = jax.vjp(gelu_tanh, pre)
    dpre = pull(back)[0].astype(jnp.bfloat16)
    act = act_full.astype(jnp.bfloat16)
    partial_input = lax.dot_general(
        dpre, weight_cols, (((1,), (1,)), ((), ())), preferred_element_type=jnp.float32
    )
    grad_input = lax.psum_scatter(
        partial_input.astype(jnp.bfloat16), "col", scatter_dimension=1, tiled=True
    )
    width = inputs_full.shape[1]
    hidden_here = dpre.shape[1]
    row_count = lax.axis_size("row")
    depth_count = lax.axis_size("depth")

    def make_term(left_inputs, left_grads):

        def weight_term(offset, amount):
            first = lax.dot_general(
                left_inputs, dpre, (((0,), (0,)), ((), ())), preferred_element_type=jnp.float32
            )
            second = lax.dot_general(
                left_grads, act, (((0,), (0,)), ((), ())), preferred_element_type=jnp.float32
            )
            return jnp.concatenate([first, second], axis=1)

        return weight_term

    term = make_term(
        reorder(inputs_full, row_count, depth_count), reorder(grads_full, row_count, depth_count)
    )
    shares = lax.psum_scatter(
        term(
            jnp.int32(0), lax.axis_size(("depth", "row")) * (width // (row_count * depth_count))
        ).astype(jnp.bfloat16),
        ("depth", "row"),
        scatter_dimension=0,
        tiled=True,
    ).astype(jnp.float32)
    summed = lax.all_gather(shares.astype(jnp.bfloat16), "depth", axis=0, tiled=True).astype(
        shares.dtype
    )
    grad_weight_in = summed[:, :hidden_here]
    grad_weight_out = summed[:, hidden_here:].T
    return (grad_input, grad_weight_in, grad_weight_out)


def solution(mesh):
    return jax.shard_map(
        on_device,
        mesh=mesh,
        in_specs=(
            P(("depth", "row"), "col"),
            P("row", "col"),
            P("col", "row"),
            P(("depth", "row"), "col"),
        ),
        out_specs=(P(("depth", "row"), "col"), P("row", "col"), P("col", "row")),
        check_vma=False,
    )
```

profile of v0, /device:TPU:1, one launch (start us, length us, event | category | flops | bytes accessed | tf_op | source)
XLA Modules:
  0.0 492.0 jit_solution(12889243107371767055)
XLA Ops:
  7.2 1.9 copy.13
  9.2 1.9 copy.14
  11.1 0.7 all-gather.8.cloned.1.call-update
  11.8 0.5 all-gather.12.cloned.1.call-update
  12.4 43.4 %all-gather.6.cloned.1.call-done = bf16[640,2048]{0,1:T(8,128)(2,1)} async-done(((bf16[640,256]{0,1:T(8,128)(2,1)}), bf16[640,2048]{0,1:T(8,128)(2,1)}) %all-gather.6.cloned.1.call-update) | async-done | bytes 2621456 | tf_op jit(solution)/shard_map/all_gather | solution.py:24
  55.8 3.5 copy.16
  59.3 43.3 %all-gather.10.cloned.1.call-done = bf16[640,2048]{0,1:T(8,128)(2,1)} async-done(((bf16[640,256]{0,1:T(8,128)(2,1)}), bf16[640,2048]{0,1:T(8,128)(2,1)}) %all-gather.10.cloned.1.call-update) | async-done | bytes 2621456 | tf_op jit(solution)/shard_map/all_gather | solution.py:23
  102.6 3.7 copy.15
  106.3 60.6 %all-gather.8.cloned.1.call-done = bf16[1024,2048]{1,0:T(8,128)(2,1)} async-done(((bf16[1024,256]{1,0:T(8,128)(2,1)}), bf16[1024,2048]{1,0:T(8,128)(2,1)}) %all-gather.8.cloned.1.call-update) | async-done | bytes 4194320 | tf_op jit(solution)/shard_map/all_gather | solution.py:28
  166.9 6.6 %fusion.15 = f32[640,1024]{1,0:T(8,128)} fusion(bf16[640,2048]{0,1:T(8,128)(2,1)S(1)} %copy-done.1, bf16[1024,2048]{1,0:T(8,128)(2,1)} %all-gather.8.cloned.1.call-done), kind=kOutput, calls=%fused_computation.23 | convolution fusion | flops 2684354560 | bytes 9437184 | tf_op jit(solution)/shard_map/dot_general | solution.py:31
  173.5 51.2 %all-gather.12.cloned.1.call-done = bf16[2048,1024]{1,0:T(8,128)(2,1)} async-done(((bf16[256,1024]{1,0:T(8,128)(2,1)}), bf16[2048,1024]{1,0:T(8,128)(2,1)}) %all-gather.12.cloned.1.call-update) | async-done | bytes 4194320 | tf_op jit(solution)/shard_map/all_gather | solution.py:27
  224.7 8.2 %fusion.6 = (bf16[640,1024]{1,0:T(8,128)(2,1)S(1)}, f32[640,1024]{1,0:T(8,128)S(1)}) fusion(f32[640,1024]{1,0:T(8,128)} %fusion.15, bf16[640,2048]{0,1:T(8,128)(2,1)} %all-gather.10.cloned.1.call-done, bf16[2048,1024]{1,0:T(8,128)(2,1)} %all-gather.12.cloned.1.call-done), kind=kOutput, calls=%fused_computation.12 | convolution fusion | flops 2697461760 | bytes 13369344 | tf_op jit(solution)/shard_map/dot_general | solution.py:30
  233.0 5.7 %convert_bitcast_fusion = bf16[2048,1024]{0,1:T(8,128)(2,1)} fusion(bf16[640,2048]{0,1:T(8,128)(2,1)S(1)} %bitcast.26, f32[640,1024]{1,0:T(8,128)S(1)} %get-tuple-element.13), kind=kOutput, calls=%fused_computation.1 | convolution fusion | flops 2692349952 | bytes 9437184 | tf_op jit(solution)/shard_map/dot_general | solution.py:54
  238.7 5.1 %convert_bitcast_fusion.1 = bf16[2048,1024]{0,1:T(8,128)(2,1)} fusion(bf16[640,1024]{1,0:T(8,128)(2,1)S(1)} %get-tuple-element.12, bf16[640,2048]{0,1:T(8,128)(2,1)S(1)} %bitcast.27), kind=kOutput, calls=%fused_computation.2 | convolution fusion | flops 2686451712 | bytes 8126464 | tf_op jit(solution)/shard_map/dot_general | solution.py:51
  243.8 8.4 %pad_maximum_fusion = bf16[2048,2048]{0,1:T(8,128)(2,1)} fusion(bf16[2048,1024]{0,1:T(8,128)(2,1)} %convert_bitcast_fusion, bf16[2048,1024]{0,1:T(8,128)(2,1)} %convert_bitcast_fusion.1), kind=kLoop, calls=%fused_computation | loop fusion | flops 16777216 | bytes 16777216 | tf_op jit(solution)/shard_map/concatenate | solution.py:57
  252.2 11.9 %copy.19 = bf16[2048,2048]{1,0:T(8,128)(2,1)} copy(bf16[2048,2048]{0,1:T(8,128)(2,1)} %pad_maximum_fusion) | data formatting | bytes 16777216
  264.2 148.4 %reduce-scatter.7.cloned.1.call-done = bf16[64,2048]{1,0:T(8,128)(2,1)} async-done(((bf16[2048,2048]{1,0:T(8,128)(2,1)}), bf16[64,2048]{1,0:T(8,128)(2,1)}) %reduce-scatter.7.cloned.1.call-update) | async-done | bytes 262160 | tf_op jit(solution)/shard_map/reduce_scatter | solution.py:64
  412.7 6.4 %convolution_convert_fusion = bf16[640,2048]{1,0:T(8,128)(2,1)} fusion(bf16[640,1024]{1,0:T(8,128)(2,1)S(1)} %copy-done.5, bf16[2048,1024]{1,0:T(8,128)(2,1)} %all-gather.12.cloned.1.call-done), kind=kOutput, calls=%fused_computation.5 | convolution fusion | flops 2685665280 | bytes 8126464 | tf_op jit(solution)/shard_map/dot_general | solution.py:37
  419.2 21.4 %all-gather.14.cloned.1.call-done = bf16[256,2048]{1,0:T(8,128)(2,1)} async-done(((bf16[64,2048]{1,0:T(8,128)(2,1)}), bf16[256,2048]{1,0:T(8,128)(2,1)}) %all-gather.14.cloned.1.call-update) | async-done | bytes 1048592 | tf_op jit(solution)/shard_map/all_gather | solution.py:72
  440.6 1.5 convert_element_type.18
  442.1 0.1 slice_bitcast_fusion
  442.2 1.3 copy.18
  443.5 1.1 slice.8
  444.6 40.6 %reduce-scatter.5.cloned.1.call-done = bf16[640,256]{1,0:T(8,128)(2,1)} async-done(((bf16[640,2048]{1,0:T(8,128)(2,1)}), bf16[640,256]{1,0:T(8,128)(2,1)}) %reduce-scatter.5.cloned.1.call-update) | async-done | bytes 327696 | tf_op jit(solution)/shard_map/reduce_scatter | solution.py:40
  (24 shorter events, 0.4 us)
Async XLA Ops:
  7.2 48.6 %all-gather.6.cloned.1.call-start = ((), (), s32[]{:S(2)}) async-start(), calls=%async_computation.2 | async-start | bytes 2949120 | tf_op jit(solution)/shard_map/all_gather | solution.py:24
  9.1 93.5 %all-gather.10.cloned.1.call-start = ((), (), s32[]{:S(2)}) async-start(), calls=%async_computation.4 | async-start | bytes 2949120 | tf_op jit(solution)/shard_map/all_gather | solution.py:23
  11.0 155.9 %all-gather.8.cloned.1.call-start = ((), (), s32[]{:S(2)}) async-start(), calls=%async_computation.3 | async-start | bytes 4718592 | tf_op jit(solution)/shard_map/all_gather | solution.py:28
  11.8 212.9 %all-gather.12.cloned.1.call-start = ((), (), s32[]{:S(2)}) async-start(), calls=%async_computation.5 | async-start | bytes 4718592 | tf_op jit(solution)/shard_map/all_gather | solution.py:27
  12.4 400.3 %reduce-scatter.7.cloned.1.call-start = ((), (), s32[]{:S(2)}) async-start(), calls=%async_computation.8 | async-start | bytes 8650752 | tf_op jit(solution)/shard_map/reduce_scatter | solution.py:64
  102.6 64.3 %copy-start.1 = (bf16[640,2048]{0,1:T(8,128)(2,1)S(1)}, bf16[640,2048]{0,1:T(8,128)(2,1)}, u32[]{:S(2)}) copy-start(bf16[640,2048]{0,1:T(8,128)(2,1)} %all-gather.6.cloned.1.call-done) | copy-start | bytes 7864324
  173.5 59.4 %copy-start.2 = (bf16[640,4,8,64]{0,3,2,1:T(8,128)(2,1)S(1)}, bf16[640,4,8,64]{0,3,2,1:T(8,128)(2,1)}, u32[]{:S(2)}) copy-start(bf16[640,4,8,64]{0,3,2,1:T(8,128)(2,1)} %copy.16) | copy-start | bytes 7864324
  233.0 5.8 %copy-start.4 = (bf16[640,1024]{1,0:T(8,128)(2,1)}, bf16[640,1024]{1,0:T(8,128)(2,1)S(1)}, u32[]{:S(2)}) copy-start(bf16[640,1024]{1,0:T(8,128)(2,1)S(1)} %get-tuple-element.12) | copy-start | bytes 3932164
  233.0 5.8 %copy-start.3 = (bf16[640,4,8,64]{0,3,2,1:T(8,128)(2,1)S(1)}, bf16[640,4,8,64]{0,3,2,1:T(8,128)(2,1)}, u32[]{:S(2)}) copy-start(bf16[640,4,8,64]{0,3,2,1:T(8,128)(2,1)} %copy.15) | copy-start | bytes 7864324
  264.1 148.6 %copy-start.5 = (bf16[640,1024]{1,0:T(8,128)(2,1)S(1)}, bf16[640,1024]{1,0:T(8,128)(2,1)}, u32[]{:S(2)}) copy-start(bf16[640,1024]{1,0:T(8,128)(2,1)} %copy-done.4) | copy-start | bytes 3932164
  264.2 176.4 %all-gather.14.cloned.1.call-start = ((), (), s32[]{:S(2)}) async-start(), calls=%async_computation.7 | async-start | bytes 1310720 | tf_op jit(solution)/shard_map/all_gather | solution.py:72
  412.7 72.5 %reduce-scatter.5.cloned.1.call-start = ((), (), s32[]{:S(2)}) async-start(), calls=%async_computation.6 | async-start | bytes 2949120 | tf_op jit(solution)/shard_map/reduce_scatter | solution.py:40
  442.1 1.4 copy-start
Sparse Core Ops, SparseCore 0:
  10.4 45.3 all-gather.5
  58.1 44.4 all-gather.9
  104.3 62.5 all-gather.7
  168.5 56.1 all-gather.11
  264.3 148.3 reduce-scatter.6
  414.3 26.2 all-gather.13
  443.7 41.3 reduce-scatter.4
where the time goes:
time: 496 us; the launch traced here: 492 us
  waiting for transfers between devices  410 us (83%)
  matrix products  32.1 us (6%)
  local copies, waits for them, and re-layouts  25.3 us (5%)
  between operations  14.2 us (3%)
  other arithmetic  9.84 us (2%)
    reduce_scatter x1, waiting for transfers between devices, on_device(): lax.psum_scatter(term(jnp.int32(0), lax.axis_size(('depth', 'row')) * (wi...  148 us
    all_gather x1, waiting for transfers between devices, on_device(): lax.all_gather(weight_out, 'row', axis=1, tiled=True)  60.6 us
    all_gather x1, waiting for transfers between devices, on_device(): lax.all_gather(weight_in, 'row', axis=0, tiled=True)  51.2 us
    all_gather x1, waiting for transfers between devices, on_device(): lax.all_gather(upstream, 'col', axis=1, tiled=True)  43.4 us
    all_gather x1, waiting for transfers between devices, on_device(): lax.all_gather(activations, 'col', axis=1, tiled=True)  43.3 us
    reduce_scatter x1, waiting for transfers between devices, on_device(): lax.psum_scatter(partial_input.astype(jnp.bfloat16), 'col', scatter_dimen...  40.6 us
    all_gather x1, waiting for transfers between devices, on_device(): lax.all_gather(shares.astype(jnp.bfloat16), 'depth', axis=0, tiled=True)  21.4 us
    unnamed x16, local copies, waits for them, and re-layouts  17 us
  transfers between devices with their start and end apart: 7, of which 7 were waited for; matrix products, arithmetic and copies ran while one was open for 5% of the time, Pallas kernels for 0%

commit v1 on v0

v1 whole, which is shorter than its diff:
```python
import functools

import jax
import jax.numpy as jnp
from jax import lax
from jax.experimental import pallas as pl
from jax.experimental.pallas import tpu as pltpu
from jax.sharding import PartitionSpec as P

VMEM_LIMIT = 56 * 1024 * 1024
ROOT_2_PI = 0.7978845608028654
CUBIC = 0.044715

CORE = [(d, d ^ 1) for d in range(4)]
Y_HI = [(d, d ^ 2) for d in range(4)]
Y_LO = [(c, c ^ 4) for c in range(8)]


def along_x(step):
    return [(c, (c & 4) | ((c + step) & 3)) for c in range(8)]


def forward_kernel(col_ref, *refs, chunks, tokens, part, half):
    own, sib = refs[:chunks], refs[chunks : 2 * chunks]
    weights, dpre_ref, grads_ref = refs[2 * chunks : 2 * chunks + 3]
    x_all, g_all, w_in, w_out, dpre_t, act_t, grads, x_sem, g_sem, w_sem, out_sem = refs[
        2 * chunks + 3 :
    ]
    col = col_ref[0]

    def place(k):
        c = (col & 4) ^ (4 * (k >> 2)) | ((col + k) & 3)
        return pl.multiple_of(c * part, part)

    w_copies, x_copies, g_copies = [], [], []
    blocks = half // part
    for c in range(chunks):
        for q in range(blocks):
            w_copies.append(
                pltpu.make_async_copy(
                    weights.at[c, pl.ds(q * part, part)],
                    w_in.at[pl.ds(c * part, part), pl.ds(q * part, part)],
                    w_sem.at[c * (blocks + 1) + q],
                )
            )
        w_copies.append(
            pltpu.make_async_copy(
                weights.at[c, pl.ds(half, half)],
                w_out.at[:, pl.ds(c * part, part)],
                w_sem.at[c * (blocks + 1) + blocks],
            )
        )
    for side, group in enumerate((own, sib)):
        for k in range(chunks):
            rows, cols = pl.ds(side * tokens, tokens), pl.ds(place(k), part)
            slot = side * chunks + k
            x_copies.append(
                pltpu.make_async_copy(
                    group[k].at[:, pl.ds(0, part)], x_all.at[rows, cols], x_sem.at[slot]
                )
            )
            g_copies.append(
                pltpu.make_async_copy(
                    group[k].at[:, pl.ds(part, part)], g_all.at[rows, cols], g_sem.at[slot]
                )
            )
    for copy in w_copies + x_copies + g_copies:
        copy.start()
    for copy in w_copies + x_copies + g_copies:
        copy.wait()

    step = 256
    for t in range(2 * tokens // step):
        rows = pl.ds(t * step, step)
        pre = jnp.dot(x_all[rows, :], w_in[...], preferred_element_type=jnp.float32)
        back = lax.dot_general(
            g_all[rows, :], w_out[...], (((1,), (1,)), ((), ())), preferred_element_type=jnp.float32
        )
        square = pre * pre
        bend = jnp.tanh(ROOT_2_PI * pre * (1.0 + CUBIC * square))
        act = 0.5 * pre * (1.0 + bend)
        slope = 0.5 * (1.0 + bend) + 0.5 * pre * (1.0 - bend * bend) * (
            ROOT_2_PI * (1.0 + 3.0 * CUBIC * square)
        )
        dpre = (back * slope).astype(jnp.bfloat16)
        dpre_ref[rows, :] = dpre
        dpre_t[:, rows] = dpre.T
        act_t[:, rows] = act.astype(jnp.bfloat16).T

    out_copies = []
    for c in range(chunks):
        cols = pl.ds(c * part, part)
        grads[c, pl.ds(0, half), :] = jnp.dot(
            dpre_t[...], x_all[:, cols], preferred_element_type=jnp.float32
        ).astype(jnp.bfloat16)
        grads[c, pl.ds(half, half), :] = jnp.dot(
            act_t[...], g_all[:, cols], preferred_element_type=jnp.float32
        ).astype(jnp.bfloat16)
        copy = pltpu.make_async_copy(grads.at[c], grads_ref.at[c], out_sem.at[c])
        copy.start()
        out_copies.append(copy)
    for copy in out_copies:
        copy.wait()


def forward(col, own, sib, weights):
    chunks = len(own)
    tokens, part = own[0].shape[0], own[0].shape[1] // 2
    half = weights.shape[1] // 2
    width = chunks * part
    blocks = half // part
    any_space = pl.BlockSpec(memory_space=pl.ANY)
    return pl.pallas_call(
        functools.partial(forward_kernel, chunks=chunks, tokens=tokens, part=part, half=half),
        out_shape=(
            jax.ShapeDtypeStruct((2 * tokens, half), jnp.bfloat16),
            jax.ShapeDtypeStruct((chunks, 2 * half, part), jnp.bfloat16),
        ),
        in_specs=[pl.BlockSpec(memory_space=pltpu.SMEM)] + [any_space] * (2 * chunks + 1),
        out_specs=(pl.BlockSpec(memory_space=pltpu.VMEM), any_space),
        scratch_shapes=[
            pltpu.VMEM((2 * tokens, width), jnp.bfloat16),
            pltpu.VMEM((2 * tokens, width), jnp.bfloat16),
            pltpu.VMEM((width, half), jnp.bfloat16),
            pltpu.VMEM((half, width), jnp.bfloat16),
            pltpu.VMEM((half, 2 * tokens), jnp.bfloat16),
            pltpu.VMEM((half, 2 * tokens), jnp.bfloat16),
            pltpu.VMEM((chunks, 2 * half, part), jnp.bfloat16),
            pltpu.SemaphoreType.DMA((2 * chunks,)),
            pltpu.SemaphoreType.DMA((2 * chunks,)),
            pltpu.SemaphoreType.DMA((chunks * (blocks + 1),)),
            pltpu.SemaphoreType.DMA((chunks,)),
        ],
        compiler_params=pltpu.CompilerParams(vmem_limit_bytes=VMEM_LIMIT),
        cost_estimate=pl.CostEstimate(
            flops=16 * tokens * width * half,
            bytes_accessed=8 * tokens * width + 8 * half * width,
            transcendentals=2 * tokens * half,
        ),
    )(col, *own, *sib, weights)


def input_kernel(col_ref, dpre, weights, out_ref, w_in, sem, *, chunks, part, half):
    col = col_ref[0]
    copies = []
    blocks = half // part
    for k in range(chunks):
        c = (col & 4) ^ (4 * (k >> 2)) | ((col + k) & 3)
        for q in range(blocks):
            copies.append(
                pltpu.make_async_copy(
                    weights.at[c, pl.ds(q * part, part)],
                    w_in.at[pl.ds(k * part, part), pl.ds(q * part, part)],
                    sem.at[k * blocks + q],
                )
            )
    for copy in copies:
        copy.start()
    for copy in copies:
        copy.wait()
    for k in range(chunks):
        where = pl.ds((k >> 2) * part, part)
        out_ref[k & 3, :, where] = lax.dot_general(
            dpre[...],
            w_in[pl.ds(k * part, part), :],
            (((1,), (1,)), ((), ())),
            preferred_element_type=jnp.float32,
        ).astype(jnp.bfloat16)


def input_grad(col, dpre, weights):
    chunks, part = weights.shape[0], weights.shape[2]
    half = weights.shape[1] // 2
    rows = dpre.shape[0]
    blocks = half // part
    return pl.pallas_call(
        functools.partial(input_kernel, chunks=chunks, part=part, half=half),
        out_shape=jax.ShapeDtypeStruct((4, rows, 2 * part), jnp.bfloat16),
        in_specs=[
            pl.BlockSpec(memory_space=pltpu.SMEM),
            pl.BlockSpec(memory_space=pltpu.VMEM),
            pl.BlockSpec(memory_space=pl.ANY),
        ],
        out_specs=pl.BlockSpec(memory_space=pltpu.VMEM),
        scratch_shapes=[
            pltpu.VMEM((chunks * part, half), jnp.bfloat16),
            pltpu.SemaphoreType.DMA((chunks * blocks,)),
        ],
        compiler_params=pltpu.CompilerParams(vmem_limit_bytes=VMEM_LIMIT),
        cost_estimate=pl.CostEstimate(
            flops=2 * rows * chunks * part * half,
            bytes_accessed=2 * rows * (half + chunks * part) + 2 * chunks * part * half,
            transcendentals=0,
        ),
    )(col, dpre, weights)


def on_device(activations, weight_in, weight_out, upstream):
    tokens, part = activations.shape
    half = weight_in.shape[1] // 2
    core = lax.axis_index("depth") % 2
    col = lax.axis_index("col").astype(jnp.int32).reshape(1)

    w_in_here = lax.dynamic_slice(weight_in, (0, core * half), (part, half))
    w_out_here = lax.dynamic_slice(weight_out, (core * half, 0), (half, part))
    packed = jnp.concatenate(
        [w_in_here[:, q * part : (q + 1) * part] for q in range(half // part)] + [w_out_here], axis=0
    )
    weights = lax.all_gather(packed, "row", axis=0, tiled=False)

    mine = jnp.concatenate([activations, upstream], axis=1)
    other = lax.ppermute(mine, "col", Y_LO)
    own = []
    for start in (mine, other):
        own += [start] + [lax.ppermute(start, "col", along_x(-k)) for k in (1, 2, 3)]
    sib = [lax.ppermute(chunk, "depth", CORE) for chunk in own]

    dpre, grads = forward(col, own, sib, weights)

    shares = lax.psum_scatter(grads, "row", scatter_dimension=0, tiled=False)
    summed = (
        shares.astype(jnp.float32) + lax.ppermute(shares, "depth", Y_HI).astype(jnp.float32)
    ).astype(jnp.bfloat16)
    swapped = lax.ppermute(summed, "depth", CORE)
    first = jnp.where(core == 0, summed, swapped).astype(jnp.float32)
    second = jnp.where(core == 0, swapped, summed).astype(jnp.float32)
    grad_weight_in = jnp.concatenate([first[:half].T, second[:half].T], axis=1)
    grad_weight_out = jnp.concatenate([first[half:], second[half:]], axis=0)

    partial = input_grad(col, dpre, weights)
    joined = partial[:, :tokens].astype(jnp.float32) + lax.ppermute(
        partial[:, tokens:], "depth", CORE
    ).astype(jnp.float32)
    joined = joined.astype(jnp.bfloat16)
    total = joined[0].astype(jnp.float32)
    for k in (1, 2, 3):
        total = total + lax.ppermute(joined[k], "col", along_x(k)).astype(jnp.float32)
    passed = lax.ppermute(total[:, part:].astype(jnp.bfloat16), "col", Y_LO)
    grad_input = (total[:, :part] + passed.astype(jnp.float32)).astype(jnp.bfloat16)
    return (grad_input, grad_weight_in, grad_weight_out)


def solution(mesh):
    return jax.shard_map(
        on_device,
        mesh=mesh,
        in_specs=(
            P(("depth", "row"), "col"),
            P("row", "col"),
            P("col", "row"),
            P(("depth", "row"), "col"),
        ),
        out_specs=(P(("depth", "row"), "col"), P("row", "col"), P("col", "row")),
        check_vma=False,
    )
```

time: 496 us -> 188 us (0.38)
  waiting for transfers between devices: 410 us -> 104 us
  matrix products: 32.1 us -> 0 us
  Pallas kernels: 0 us -> 27.9 us
  starting transfers between devices: 0.28 us -> 26.2 us
  local copies, waits for them, and re-layouts: 25.3 us -> 8.87 us
    all_gather x5 -> x1, waiting for transfers between devices: 220 us -> 0.01 us  [on_device(): weights = lax.all_gather(packed, 'row', axis=0, tiled=False)]
    reduce_scatter x2 -> x1, waiting for transfers between devices: 189 us -> 35.7 us  [on_device(): shares = lax.psum_scatter(grads, 'row', scatter_dimension=0, tiled=False)]
    ppermute x0 -> x22, waiting for transfers between devices: none -> 68.4 us  [the longest x6 41.2 us: on_device(): lax.ppermute(start, 'col', along_x(-k))]
    dot_general x5 -> x0, matrix products: 32.1 us -> none  [the longest x1 8.25 us: on_device(): pre = jnp.dot(inputs_full, weight_cols, preferred_element_type=jnp.float32)]
    pallas_call x0 -> x2, Pallas kernels: none -> 27.9 us  [the longest x1 19.4 us: forward(): pl.pallas_call(functools.partial(forward_kernel, chunks=chunks, tokens=to...]
    ppermute x0 -> x22, starting transfers between devices: none -> 26.1 us  [the longest x6 7.31 us: on_device(): lax.ppermute(start, 'col', along_x(-k))]
    unnamed x16 -> x26, local copies, waits for them, and re-layouts: 17 us -> 4.26 us
    transpose x3 -> x0, local copies, waits for them, and re-layouts: 7.25 us -> none  [the longest x2 7.14 us: reorder(): return matrix.reshape(tokens_here, row_count, depth_count, share).transpo...]
  transfers between devices with their start and end apart: 7 -> 24, of which waited for: 7 -> 12; matrix products, arithmetic and copies ran while one was open for 5% -> 4% of each run, Pallas kernels for 0% -> 5%
where the time goes in v1:
time: 188 us
  waiting for transfers between devices  104 us (55%)
  Pallas kernels  27.9 us (15%)
  starting transfers between devices  26.2 us (14%)
  between operations  14.3 us (8%)
  local copies, waits for them, and re-layouts  8.87 us (5%)
  other arithmetic  6.78 us (4%)
    ppermute x6, waiting for transfers between devices, on_device(): lax.ppermute(start, 'col', along_x(-k))  41.2 us
    reduce_scatter x1, waiting for transfers between devices, on_device(): shares = lax.psum_scatter(grads, 'row', scatter_dimension=0, tiled=False)  35.7 us
    pallas_call x1, Pallas kernels, forward(): pl.pallas_call(functools.partial(forward_kernel, chunks=chunks, tokens=to...  19.4 us
    pallas_call x1, Pallas kernels, input_grad(): pl.pallas_call(functools.partial(input_kernel, chunks=chunks, part=part,...  8.51 us
    ppermute x1, waiting for transfers between devices, on_device(): lax.ppermute(shares, 'depth', Y_HI).astype(jnp.float32)  8.45 us
    ppermute x1, waiting for transfers between devices, on_device(): other = lax.ppermute(mine, 'col', Y_LO)  7.44 us
    ppermute x6, starting transfers between devices, on_device(): lax.ppermute(start, 'col', along_x(-k))  7.31 us
    ppermute x8, starting transfers between devices, on_device(): sib = [lax.ppermute(chunk, 'depth', CORE) for chunk in own]  7.17 us
  transfers between devices with their start and end apart: 24, of which 12 were waited for; matrix products, arithmetic and copies ran while one was open for 4% of the time, Pallas kernels for 5%

profile of v1, /device:TPU:1, one launch (start us, length us, event | category | flops | bytes accessed | tf_op | source)
XLA Modules:
  0.0 188.1 jit_solution(16222975210472728539)
XLA Ops:
  10.2 2.2 %collective-permute-start.3 = (bf16[640,512]{1,0:T(8,128)(2,1)S(1)}, bf16[640,512]{1,0:T(8,128)(2,1)S(1)}, u32[]{:S(2)}, u32[]{:S(2)}) collective-permute-start(bf16[640,512]{1,0:T(8,128)(2,1)S(1)} %constant_dynamic-update-slice_fusion.refs_0_), channel_id=1, source_target_pairs={{0,4},{1,5},{2,6},{3,7},{4,0},{5,1},{6,2},{7,3},{8,12},{9,13},{10,... | collective-permute-start | bytes 1966088 | tf_op jit(solution)/shard_map/ppermute | solution.py:212
  14.6 2.5 %collective-permute-start.1 = (bf16[640,512]{1,0:T(8,128)(2,1)S(1)}, bf16[640,512]{1,0:T(8,128)(2,1)}, u32[]{:S(2)}, u32[]{:S(2)}) collective-permute-start(bf16[640,512]{1,0:T(8,128)(2,1)S(1)} %constant_dynamic-update-slice_fusion.refs_0_), channel_id=1, source_target_pairs={{0,2},{1,3},{2,0},{3,1},{4,6},{5,7},{6,4},{7,5},{8,10},{9,11},{10,... | collective-permute-start | bytes 1966088 | tf_op jit(solution)/shard_map/ppermute | solution.py:215
  18.2 7.4 %collective-permute-done.3.refs_4_ = bf16[640,512]{1,0:T(8,128)(2,1)S(1)} collective-permute-done((bf16[640,512]{1,0:T(8,128)(2,1)S(1)}, bf16[640,512]{1,0:T(8,128)(2,1)S(1)}, u32[]{:S(2)}, u32[]{:S(2)}) %collective-permute-start.3) | collective-permute-done | bytes 655392 | tf_op jit(solution)/shard_map/ppermute | solution.py:212
  25.7 2.5 %collective-permute-start.11 = (bf16[640,512]{1,0:T(8,128)(2,1)S(1)}, bf16[640,512]{1,0:T(8,128)(2,1)S(1)}, u32[]{:S(2)}, u32[]{:S(2)}) collective-permute-start(bf16[640,512]{1,0:T(8,128)(2,1)S(1)} %collective-permute-done.3.refs_4_), channel_id=1, source_target_pairs={{0,64},{64,0},{128,192},{192,128},{1,65},{65,1},{129,193},{193,129... | collective-permute-start | bytes 1966088 | tf_op jit(solution)/shard_map/ppermute | solution.py:216
  28.1 1.4 collective-permute-start.6
  29.5 1.7 collective-permute-done.2.refs_3_
  31.3 1.4 collective-permute-start.5
  32.6 13.5 %collective-permute-done.1.refs_2_ = bf16[640,512]{1,0:T(8,128)(2,1)} collective-permute-done((bf16[640,512]{1,0:T(8,128)(2,1)S(1)}, bf16[640,512]{1,0:T(8,128)(2,1)}, u32[]{:S(2)}, u32[]{:S(2)}) %collective-permute-start.1) | collective-permute-done | bytes 655392 | tf_op jit(solution)/shard_map/ppermute | solution.py:215
  46.2 1.4 collective-permute-start.10
  47.7 12.3 %collective-permute-done.6.refs_7_ = bf16[640,512]{1,0:T(8,128)(2,1)} collective-permute-done((bf16[640,512]{1,0:T(8,128)(2,1)S(1)}, bf16[640,512]{1,0:T(8,128)(2,1)}, u32[]{:S(2)}, u32[]{:S(2)}) %collective-permute-start.6) | collective-permute-done | bytes 655392 | tf_op jit(solution)/shard_map/ppermute | solution.py:215
  60.6 13.6 %collective-permute-done.5.refs_6_ = bf16[640,512]{1,0:T(8,128)(2,1)} collective-permute-done((bf16[640,512]{1,0:T(8,128)(2,1)S(1)}, bf16[640,512]{1,0:T(8,128)(2,1)}, u32[]{:S(2)}, u32[]{:S(2)}) %collective-permute-start.5) | collective-permute-done | bytes 655392 | tf_op jit(solution)/shard_map/ppermute | solution.py:215
  79.0 19.4 %shard_map.67 = (bf16[1280,512]{1,0:T(8,128)(2,1)}, bf16[8,1024,256]{2,1,0:T(8,128)(2,1)}) custom-call(s32[1]{0:T(128)} %bitcast.col_ref, bf16[640,512]{1,0:T(8,128)(2,1)} %copy-done.6, bf16[640,512]{1,0:T(8,128)(2,1)} %collective-permute-done.refs_1_, bf16[640,512]{1,0:T(8,128)(2,1)} %collective-permute-done.1.refs_2_, bf16[640,512]{1,0:T(8,128)(2,1)} %copy-done.9, ...), custom_call_target="tpu_custom_call" | custom-call | flops 10737418240 | bytes 18874368 | tf_op jit(solution)/shard_map/pallas_call | solution.py:113
  98.4 8.5 %shard_map.68 = bf16[4,1280,512]{2,1,0:T(8,128)(2,1)} custom-call(s32[1]{0:T(128)} %bitcast.col_ref, bf16[1280,512]{1,0:T(8,128)(2,1)} %get-tuple-element.5.dpre, bf16[8,1024,256]{2,1,0:T(8,128)(2,1)} %bitcast.20), custom_call_target="tpu_custom_call" | custom-call | flops 2684354560 | bytes 8650752 | tf_op jit(solution)/shard_map/pallas_call | solution.py:176
  106.9 2.1 %slice.58 = bf16[4,640,512]{2,1,0:T(8,128)(2,1)S(1)} slice(bf16[4,1280,512]{2,1,0:T(8,128)(2,1)} %shard_map.68), slice={[0:4], [640:1280], [0:512]} | slice | bytes 5242880 | tf_op jit(solution)/shard_map/slice | solution.py:232
  109.5 4.5 %collective-permute-done.15 = bf16[4,640,512]{2,1,0:T(8,128)(2,1)S(1)} collective-permute-done((bf16[4,640,512]{2,1,0:T(8,128)(2,1)S(1)}, bf16[4,640,512]{2,1,0:T(8,128)(2,1)S(1)}, u32[]{:S(2)}, u32[]{:S(2)}) %collective-permute-start.15) | collective-permute-done | bytes 2621472 | tf_op jit(solution)/shard_map/ppermute | solution.py:231
  114.9 1.3 slice_bitcast_fusion.2
  116.8 2.0 %collective-permute-start.18 = (bf16[640,512]{1,0:T(8,128)(2,1)}, bf16[640,512]{1,0:T(8,128)(2,1)}, u32[]{:S(2)}, u32[]{:S(2)}) collective-permute-start(bf16[640,512]{1,0:T(8,128)(2,1)} %get-tuple-element.11), channel_id=1, source_target_pairs={{0,3},{1,0},{2,1},{3,2},{4,7},{5,4},{6,5},{7,6},{8,11},{9,8},{10,9... | collective-permute-start | bytes 1966088 | tf_op jit(solution)/shard_map/ppermute | solution.py:237
  119.4 35.7 %reduce-scatter.2.cloned.1.call-done = bf16[1,1024,256]{2,1,0:T(8,128)(2,1)} async-done(((bf16[8,1024,256]{2,1,0:T(8,128)(2,1)}), bf16[1,1024,256]{2,1,0:T(8,128)(2,1)}) %reduce-scatter.2.cloned.1.call-update) | async-done | bytes 524304 | tf_op jit(solution)/shard_map/reduce_scatter | solution.py:220
  155.1 2.7 %collective-permute-start.20 = (bf16[1024,256]{1,0:T(8,128)(2,1)}, bf16[1024,256]{1,0:T(8,128)(2,1)S(1)}, u32[]{:S(2)}, u32[]{:S(2)}) collective-permute-start(bf16[1024,256]{1,0:T(8,128)(2,1)} %bitcast.21), channel_id=1, source_target_pairs={{0,128},{64,192},{128,0},{192,64},{1,129},{65,193},{129,1},{193,65... | collective-permute-start | bytes 1572872 | tf_op jit(solution)/shard_map/ppermute | solution.py:222
  157.8 1.8 fusion.1
  161.2 8.4 %collective-permute-done.20 = bf16[1024,256]{1,0:T(8,128)(2,1)S(1)} collective-permute-done((bf16[1024,256]{1,0:T(8,128)(2,1)}, bf16[1024,256]{1,0:T(8,128)(2,1)S(1)}, u32[]{:S(2)}, u32[]{:S(2)}) %collective-permute-start.20) | collective-permute-done | bytes 524320 | tf_op jit(solution)/shard_map/ppermute | solution.py:222
  169.8 2.7 %collective-permute-start.21 = (bf16[1024,256]{1,0:T(8,128)(2,1)S(1)}, bf16[1024,256]{1,0:T(8,128)(2,1)S(1)}, u32[]{:S(2)}, u32[]{:S(2)}) collective-permute-start(bf16[1024,256]{1,0:T(8,128)(2,1)S(1)} %add_convert_fusion.1), channel_id=1, source_target_pairs={{0,64},{64,0},{128,192},{192,128},{1,65},{65,1},{129,193},{193,129... | collective-permute-start | bytes 1572872 | tf_op jit(solution)/shard_map/ppermute | solution.py:224
  172.4 4.3 %collective-permute-done.19 = bf16[640,256]{1,0:T(8,128)(2,1)S(1)} collective-permute-done((bf16[640,256]{1,0:T(8,128)(2,1)S(1)}, bf16[640,256]{1,0:T(8,128)(2,1)S(1)}, u32[]{:S(2)}, u32[]{:S(2)}) %collective-permute-start.19) | collective-permute-done | bytes 327712 | tf_op jit(solution)/shard_map/ppermute | solution.py:238
  176.7 1.9 fusion.2
  (69 shorter events, 18.7 us)
Async XLA Ops:
  7.2 71.8 %all-gather.3.cloned.1.call-start = ((), (), s32[]{:S(2)}) async-start(), calls=%async_computation.2 | async-start | bytes 4718592 | tf_op jit(solution)/shard_map/all_gather | solution.py:209
  10.1 145.0 %reduce-scatter.2.cloned.1.call-start = ((), (), s32[]{:S(2)}) async-start(), calls=%async_computation.1 | async-start | bytes 4718592 | tf_op jit(solution)/shard_map/reduce_scatter | solution.py:220
  10.2 15.4 %collective-permute-start.3 = (bf16[640,512]{1,0:T(8,128)(2,1)S(1)}, bf16[640,512]{1,0:T(8,128)(2,1)S(1)}, u32[]{:S(2)}, u32[]{:S(2)}) collective-permute-start(bf16[640,512]{1,0:T(8,128)(2,1)S(1)} %constant_dynamic-update-slice_fusion.refs_0_), channel_id=1, source_target_pairs={{0,4},{1,5},{2,6},{3,7},{4,0},{5,1},{6,2},{7,3},{8,12},{9,13},{10,... | collective-permute-start | bytes 1966088 | tf_op jit(solution)/shard_map/ppermute | solution.py:212
  12.4 15.7 %collective-permute-start.7 = (bf16[640,512]{1,0:T(8,128)(2,1)S(1)}, bf16[640,512]{1,0:T(8,128)(2,1)S(1)}, u32[]{:S(2)}, u32[]{:S(2)}) collective-permute-start(bf16[640,512]{1,0:T(8,128)(2,1)S(1)} %constant_dynamic-update-slice_fusion.refs_0_), channel_id=1, source_target_pairs={{0,64},{64,0},{128,192},{192,128},{1,65},{65,1},{129,193},{193,129... | collective-permute-start | bytes 1966088 | tf_op jit(solution)/shard_map/ppermute | solution.py:216
  13.7 17.6 %collective-permute-start.2 = (bf16[640,512]{1,0:T(8,128)(2,1)S(1)}, bf16[640,512]{1,0:T(8,128)(2,1)S(1)}, u32[]{:S(2)}, u32[]{:S(2)}) collective-permute-start(bf16[640,512]{1,0:T(8,128)(2,1)S(1)} %constant_dynamic-update-slice_fusion.refs_0_), channel_id=1, source_target_pairs={{0,1},{1,2},{2,3},{3,0},{4,5},{5,6},{6,7},{7,4},{8,9},{9,10},{10,1... | collective-permute-start | bytes 1966088 | tf_op jit(solution)/shard_map/ppermute | solution.py:215
  14.6 31.5 %collective-permute-start.1 = (bf16[640,512]{1,0:T(8,128)(2,1)S(1)}, bf16[640,512]{1,0:T(8,128)(2,1)}, u32[]{:S(2)}, u32[]{:S(2)}) collective-permute-start(bf16[640,512]{1,0:T(8,128)(2,1)S(1)} %constant_dynamic-update-slice_fusion.refs_0_), channel_id=1, source_target_pairs={{0,2},{1,3},{2,0},{3,1},{4,6},{5,7},{6,4},{7,5},{8,10},{9,11},{10,... | collective-permute-start | bytes 1966088 | tf_op jit(solution)/shard_map/ppermute | solution.py:215
  17.1 29.1 %collective-permute-start = (bf16[640,512]{1,0:T(8,128)(2,1)S(1)}, bf16[640,512]{1,0:T(8,128)(2,1)}, u32[]{:S(2)}, u32[]{:S(2)}) collective-permute-start(bf16[640,512]{1,0:T(8,128)(2,1)S(1)} %constant_dynamic-update-slice_fusion.refs_0_), channel_id=1, source_target_pairs={{0,3},{1,0},{2,1},{3,2},{4,7},{5,4},{6,5},{7,6},{8,11},{9,8},{10,9... | collective-permute-start | bytes 1966088 | tf_op jit(solution)/shard_map/ppermute | solution.py:215
  25.7 21.9 %collective-permute-start.11 = (bf16[640,512]{1,0:T(8,128)(2,1)S(1)}, bf16[640,512]{1,0:T(8,128)(2,1)S(1)}, u32[]{:S(2)}, u32[]{:S(2)}) collective-permute-start(bf16[640,512]{1,0:T(8,128)(2,1)S(1)} %collective-permute-done.3.refs_4_), channel_id=1, source_target_pairs={{0,64},{64,0},{128,192},{192,128},{1,65},{65,1},{129,193},{193,129... | collective-permute-start | bytes 1966088 | tf_op jit(solution)/shard_map/ppermute | solution.py:216
  28.1 31.8 %collective-permute-start.6 = (bf16[640,512]{1,0:T(8,128)(2,1)S(1)}, bf16[640,512]{1,0:T(8,128)(2,1)}, u32[]{:S(2)}, u32[]{:S(2)}) collective-permute-start(bf16[640,512]{1,0:T(8,128)(2,1)S(1)} %collective-permute-done.3.refs_4_), channel_id=1, source_target_pairs={{0,1},{1,2},{2,3},{3,0},{4,5},{5,6},{6,7},{7,4},{8,9},{9,10},{10,1... | collective-permute-start | bytes 1966088 | tf_op jit(solution)/shard_map/ppermute | solution.py:215
  31.3 43.0 %collective-permute-start.5 = (bf16[640,512]{1,0:T(8,128)(2,1)S(1)}, bf16[640,512]{1,0:T(8,128)(2,1)}, u32[]{:S(2)}, u32[]{:S(2)}) collective-permute-start(bf16[640,512]{1,0:T(8,128)(2,1)S(1)} %collective-permute-done.3.refs_4_), channel_id=1, source_target_pairs={{0,2},{1,3},{2,0},{3,1},{4,6},{5,7},{6,4},{7,5},{8,10},{9,11},{10,... | collective-permute-start | bytes 1966088 | tf_op jit(solution)/shard_map/ppermute | solution.py:215
  46.2 28.9 %collective-permute-start.4 = (bf16[640,512]{1,0:T(8,128)(2,1)S(1)}, bf16[640,512]{1,0:T(8,128)(2,1)}, u32[]{:S(2)}, u32[]{:S(2)}) collective-permute-start(bf16[640,512]{1,0:T(8,128)(2,1)S(1)} %collective-permute-done.3.refs_4_), channel_id=1, source_target_pairs={{0,3},{1,0},{2,1},{3,2},{4,7},{5,4},{6,5},{7,6},{8,11},{9,8},{10,9... | collective-permute-start | bytes 1966088 | tf_op jit(solution)/shard_map/ppermute | solution.py:215
  46.2 28.9 %collective-permute-start.10 = (bf16[640,512]{1,0:T(8,128)(2,1)S(1)}, bf16[640,512]{1,0:T(8,128)(2,1)S(1)}, u32[]{:S(2)}, u32[]{:S(2)}) collective-permute-start(bf16[640,512]{1,0:T(8,128)(2,1)S(1)} %collective-permute-done.2.refs_3_), channel_id=1, source_target_pairs={{0,64},{64,0},{128,192},{192,128},{1,65},{65,1},{129,193},{193,129... | collective-permute-start | bytes 1966088 | tf_op jit(solution)/shard_map/ppermute | solution.py:216
  47.6 28.8 %collective-permute-start.9 = (bf16[640,512]{1,0:T(8,128)(2,1)}, bf16[640,512]{1,0:T(8,128)(2,1)}, u32[]{:S(2)}, u32[]{:S(2)}) collective-permute-start(bf16[640,512]{1,0:T(8,128)(2,1)} %collective-permute-done.1.refs_2_), channel_id=1, source_target_pairs={{0,64},{64,0},{128,192},{192,128},{1,65},{65,1},{129,193},{193,129... | collective-permute-start | bytes 1966088 | tf_op jit(solution)/shard_map/ppermute | solution.py:216
  59.9 16.5 %collective-permute-start.8 = (bf16[640,512]{1,0:T(8,128)(2,1)}, bf16[640,512]{1,0:T(8,128)(2,1)}, u32[]{:S(2)}, u32[]{:S(2)}) collective-permute-start(bf16[640,512]{1,0:T(8,128)(2,1)} %collective-permute-done.refs_1_), channel_id=1, source_target_pairs={{0,64},{64,0},{128,192},{192,128},{1,65},{65,1},{129,193},{193,129... | collective-permute-start | bytes 1966088 | tf_op jit(solution)/shard_map/ppermute | solution.py:216
  74.3 2.9 %collective-permute-start.14 = (bf16[640,512]{1,0:T(8,128)(2,1)}, bf16[640,512]{1,0:T(8,128)(2,1)}, u32[]{:S(2)}, u32[]{:S(2)}) collective-permute-start(bf16[640,512]{1,0:T(8,128)(2,1)} %collective-permute-done.6.refs_7_), channel_id=1, source_target_pairs={{0,64},{64,0},{128,192},{192,128},{1,65},{65,1},{129,193},{193,129... | collective-permute-start | bytes 1966088 | tf_op jit(solution)/shard_map/ppermute | solution.py:216
  75.0 3.0 %collective-permute-start.13 = (bf16[640,512]{1,0:T(8,128)(2,1)}, bf16[640,512]{1,0:T(8,128)(2,1)}, u32[]{:S(2)}, u32[]{:S(2)}) collective-permute-start(bf16[640,512]{1,0:T(8,128)(2,1)} %collective-permute-done.5.refs_6_), channel_id=1, source_target_pairs={{0,64},{64,0},{128,192},{192,128},{1,65},{65,1},{129,193},{193,129... | collective-permute-start | bytes 1966088 | tf_op jit(solution)/shard_map/ppermute | solution.py:216
  75.9 3.1 %collective-permute-start.12 = (bf16[640,512]{1,0:T(8,128)(2,1)}, bf16[640,512]{1,0:T(8,128)(2,1)}, u32[]{:S(2)}, u32[]{:S(2)}) collective-permute-start(bf16[640,512]{1,0:T(8,128)(2,1)} %collective-permute-done.4.refs_5_), channel_id=1, source_target_pairs={{0,64},{64,0},{128,192},{192,128},{1,65},{65,1},{129,193},{193,129... | collective-permute-start | bytes 1966088 | tf_op jit(solution)/shard_map/ppermute | solution.py:216
  109.0 5.0 %collective-permute-start.15 = (bf16[4,640,512]{2,1,0:T(8,128)(2,1)S(1)}, bf16[4,640,512]{2,1,0:T(8,128)(2,1)S(1)}, u32[]{:S(2)}, u32[]{:S(2)}) collective-permute-start(bf16[4,640,512]{2,1,0:T(8,128)(2,1)S(1)} %slice.58), channel_id=1, source_target_pairs={{0,64},{64,0},{128,192},{192,128},{1,65},{65,1},{129,193},{193,129... | collective-permute-start | bytes 7864328 | tf_op jit(solution)/shard_map/ppermute | solution.py:231
  116.2 41.6 %collective-permute-start.16 = (bf16[640,512]{1,0:T(8,128)(2,1)}, bf16[640,512]{1,0:T(8,128)(2,1)}, u32[]{:S(2)}, u32[]{:S(2)}) collective-permute-start(bf16[640,512]{1,0:T(8,128)(2,1)} %get-tuple-element.10), channel_id=1, source_target_pairs={{0,1},{1,2},{2,3},{3,0},{4,5},{5,6},{6,7},{7,4},{8,9},{9,10},{10,1... | collective-permute-start | bytes 1966088 | tf_op jit(solution)/shard_map/ppermute | solution.py:237
  116.8 41.0 %collective-permute-start.18 = (bf16[640,512]{1,0:T(8,128)(2,1)}, bf16[640,512]{1,0:T(8,128)(2,1)}, u32[]{:S(2)}, u32[]{:S(2)}) collective-permute-start(bf16[640,512]{1,0:T(8,128)(2,1)} %get-tuple-element.11), channel_id=1, source_target_pairs={{0,3},{1,0},{2,1},{3,2},{4,7},{5,4},{6,5},{7,6},{8,11},{9,8},{10,9... | collective-permute-start | bytes 1966088 | tf_op jit(solution)/shard_map/ppermute | solution.py:237
  118.9 38.9 %collective-permute-start.17 = (bf16[640,512]{1,0:T(8,128)(2,1)}, bf16[640,512]{1,0:T(8,128)(2,1)}, u32[]{:S(2)}, u32[]{:S(2)}) collective-permute-start(bf16[640,512]{1,0:T(8,128)(2,1)} %get-tuple-element.12), channel_id=1, source_target_pairs={{0,2},{1,3},{2,0},{3,1},{4,6},{5,7},{6,4},{7,5},{8,10},{9,11},{10,... | collective-permute-start | bytes 1966088 | tf_op jit(solution)/shard_map/ppermute | solution.py:237
  155.1 14.6 %collective-permute-start.20 = (bf16[1024,256]{1,0:T(8,128)(2,1)}, bf16[1024,256]{1,0:T(8,128)(2,1)S(1)}, u32[]{:S(2)}, u32[]{:S(2)}) collective-permute-start(bf16[1024,256]{1,0:T(8,128)(2,1)} %bitcast.21), channel_id=1, source_target_pairs={{0,128},{64,192},{128,0},{192,64},{1,129},{65,193},{129,1},{193,65... | collective-permute-start | bytes 1572872 | tf_op jit(solution)/shard_map/ppermute | solution.py:222
  160.8 15.9 %collective-permute-start.19 = (bf16[640,256]{1,0:T(8,128)(2,1)S(1)}, bf16[640,256]{1,0:T(8,128)(2,1)S(1)}, u32[]{:S(2)}, u32[]{:S(2)}) collective-permute-start(bf16[640,256]{1,0:T(8,128)(2,1)S(1)} %slice.82), channel_id=1, source_target_pairs={{0,4},{1,5},{2,6},{3,7},{4,0},{5,1},{6,2},{7,3},{8,12},{9,13},{10,... | collective-permute-start | bytes 983048 | tf_op jit(solution)/shard_map/ppermute | solution.py:238
  169.8 8.8 %collective-permute-start.21 = (bf16[1024,256]{1,0:T(8,128)(2,1)S(1)}, bf16[1024,256]{1,0:T(8,128)(2,1)S(1)}, u32[]{:S(2)}, u32[]{:S(2)}) collective-permute-start(bf16[1024,256]{1,0:T(8,128)(2,1)S(1)} %add_convert_fusion.1), channel_id=1, source_target_pairs={{0,64},{64,0},{128,192},{192,128},{1,65},{65,1},{129,193},{193,129... | collective-permute-start | bytes 1572872 | tf_op jit(solution)/shard_map/ppermute | solution.py:224
  (12 other events, 278.7 us)
Sparse Core Ops, SparseCore 0:
  10.2 58.6 all-gather.2
  98.5 56.4 reduce-scatter.1

commit v2 on v0

v2 whole, which is shorter than its diff:
```python
import functools

import jax
import jax.numpy as jnp
from jax import lax
from jax.experimental import pallas as pl
from jax.experimental.pallas import tpu as pltpu
from jax.sharding import PartitionSpec as P

VMEM_LIMIT = 60 * 1024 * 1024
ROOT_2_PI = 0.7978845608028654
CUBIC = 0.044715

CORE = [(d, d ^ 1) for d in range(4)]
Y_HI = [(d, d ^ 2) for d in range(4)]
Y_LO = [(c, c ^ 4) for c in range(8)]


def along_x(step):
    return [(c, (c & 4) | ((c + step) & 3)) for c in range(8)]


def along_z(step):
    return [(z, (z + step) % 8) for z in range(8)]


def by_core(first, second):
    return [
        (d * 8 + a, d * 8 + b) for d in range(4) for a, b in (first if d % 2 == 0 else second)
    ]


def after(value, *others):
    return lax.optimization_barrier((value, *others))[0]


def hbm():
    return pl.BlockSpec(memory_space=pl.ANY)


def vmem():
    return pl.BlockSpec(memory_space=pltpu.VMEM)


def smem():
    return pl.BlockSpec(memory_space=pltpu.SMEM)


def chunk_of(z, rel, size):
    return pl.multiple_of(((z + rel) & 7) * size, size)


def column_of(col, k, size):
    return pl.multiple_of(((col & 4) ^ (4 * (k >> 2)) | ((col + k) & 3)) * size, size)


def pack_kernel(place, activations, upstream, weight_in, weight_out, mine, packed):
    part = activations.shape[1]
    half = packed.shape[0] // 2
    at = pl.multiple_of(place[2] * half, half)
    for q in range(half // part):
        packed[pl.ds(q * part, part), :] = weight_in[:, pl.ds(pl.multiple_of(at + q * part, part), part)]
    packed[pl.ds(half, half), :] = weight_out[pl.ds(at, half), :]
    mine[:, pl.ds(0, part)] = activations[...]
    mine[:, pl.ds(part, part)] = upstream[...]


def pack(place, activations, upstream, weight_in, weight_out):
    tokens, part = activations.shape
    half = weight_in.shape[1] // 2
    return pl.pallas_call(
        pack_kernel,
        out_shape=(
            jax.ShapeDtypeStruct((tokens, 2 * part), jnp.bfloat16),
            jax.ShapeDtypeStruct((2 * half, part), jnp.bfloat16),
        ),
        in_specs=[smem()] + [vmem()] * 4,
        out_specs=(vmem(), vmem()),
        compiler_params=pltpu.CompilerParams(vmem_limit_bytes=VMEM_LIMIT),
    )(place, activations, upstream, weight_in, weight_out)


def token_copies(col, own, sib, x_all, g_all, x_sem, g_sem, tokens, part):
    x_copies, g_copies = ([], []), ([], [])
    for side, group in enumerate((own, sib)):
        for k in range(8):
            rows, cols = pl.ds(side * tokens, tokens), pl.ds(column_of(col, k, part), part)
            slot = side * 8 + k
            x_copies[side].append(
                pltpu.make_async_copy(
                    group[k].at[:, pl.ds(0, part)], x_all.at[rows, cols], x_sem.at[slot]
                )
            )
            g_copies[side].append(
                pltpu.make_async_copy(
                    group[k].at[:, pl.ds(part, part)], g_all.at[rows, cols], g_sem.at[slot]
                )
            )
    return x_copies, g_copies


def w_in_copies(weights, w_in, sem, part, half):
    blocks = half // part
    return [
        pltpu.make_async_copy(
            weights.at[c, pl.ds(q * part, part)],
            w_in.at[pl.ds(c * part, part), pl.ds(q * part, part)],
            sem.at[c * blocks + q],
        )
        for c in range(8)
        for q in range(blocks)
    ]


def start(*groups):
    for group in groups:
        for copy in group:
            copy.start()


def wait(*groups):
    for group in groups:
        for copy in group:
            copy.wait()


TILES = ((0, 384), (384, 256))


def forward_kernel(place, *refs, tokens, part, half):
    own, sib, weights = refs[:8], refs[8:16], refs[16]
    dpre_ref, terms_ref = refs[17:19]
    x_all, g_all, w_in, w_out, both, terms, x_sem, g_sem, w_sem, v_sem, out_sem = refs[19:]
    x_copies, g_copies = token_copies(
        place[1], own, sib, x_all, g_all, x_sem, g_sem, tokens, part
    )
    w_copies = w_in_copies(weights, w_in, w_sem, part, half)
    v_copies = [
        pltpu.make_async_copy(
            weights.at[c, pl.ds(half, half)], w_out.at[:, pl.ds(c * part, part)], v_sem.at[c]
        )
        for c in range(8)
    ]
    start(w_copies, x_copies[0], v_copies, g_copies[0], x_copies[1], g_copies[1])
    wait(w_copies)
    for side in range(2):
        wait(x_copies[side])
        if side:
            wait(g_copies[side])
        for n, (first, size) in enumerate(TILES):
            rows = pl.ds(side * tokens + first, size)
            pre = jnp.dot(x_all[rows, :], w_in[...], preferred_element_type=jnp.float32)
            if side == 0 and n == 0:
                wait(v_copies, g_copies[0])
            back = lax.dot_general(
                g_all[rows, :], w_out[...], (((1,), (1,)), ((), ())), preferred_element_type=jnp.float32
            )
            square = pre * pre
            bend = jnp.tanh(ROOT_2_PI * pre * (1.0 + CUBIC * square))
            act = 0.5 * pre * (1.0 + bend)
            slope = 0.5 * (1.0 + bend) + 0.5 * pre * (1.0 - bend * bend) * (
                ROOT_2_PI * (1.0 + 3.0 * CUBIC * square)
            )
            dpre = (back * slope).astype(jnp.bfloat16)
            dpre_ref[rows, :] = dpre
            both[pl.ds(0, half), rows] = dpre.T
            both[pl.ds(half, half), rows] = act.astype(jnp.bfloat16).T

    outs = []
    for c in range(8):
        cols = pl.ds(c * part, part)
        for n, source in enumerate((x_all, g_all)):
            rows = pl.ds(n * half, half)
            terms[c, rows, :] = jnp.dot(
                both[rows, :], source[:, cols], preferred_element_type=jnp.float32
            ).astype(jnp.bfloat16)
        outs.append(pltpu.make_async_copy(terms.at[c], terms_ref.at[c], out_sem.at[c]))
        outs[-1].start()
    wait(outs)


def forward(place, own, sib, weights):
    tokens, part = own[0].shape[0], own[0].shape[1] // 2
    half = weights.shape[1] // 2
    width = 8 * part
    bf16 = jnp.bfloat16
    return pl.pallas_call(
        functools.partial(forward_kernel, tokens=tokens, part=part, half=half),
        out_shape=[
            jax.ShapeDtypeStruct((2 * tokens, half), bf16),
            jax.ShapeDtypeStruct((8, 2 * half, part), bf16),
        ],
        in_specs=[smem()] + [hbm()] * 17,
        out_specs=[vmem(), hbm()],
        scratch_shapes=[
            pltpu.VMEM((2 * tokens, width), bf16),
            pltpu.VMEM((2 * tokens, width), bf16),
            pltpu.VMEM((width, half), bf16),
            pltpu.VMEM((half, width), bf16),
            pltpu.VMEM((2 * half, 2 * tokens), bf16),
            pltpu.VMEM((8, 2 * half, part), bf16),
            pltpu.SemaphoreType.DMA((16,)),
            pltpu.SemaphoreType.DMA((16,)),
            pltpu.SemaphoreType.DMA((8 * (half // part),)),
            pltpu.SemaphoreType.DMA((8,)),
            pltpu.SemaphoreType.DMA((8,)),
        ],
        compiler_params=pltpu.CompilerParams(vmem_limit_bytes=VMEM_LIMIT),
        cost_estimate=pl.CostEstimate(
            flops=16 * tokens * width * half,
            bytes_accessed=8 * tokens * width + 12 * half * width,
            transcendentals=2 * tokens * half,
        ),
    )(place, *own, *sib, weights)


def input_kernel(place, dpre, weights, sib_ref, own_ref, w_in, sem, *, part, half):
    col = place[1]
    tokens = own_ref.shape[1]
    copies = w_in_copies(weights, w_in, sem, part, half)
    start(copies)
    wait(copies)
    for out_ref, rows in ((sib_ref, pl.ds(tokens, tokens)), (own_ref, pl.ds(0, tokens))):
        for k in range(8):
            out_ref[k & 3, :, pl.ds((k >> 2) * part, part)] = lax.dot_general(
                dpre[rows, :],
                w_in[pl.ds(column_of(col, k, part), part), :],
                (((1,), (1,)), ((), ())),
                preferred_element_type=jnp.float32,
            ).astype(jnp.bfloat16)


def input_terms(place, dpre, weights):
    count, half = dpre.shape
    part = weights.shape[2]
    out = jax.ShapeDtypeStruct((4, count // 2, 2 * part), jnp.bfloat16)
    return pl.pallas_call(
        functools.partial(input_kernel, part=part, half=half),
        out_shape=(out, out),
        in_specs=[smem(), vmem(), hbm()],
        out_specs=(vmem(), vmem()),
        scratch_shapes=[
            pltpu.VMEM((8 * part, half), jnp.bfloat16),
            pltpu.SemaphoreType.DMA((8 * (half // part),)),
        ],
        compiler_params=pltpu.CompilerParams(vmem_limit_bytes=VMEM_LIMIT),
        cost_estimate=pl.CostEstimate(
            flops=16 * half * count * part,
            bytes_accessed=2 * count * half + 16 * (half + count) * part,
            transcendentals=0,
        ),
    )(place, dpre, weights)


def add(*terms):
    total = terms[0].astype(jnp.float32)
    for term in terms[1:]:
        total = total + term.astype(jnp.float32)
    return total


def on_device(activations, weight_in, weight_out, upstream):
    tokens, part = activations.shape
    core = lax.axis_index("depth") % 2
    first = core == 0
    place = jnp.stack([lax.axis_index("row"), lax.axis_index("col"), core]).astype(jnp.int32)
    bf16 = jnp.bfloat16

    def swap(chunk):
        return lax.ppermute(chunk, "depth", CORE)

    def across(up, down):
        return lax.ppermute(
            jnp.where(first, up, down), ("depth", "col"), by_core(along_x(-1), along_x(1))
        )

    mine, packed = pack(place, activations, upstream, weight_in, weight_out)
    weights = lax.all_gather(packed, "row", axis=0, tiled=False)

    own = {0: mine}
    own[1] = lax.ppermute(mine, "col", along_x(-1))
    own[3] = lax.ppermute(mine, "col", along_x(1))
    own[4] = lax.ppermute(mine, "col", Y_LO)
    sib = {0: swap(mine)}
    own[5] = lax.ppermute(own[4], "col", along_x(-1))
    own[7] = lax.ppermute(own[4], "col", along_x(1))
    own[2] = across(after(own[1], own[4]), own[3])
    for k in (1, 3, 4):
        sib[k] = swap(after(own[k], own[1], own[3], own[4]))
    own[6] = across(own[5], own[7])
    for k in (5, 7, 2):
        sib[k] = swap(after(own[k], own[5], own[7]))
    sib[6] = swap(own[6])
    own, sib = [[group[k] for k in range(8)] for group in (own, sib)]

    dpre, terms = forward(place, own, sib, weights)

    shares = lax.psum_scatter(terms, "row", scatter_dimension=0, tiled=False)
    theirs, ours = input_terms(place, dpre, weights)
    joined = add(ours, swap(theirs)).astype(bf16)
    moved = [lax.ppermute(joined[k], "col", along_x(k)) for k in (2, 1, 3)]
    total = add(joined[0], *moved)
    passed = lax.ppermute(total[:, part:].astype(bf16), "col", Y_LO)
    grad_input = add(total[:, :part], passed).astype(bf16)

    shares = after(shares, grad_input)
    shares = add(shares, lax.ppermute(shares, "depth", Y_HI)).astype(bf16)
    swapped = swap(shares)
    left = jnp.where(first, shares, swapped).astype(jnp.float32)
    right = jnp.where(first, swapped, shares).astype(jnp.float32)
    half = shares.shape[0] // 2
    grad_weight_in = jnp.concatenate([left[:half].T, right[:half].T], axis=1)
    grad_weight_out = jnp.concatenate([left[half:], right[half:]], axis=0)
    return (grad_input, grad_weight_in, grad_weight_out)


def solution(mesh):
    return jax.shard_map(
        on_device,
        mesh=mesh,
        in_specs=(
            P(("depth", "row"), "col"),
            P("row", "col"),
            P("col", "row"),
            P(("depth", "row"), "col"),
        ),
        out_specs=(P(("depth", "row"), "col"), P("row", "col"), P("col", "row")),
        check_vma=False,
    )
```

time: 496 us -> 177 us (0.36)
  waiting for transfers between devices: 410 us -> 90.4 us
  matrix products: 32.1 us -> 0 us
  Pallas kernels: 0 us -> 30.4 us
  starting transfers between devices: 0.28 us -> 30.6 us
  local copies, waits for them, and re-layouts: 25.3 us -> 3.72 us
    all_gather x5 -> x1, waiting for transfers between devices: 220 us -> 7.42 us  [on_device(): weights = lax.all_gather(packed, 'row', axis=0, tiled=False)]
    reduce_scatter x2 -> x1, waiting for transfers between devices: 189 us -> 0.01 us  [on_device(): shares = lax.psum_scatter(terms, 'row', scatter_dimension=0, tiled=False)]
    ppermute x0 -> x22, waiting for transfers between devices: none -> 82.9 us  [the longest x3 28.1 us: on_device(): moved = [lax.ppermute(joined[k], 'col', along_x(k)) for k in (2, 1, 3)]]
    dot_general x5 -> x0, matrix products: 32.1 us -> none  [the longest x1 8.25 us: on_device(): pre = jnp.dot(inputs_full, weight_cols, preferred_element_type=jnp.float32)]
    ppermute x0 -> x22, starting transfers between devices: none -> 30.6 us  [the longest x10 13.5 us: swap(): return lax.ppermute(chunk, 'depth', CORE)]
    pallas_call x0 -> x3, Pallas kernels: none -> 30.4 us  [the longest x1 20.1 us: forward(): pl.pallas_call(functools.partial(forward_kernel, tokens=tokens, part=part...]
    unnamed x16 -> x27, local copies, waits for them, and re-layouts: 17 us -> 3.41 us
    concatenate x1 -> x2, other arithmetic: 8.38 us -> 1.11 us  [the longest x1 1.04 us: on_device(): grad_weight_out = jnp.concatenate([left[half:], right[half:]], axis=0)]
  transfers between devices with their start and end apart: 7 -> 24, of which waited for: 7 -> 12; matrix products, arithmetic and copies ran while one was open for 5% -> 2% of each run, Pallas kernels for 0% -> 4%
where the time goes in v2:
time: 177 us; the launch traced here: 176 us
  waiting for transfers between devices  90.4 us (51%)
  starting transfers between devices  30.6 us (17%)
  Pallas kernels  30.4 us (17%)
  between operations  14.2 us (8%)
  other arithmetic  6.93 us (4%)
  local copies, waits for them, and re-layouts  3.72 us (2%)
    ppermute x3, waiting for transfers between devices, on_device(): moved = [lax.ppermute(joined[k], 'col', along_x(k)) for k in (2, 1, 3)]  28.1 us
    pallas_call x1, Pallas kernels, forward(): pl.pallas_call(functools.partial(forward_kernel, tokens=tokens, part=part...  20.1 us
    ppermute x10, starting transfers between devices, swap(): return lax.ppermute(chunk, 'depth', CORE)  13.5 us
    ppermute x1, waiting for transfers between devices, on_device(): shares = add(shares, lax.ppermute(shares, 'depth', Y_HI)).astype(bf16)  11.1 us
    ppermute x1, waiting for transfers between devices, on_device(): own[4] = lax.ppermute(mine, 'col', Y_LO)  10.9 us
    ppermute x2, waiting for transfers between devices, across(): lax.ppermute(jnp.where(first, up, down), ('depth', 'col'), by_core(along_...  10.2 us
    ppermute x1, waiting for transfers between devices, on_device(): own[7] = lax.ppermute(own[4], 'col', along_x(1))  8.62 us
    pallas_call x1, Pallas kernels, input_terms(): pl.pallas_call(functools.partial(input_kernel, part=part, half=half), out...  7.79 us
  transfers between devices with their start and end apart: 24, of which 12 were waited for; matrix products, arithmetic and copies ran while one was open for 2% of the time, Pallas kernels for 4%

profile of v2, /device:TPU:1, one launch (start us, length us, event | category | flops | bytes accessed | tf_op | source)
XLA Modules:
  0.0 176.3 jit_solution(10285898038032409607)
XLA Ops:
  7.9 2.5 %shard_map.67 = (bf16[640,512]{1,0:T(8,128)(2,1)}, bf16[1024,256]{1,0:T(8,128)(2,1)}) custom-call(s32[3]{0:T(128)} %pad_add_fusion.place, bf16[640,256]{1,0:T(8,128)(2,1)} %activations.1, bf16[640,256]{1,0:T(8,128)(2,1)} %upstream.1, bf16[256,1024]{1,0:T(8,128)(2,1)} %weight_in.1, bf16[1024,256]{1,0:T(8,128)(2,1)} %weight_out.1), custom_call_target="tpu_custom_call" | custom-call | tf_op jit(solution)/shard_map/pallas_call | solution.py:71
  10.4 2.2 %collective-permute-start.1 = (bf16[640,512]{1,0:T(8,128)(2,1)}, bf16[640,512]{1,0:T(8,128)(2,1)S(1)}, u32[]{:S(2)}, u32[]{:S(2)}) collective-permute-start(bf16[640,512]{1,0:T(8,128)(2,1)} %get-tuple-element.17.refs_0_), channel_id=1, source_target_pairs={{0,4},{1,5},{2,6},{3,7},{4,0},{5,1},{6,2},{7,3},{8,12},{9,13},{10,... | collective-permute-start | bytes 1966088 | tf_op jit(solution)/shard_map/ppermute | solution.py:283
  13.8 1.5 collective-permute-start
  15.3 10.9 %collective-permute-done.1.refs_4_ = bf16[640,512]{1,0:T(8,128)(2,1)S(1)} collective-permute-done((bf16[640,512]{1,0:T(8,128)(2,1)}, bf16[640,512]{1,0:T(8,128)(2,1)S(1)}, u32[]{:S(2)}, u32[]{:S(2)}) %collective-permute-start.1) | collective-permute-done | bytes 655392 | tf_op jit(solution)/shard_map/ppermute | solution.py:283
  26.2 2.2 %collective-permute-start.5 = (bf16[640,512]{1,0:T(8,128)(2,1)S(1)}, bf16[640,512]{1,0:T(8,128)(2,1)S(1)}, u32[]{:S(2)}, u32[]{:S(2)}) collective-permute-start(bf16[640,512]{1,0:T(8,128)(2,1)S(1)} %collective-permute-done.1.refs_4_), channel_id=1, source_target_pairs={{0,1},{1,2},{2,3},{3,0},{4,5},{5,6},{6,7},{7,4},{8,9},{9,10},{10,1... | collective-permute-start | bytes 1966088 | tf_op jit(solution)/shard_map/ppermute | solution.py:286
  29.6 2.1 %collective-permute-start.7 = (bf16[640,512]{1,0:T(8,128)(2,1)}, bf16[640,512]{1,0:T(8,128)(2,1)}, u32[]{:S(2)}, u32[]{:S(2)}) collective-permute-start(bf16[640,512]{1,0:T(8,128)(2,1)} %get-tuple-element.17.refs_0_), channel_id=1, source_target_pairs={{0,64},{64,0},{128,192},{192,128},{1,65},{65,1},{129,193},{193,129... | collective-permute-start | bytes 1966088 | tf_op jit(solution)/shard_map/ppermute | solution.py:270
  32.1 2.2 %collective-permute-start.8 = (bf16[640,512]{1,0:T(8,128)(2,1)S(1)}, bf16[640,512]{1,0:T(8,128)(2,1)S(1)}, u32[]{:S(2)}, u32[]{:S(2)}) collective-permute-start(bf16[640,512]{1,0:T(8,128)(2,1)S(1)} %collective-permute-done.refs_1_), channel_id=1, source_target_pairs={{0,64},{64,0},{128,192},{192,128},{1,65},{65,1},{129,193},{193,129... | collective-permute-start | bytes 1966088 | tf_op jit(solution)/shard_map/ppermute | solution.py:270
  34.3 8.6 %collective-permute-done.5.refs_7_ = bf16[640,512]{1,0:T(8,128)(2,1)S(1)} collective-permute-done((bf16[640,512]{1,0:T(8,128)(2,1)S(1)}, bf16[640,512]{1,0:T(8,128)(2,1)S(1)}, u32[]{:S(2)}, u32[]{:S(2)}) %collective-permute-start.5) | collective-permute-done | bytes 655392 | tf_op jit(solution)/shard_map/ppermute | solution.py:286
  42.9 4.5 %collective-permute-start.10 = (bf16[640,512]{1,0:T(8,128)(2,1)S(1)}, bf16[640,512]{1,0:T(8,128)(2,1)S(1)}, u32[]{:S(2)}, u32[]{:S(2)}) collective-permute-start(bf16[640,512]{1,0:T(8,128)(2,1)S(1)} %collective-permute-done.2.refs_3_), channel_id=1, source_target_pairs={{0,64},{64,0},{128,192},{192,128},{1,65},{65,1},{129,193},{193,129... | collective-permute-start | bytes 1966088 | tf_op jit(solution)/shard_map/ppermute | solution.py:270
  47.7 4.3 %collective-permute-done.3.refs_2_ = bf16[640,512]{1,0:T(8,128)(2,1)S(1)} collective-permute-done((bf16[640,512]{1,0:T(8,128)(2,1)S(1)}, bf16[640,512]{1,0:T(8,128)(2,1)S(1)}, u32[]{:S(2)}, u32[]{:S(2)}) %collective-permute-start.3) | collective-permute-done | bytes 655392 | tf_op jit(solution)/shard_map/ppermute | solution.py:273
  53.2 5.9 %collective-permute-done.6.refs_6_ = bf16[640,512]{1,0:T(8,128)(2,1)S(1)} collective-permute-done((bf16[640,512]{1,0:T(8,128)(2,1)S(1)}, bf16[640,512]{1,0:T(8,128)(2,1)S(1)}, u32[]{:S(2)}, u32[]{:S(2)}) %collective-permute-start.6) | collective-permute-done | bytes 655392 | tf_op jit(solution)/shard_map/ppermute | solution.py:273
  61.7 7.4 %all-gather.3.cloned.1.call-done = bf16[8192,256]{1,0:T(8,128)(2,1)} async-done(((bf16[1024,256]{1,0:T(8,128)(2,1)}), bf16[8192,256]{1,0:T(8,128)(2,1)}) %all-gather.3.cloned.1.call-update) | async-done | bytes 4194320 | tf_op jit(solution)/shard_map/all_gather | solution.py:278
  69.2 20.1 %shard_map.68 = (bf16[1280,512]{1,0:T(8,128)(2,1)}, bf16[8,1024,256]{2,1,0:T(8,128)(2,1)}) custom-call(s32[3]{0:T(128)} %pad_add_fusion.place, bf16[640,512]{1,0:T(8,128)(2,1)} %get-tuple-element.17.refs_0_, bf16[640,512]{1,0:T(8,128)(2,1)} %copy-done.1, bf16[640,512]{1,0:T(8,128)(2,1)} %copy-done.5, bf16[640,512]{1,0:T(8,128)(2,1)} %copy-done, ...), custom_call_target="tpu_custom_call" | custom-call | flops 10737418240 | bytes 23068672 | tf_op jit(solution)/shard_map/pallas_call | solution.py:187
  89.3 7.8 %shard_map.69 = (bf16[4,640,512]{2,1,0:T(8,128)(2,1)}, bf16[4,640,512]{2,1,0:T(8,128)(2,1)}) custom-call(s32[3]{0:T(128)} %pad_add_fusion.place, bf16[1280,512]{1,0:T(8,128)(2,1)} %get-tuple-element.26.dpre, bf16[8,1024,256]{2,1,0:T(8,128)(2,1)} %bitcast.23), custom_call_target="tpu_custom_call" | custom-call | flops 2684354560 | bytes 8650752 | tf_op jit(solution)/shard_map/pallas_call | solution.py:237
  97.9 4.7 %collective-permute-done.15 = bf16[4,640,512]{2,1,0:T(8,128)(2,1)S(1)} collective-permute-done((bf16[4,640,512]{2,1,0:T(8,128)(2,1)}, bf16[4,640,512]{2,1,0:T(8,128)(2,1)S(1)}, u32[]{:S(2)}, u32[]{:S(2)}) %collective-permute-start.15) | collective-permute-done | bytes 2621472 | tf_op jit(solution)/shard_map/ppermute | solution.py:270
  102.6 2.6 %add_convert_fusion = bf16[4,640,512]{2,1,0:T(8,128)(2,1)S(1)} fusion(bf16[4,640,512]{2,1,0:T(8,128)(2,1)S(1)} %collective-permute-done.15, bf16[4,640,512]{2,1,0:T(8,128)(2,1)} %get-tuple-element.27), kind=kLoop, calls=%fused_computation | loop fusion | flops 5242880 | bytes 7864320 | tf_op jit(solution)/shard_map/convert_element_type | solution.py:300
  105.3 2.8 %collective-permute-start.16 = (bf16[640,512]{1,0:T(8,128)(2,1)S(1)}, bf16[640,512]{1,0:T(8,128)(2,1)S(1)}, u32[]{:S(2)}, u32[]{:S(2)}) collective-permute-start(bf16[640,512]{1,0:T(8,128)(2,1)S(1)} %get-tuple-element.34), channel_id=1, source_target_pairs={{0,2},{1,3},{2,0},{3,1},{4,6},{5,7},{6,4},{7,5},{8,10},{9,11},{10,... | collective-permute-start | bytes 1966088 | tf_op jit(solution)/shard_map/ppermute | solution.py:301
  109.6 13.3 %collective-permute-done.16 = bf16[640,512]{1,0:T(8,128)(2,1)S(1)} collective-permute-done((bf16[640,512]{1,0:T(8,128)(2,1)S(1)}, bf16[640,512]{1,0:T(8,128)(2,1)S(1)}, u32[]{:S(2)}, u32[]{:S(2)}) %collective-permute-start.16) | collective-permute-done | bytes 655392 | tf_op jit(solution)/shard_map/ppermute | solution.py:301
  122.9 14.2 %collective-permute-done.18 = bf16[640,512]{1,0:T(8,128)(2,1)S(1)} collective-permute-done((bf16[640,512]{1,0:T(8,128)(2,1)S(1)}, bf16[640,512]{1,0:T(8,128)(2,1)S(1)}, u32[]{:S(2)}, u32[]{:S(2)}) %collective-permute-start.18) | collective-permute-done | bytes 655392 | tf_op jit(solution)/shard_map/ppermute | solution.py:301
  139.4 7.6 %collective-permute-done.19 = bf16[640,256]{1,0:T(8,128)(2,1)S(1)} collective-permute-done((bf16[640,256]{1,0:T(8,128)(2,1)S(1)}, bf16[640,256]{1,0:T(8,128)(2,1)S(1)}, u32[]{:S(2)}, u32[]{:S(2)}) %collective-permute-start.19) | collective-permute-done | bytes 327712 | tf_op jit(solution)/shard_map/ppermute | solution.py:303
  147.9 2.7 %collective-permute-start.20 = (bf16[1024,256]{1,0:T(8,128)(2,1)}, bf16[1024,256]{1,0:T(8,128)(2,1)S(1)}, u32[]{:S(2)}, u32[]{:S(2)}) collective-permute-start(bf16[1024,256]{1,0:T(8,128)(2,1)} %bitcast.20), channel_id=1, source_target_pairs={{0,128},{64,192},{128,0},{192,64},{1,129},{65,193},{129,1},{193,65... | collective-permute-start | bytes 1572872 | tf_op jit(solution)/shard_map/ppermute | solution.py:307
  150.6 11.1 %collective-permute-done.20 = bf16[1024,256]{1,0:T(8,128)(2,1)S(1)} collective-permute-done((bf16[1024,256]{1,0:T(8,128)(2,1)}, bf16[1024,256]{1,0:T(8,128)(2,1)S(1)}, u32[]{:S(2)}, u32[]{:S(2)}) %collective-permute-start.20) | collective-permute-done | bytes 524320 | tf_op jit(solution)/shard_map/ppermute | solution.py:307
  162.9 2.3 %collective-permute-start.21 = (bf16[1024,256]{1,0:T(8,128)(2,1)S(1)}, bf16[1024,256]{1,0:T(8,128)(2,1)S(1)}, u32[]{:S(2)}, u32[]{:S(2)}) collective-permute-start(bf16[1024,256]{1,0:T(8,128)(2,1)S(1)} %add_convert_fusion.1), channel_id=1, source_target_pairs={{0,64},{64,0},{128,192},{192,128},{1,65},{65,1},{129,193},{193,129... | collective-permute-start | bytes 1572872 | tf_op jit(solution)/shard_map/ppermute | solution.py:270
  165.2 1.5 collective-permute-done.21
  (69 shorter events, 17.0 us)
Async XLA Ops:
  7.2 62.0 %all-gather.3.cloned.1.call-start = ((), (), s32[]{:S(2)}) async-start(), calls=%async_computation.2 | async-start | bytes 4718592 | tf_op jit(solution)/shard_map/all_gather | solution.py:278
  10.4 137.5 %reduce-scatter.2.cloned.1.call-start = ((), (), s32[]{:S(2)}) async-start(), calls=%async_computation.1 | async-start | bytes 4718592 | tf_op jit(solution)/shard_map/reduce_scatter | solution.py:298
  10.4 15.7 %collective-permute-start.1 = (bf16[640,512]{1,0:T(8,128)(2,1)}, bf16[640,512]{1,0:T(8,128)(2,1)S(1)}, u32[]{:S(2)}, u32[]{:S(2)}) collective-permute-start(bf16[640,512]{1,0:T(8,128)(2,1)} %get-tuple-element.17.refs_0_), channel_id=1, source_target_pairs={{0,4},{1,5},{2,6},{3,7},{4,0},{5,1},{6,2},{7,3},{8,12},{9,13},{10,... | collective-permute-start | bytes 1966088 | tf_op jit(solution)/shard_map/ppermute | solution.py:283
  12.6 19.1 %collective-permute-start.2 = (bf16[640,512]{1,0:T(8,128)(2,1)}, bf16[640,512]{1,0:T(8,128)(2,1)S(1)}, u32[]{:S(2)}, u32[]{:S(2)}) collective-permute-start(bf16[640,512]{1,0:T(8,128)(2,1)} %get-tuple-element.17.refs_0_), channel_id=1, source_target_pairs={{0,1},{1,2},{2,3},{3,0},{4,5},{5,6},{6,7},{7,4},{8,9},{9,10},{10,1... | collective-permute-start | bytes 1966088 | tf_op jit(solution)/shard_map/ppermute | solution.py:282
  13.8 17.9 %collective-permute-start = (bf16[640,512]{1,0:T(8,128)(2,1)}, bf16[640,512]{1,0:T(8,128)(2,1)S(1)}, u32[]{:S(2)}, u32[]{:S(2)}) collective-permute-start(bf16[640,512]{1,0:T(8,128)(2,1)} %get-tuple-element.17.refs_0_), channel_id=1, source_target_pairs={{0,3},{1,0},{2,1},{3,2},{4,7},{5,4},{6,5},{7,6},{8,11},{9,8},{10,9... | collective-permute-start | bytes 1966088 | tf_op jit(solution)/shard_map/ppermute | solution.py:281
  26.2 16.8 %collective-permute-start.5 = (bf16[640,512]{1,0:T(8,128)(2,1)S(1)}, bf16[640,512]{1,0:T(8,128)(2,1)S(1)}, u32[]{:S(2)}, u32[]{:S(2)}) collective-permute-start(bf16[640,512]{1,0:T(8,128)(2,1)S(1)} %collective-permute-done.1.refs_4_), channel_id=1, source_target_pairs={{0,1},{1,2},{2,3},{3,0},{4,5},{5,6},{6,7},{7,4},{8,9},{9,10},{10,1... | collective-permute-start | bytes 1966088 | tf_op jit(solution)/shard_map/ppermute | solution.py:286
  28.4 19.1 %collective-permute-start.4 = (bf16[640,512]{1,0:T(8,128)(2,1)S(1)}, bf16[640,512]{1,0:T(8,128)(2,1)S(1)}, u32[]{:S(2)}, u32[]{:S(2)}) collective-permute-start(bf16[640,512]{1,0:T(8,128)(2,1)S(1)} %collective-permute-done.1.refs_4_), channel_id=1, source_target_pairs={{0,3},{1,0},{2,1},{3,2},{4,7},{5,4},{6,5},{7,6},{8,11},{9,8},{10,9... | collective-permute-start | bytes 1966088 | tf_op jit(solution)/shard_map/ppermute | solution.py:285
  29.6 22.9 %collective-permute-start.7 = (bf16[640,512]{1,0:T(8,128)(2,1)}, bf16[640,512]{1,0:T(8,128)(2,1)}, u32[]{:S(2)}, u32[]{:S(2)}) collective-permute-start(bf16[640,512]{1,0:T(8,128)(2,1)} %get-tuple-element.17.refs_0_), channel_id=1, source_target_pairs={{0,64},{64,0},{128,192},{192,128},{1,65},{65,1},{129,193},{193,129... | collective-permute-start | bytes 1966088 | tf_op jit(solution)/shard_map/ppermute | solution.py:270
  31.9 20.2 %collective-permute-start.3 = (bf16[640,512]{1,0:T(8,128)(2,1)S(1)}, bf16[640,512]{1,0:T(8,128)(2,1)S(1)}, u32[]{:S(2)}, u32[]{:S(2)}) collective-permute-start(bf16[640,512]{1,0:T(8,128)(2,1)S(1)} %broadcast_select_fusion.1), channel_id=1, source_target_pairs={{0,3},{1,0},{2,1},{3,2},{4,7},{5,4},{6,5},{7,6},{64,65},{65,66},{6... | collective-permute-start | bytes 1966088 | tf_op jit(solution)/shard_map/ppermute | solution.py:273
  32.1 20.5 %collective-permute-start.8 = (bf16[640,512]{1,0:T(8,128)(2,1)S(1)}, bf16[640,512]{1,0:T(8,128)(2,1)S(1)}, u32[]{:S(2)}, u32[]{:S(2)}) collective-permute-start(bf16[640,512]{1,0:T(8,128)(2,1)S(1)} %collective-permute-done.refs_1_), channel_id=1, source_target_pairs={{0,64},{64,0},{128,192},{192,128},{1,65},{65,1},{129,193},{193,129... | collective-permute-start | bytes 1966088 | tf_op jit(solution)/shard_map/ppermute | solution.py:270
  42.9 10.1 %collective-permute-start.10 = (bf16[640,512]{1,0:T(8,128)(2,1)S(1)}, bf16[640,512]{1,0:T(8,128)(2,1)S(1)}, u32[]{:S(2)}, u32[]{:S(2)}) collective-permute-start(bf16[640,512]{1,0:T(8,128)(2,1)S(1)} %collective-permute-done.2.refs_3_), channel_id=1, source_target_pairs={{0,64},{64,0},{128,192},{192,128},{1,65},{65,1},{129,193},{193,129... | collective-permute-start | bytes 1966088 | tf_op jit(solution)/shard_map/ppermute | solution.py:270
  47.5 11.6 %collective-permute-start.6 = (bf16[640,512]{1,0:T(8,128)(2,1)S(1)}, bf16[640,512]{1,0:T(8,128)(2,1)S(1)}, u32[]{:S(2)}, u32[]{:S(2)}) collective-permute-start(bf16[640,512]{1,0:T(8,128)(2,1)S(1)} %broadcast_select_fusion), channel_id=1, source_target_pairs={{0,3},{1,0},{2,1},{3,2},{4,7},{5,4},{6,5},{7,6},{64,65},{65,66},{6... | collective-permute-start | bytes 1966088 | tf_op jit(solution)/shard_map/ppermute | solution.py:273
  52.1 7.5 %collective-permute-start.11 = (bf16[640,512]{1,0:T(8,128)(2,1)S(1)}, bf16[640,512]{1,0:T(8,128)(2,1)S(1)}, u32[]{:S(2)}, u32[]{:S(2)}) collective-permute-start(bf16[640,512]{1,0:T(8,128)(2,1)S(1)} %collective-permute-done.1.refs_4_), channel_id=1, source_target_pairs={{0,64},{64,0},{128,192},{192,128},{1,65},{65,1},{129,193},{193,129... | collective-permute-start | bytes 1966088 | tf_op jit(solution)/shard_map/ppermute | solution.py:270
  52.5 7.0 %collective-permute-start.12 = (bf16[640,512]{1,0:T(8,128)(2,1)S(1)}, bf16[640,512]{1,0:T(8,128)(2,1)S(1)}, u32[]{:S(2)}, u32[]{:S(2)}) collective-permute-start(bf16[640,512]{1,0:T(8,128)(2,1)S(1)} %collective-permute-done.4.refs_5_), channel_id=1, source_target_pairs={{0,64},{64,0},{128,192},{192,128},{1,65},{65,1},{129,193},{193,129... | collective-permute-start | bytes 1966088 | tf_op jit(solution)/shard_map/ppermute | solution.py:270
  52.6 6.9 %collective-permute-start.14 = (bf16[640,512]{1,0:T(8,128)(2,1)S(1)}, bf16[640,512]{1,0:T(8,128)(2,1)S(1)}, u32[]{:S(2)}, u32[]{:S(2)}) collective-permute-start(bf16[640,512]{1,0:T(8,128)(2,1)S(1)} %collective-permute-done.5.refs_7_), channel_id=1, source_target_pairs={{0,64},{64,0},{128,192},{192,128},{1,65},{65,1},{129,193},{193,129... | collective-permute-start | bytes 1966088 | tf_op jit(solution)/shard_map/ppermute | solution.py:270
  53.1 6.6 %collective-permute-start.9 = (bf16[640,512]{1,0:T(8,128)(2,1)S(1)}, bf16[640,512]{1,0:T(8,128)(2,1)S(1)}, u32[]{:S(2)}, u32[]{:S(2)}) collective-permute-start(bf16[640,512]{1,0:T(8,128)(2,1)S(1)} %collective-permute-done.3.refs_2_), channel_id=1, source_target_pairs={{0,64},{64,0},{128,192},{192,128},{1,65},{65,1},{129,193},{193,129... | collective-permute-start | bytes 1966088 | tf_op jit(solution)/shard_map/ppermute | solution.py:270
  59.1 2.6 %collective-permute-start.13 = (bf16[640,512]{1,0:T(8,128)(2,1)S(1)}, bf16[640,512]{1,0:T(8,128)(2,1)}, u32[]{:S(2)}, u32[]{:S(2)}) collective-permute-start(bf16[640,512]{1,0:T(8,128)(2,1)S(1)} %collective-permute-done.6.refs_6_), channel_id=1, source_target_pairs={{0,64},{64,0},{128,192},{192,128},{1,65},{65,1},{129,193},{193,129... | collective-permute-start | bytes 1966088 | tf_op jit(solution)/shard_map/ppermute | solution.py:270
  97.1 5.5 %collective-permute-start.15 = (bf16[4,640,512]{2,1,0:T(8,128)(2,1)}, bf16[4,640,512]{2,1,0:T(8,128)(2,1)S(1)}, u32[]{:S(2)}, u32[]{:S(2)}) collective-permute-start(bf16[4,640,512]{2,1,0:T(8,128)(2,1)} %get-tuple-element.28), channel_id=1, source_target_pairs={{0,64},{64,0},{128,192},{192,128},{1,65},{65,1},{129,193},{193,129... | collective-permute-start | bytes 7864328 | tf_op jit(solution)/shard_map/ppermute | solution.py:270
  105.3 17.6 %collective-permute-start.16 = (bf16[640,512]{1,0:T(8,128)(2,1)S(1)}, bf16[640,512]{1,0:T(8,128)(2,1)S(1)}, u32[]{:S(2)}, u32[]{:S(2)}) collective-permute-start(bf16[640,512]{1,0:T(8,128)(2,1)S(1)} %get-tuple-element.34), channel_id=1, source_target_pairs={{0,2},{1,3},{2,0},{3,1},{4,6},{5,7},{6,4},{7,5},{8,10},{9,11},{10,... | collective-permute-start | bytes 1966088 | tf_op jit(solution)/shard_map/ppermute | solution.py:301
  108.1 29.0 %collective-permute-start.18 = (bf16[640,512]{1,0:T(8,128)(2,1)S(1)}, bf16[640,512]{1,0:T(8,128)(2,1)S(1)}, u32[]{:S(2)}, u32[]{:S(2)}) collective-permute-start(bf16[640,512]{1,0:T(8,128)(2,1)S(1)} %get-tuple-element.35), channel_id=1, source_target_pairs={{0,3},{1,0},{2,1},{3,2},{4,7},{5,4},{6,5},{7,6},{8,11},{9,8},{10,9... | collective-permute-start | bytes 1966088 | tf_op jit(solution)/shard_map/ppermute | solution.py:301
  109.0 28.7 %collective-permute-start.17 = (bf16[640,512]{1,0:T(8,128)(2,1)S(1)}, bf16[640,512]{1,0:T(8,128)(2,1)S(1)}, u32[]{:S(2)}, u32[]{:S(2)}) collective-permute-start(bf16[640,512]{1,0:T(8,128)(2,1)S(1)} %get-tuple-element.36), channel_id=1, source_target_pairs={{0,1},{1,2},{2,3},{3,0},{4,5},{5,6},{6,7},{7,4},{8,9},{9,10},{10,1... | collective-permute-start | bytes 1966088 | tf_op jit(solution)/shard_map/ppermute | solution.py:301
  138.1 8.9 %collective-permute-start.19 = (bf16[640,256]{1,0:T(8,128)(2,1)S(1)}, bf16[640,256]{1,0:T(8,128)(2,1)S(1)}, u32[]{:S(2)}, u32[]{:S(2)}) collective-permute-start(bf16[640,256]{1,0:T(8,128)(2,1)S(1)} %slice.63), channel_id=1, source_target_pairs={{0,4},{1,5},{2,6},{3,7},{4,0},{5,1},{6,2},{7,3},{8,12},{9,13},{10,... | collective-permute-start | bytes 983048 | tf_op jit(solution)/shard_map/ppermute | solution.py:303
  147.9 13.8 %collective-permute-start.20 = (bf16[1024,256]{1,0:T(8,128)(2,1)}, bf16[1024,256]{1,0:T(8,128)(2,1)S(1)}, u32[]{:S(2)}, u32[]{:S(2)}) collective-permute-start(bf16[1024,256]{1,0:T(8,128)(2,1)} %bitcast.20), channel_id=1, source_target_pairs={{0,128},{64,192},{128,0},{192,64},{1,129},{65,193},{129,1},{193,65... | collective-permute-start | bytes 1572872 | tf_op jit(solution)/shard_map/ppermute | solution.py:307
  162.9 3.8 %collective-permute-start.21 = (bf16[1024,256]{1,0:T(8,128)(2,1)S(1)}, bf16[1024,256]{1,0:T(8,128)(2,1)S(1)}, u32[]{:S(2)}, u32[]{:S(2)}) collective-permute-start(bf16[1024,256]{1,0:T(8,128)(2,1)S(1)} %add_convert_fusion.1), channel_id=1, source_target_pairs={{0,64},{64,0},{128,192},{192,128},{1,65},{65,1},{129,193},{193,129... | collective-permute-start | bytes 1572872 | tf_op jit(solution)/shard_map/ppermute | solution.py:270
  (13 other events, 191.6 us)
Sparse Core Ops, SparseCore 0:
  10.5 58.6 all-gather.2
  89.5 53.9 reduce-scatter.1

commit v3 on v2

--- a/solution.py
+++ b/solution.py
@@ -124,7 +124,7 @@
             copy.wait()
 
 
-TILES = ((0, 384), (384, 256))
+TILES = ((0, 384), (384, 256), (640, 384), (1024, 256))
 
 
 def forward_kernel(place, *refs, tokens, part, half):
@@ -141,30 +141,33 @@
         )
         for c in range(8)
     ]
-    start(w_copies, x_copies[0], v_copies, g_copies[0], x_copies[1], g_copies[1])
-    wait(w_copies)
+    start(w_copies, x_copies[0])
+    wait(w_copies, x_copies[0])
+    start(v_copies, g_copies[0])
     for side in range(2):
-        wait(x_copies[side])
+        rows = pl.ds(side * tokens, tokens)
         if side:
-            wait(g_copies[side])
-        for n, (first, size) in enumerate(TILES):
-            rows = pl.ds(side * tokens + first, size)
-            pre = jnp.dot(x_all[rows, :], w_in[...], preferred_element_type=jnp.float32)
-            if side == 0 and n == 0:
-                wait(v_copies, g_copies[0])
-            back = lax.dot_general(
-                g_all[rows, :], w_out[...], (((1,), (1,)), ((), ())), preferred_element_type=jnp.float32
-            )
-            square = pre * pre
-            bend = jnp.tanh(ROOT_2_PI * pre * (1.0 + CUBIC * square))
-            act = 0.5 * pre * (1.0 + bend)
-            slope = 0.5 * (1.0 + bend) + 0.5 * pre * (1.0 - bend * bend) * (
-                ROOT_2_PI * (1.0 + 3.0 * CUBIC * square)
-            )
-            dpre = (back * slope).astype(jnp.bfloat16)
-            dpre_ref[rows, :] = dpre
-            both[pl.ds(0, half), rows] = dpre.T
-            both[pl.ds(half, half), rows] = act.astype(jnp.bfloat16).T
+            wait(x_copies[1])
+        pre = jnp.dot(x_all[rows, :], w_in[...], preferred_element_type=jnp.float32)
+        if side == 0:
+            start(x_copies[1])
+            wait(v_copies, g_copies[0])
+            start(g_copies[1])
+        else:
+            wait(g_copies[1])
+        back = lax.dot_general(
+            g_all[rows, :], w_out[...], (((1,), (1,)), ((), ())), preferred_element_type=jnp.float32
+        )
+        square = pre * pre
+        weight = 0.5 + 0.5 * jnp.tanh(pre * (ROOT_2_PI + (ROOT_2_PI * CUBIC) * square))
+        act = pre * weight
+        slope = weight + act * (1.0 - weight) * (
+            2.0 * ROOT_2_PI + (6.0 * ROOT_2_PI * CUBIC) * square
+        )
+        dpre = (back * slope).astype(jnp.bfloat16)
+        dpre_ref[rows, :] = dpre
+        both[pl.ds(0, half), rows] = dpre.T
+        both[pl.ds(half, half), rows] = act.astype(jnp.bfloat16).T
 
     outs = []
     for c in range(8):
@@ -187,8 +190,8 @@
     return pl.pallas_call(
         functools.partial(forward_kernel, tokens=tokens, part=part, half=half),
         out_shape=[
-            jax.ShapeDtypeStruct((2 * tokens, half), bf16),
-            jax.ShapeDtypeStruct((8, 2 * half, part), bf16),
+            pltpu.VMEM((2 * tokens, half), bf16),
+            pltpu.HBM((8, 2 * half, part), bf16),
         ],
         in_specs=[smem()] + [hbm()] * 17,
         out_specs=[vmem(), hbm()],
@@ -211,45 +214,47 @@
             bytes_accessed=8 * tokens * width + 12 * half * width,
             transcendentals=2 * tokens * half,
         ),
-    )(place, *own, *sib, weights)
-
-
-def input_kernel(place, dpre, weights, sib_ref, own_ref, w_in, sem, *, part, half):
+    )(place, *own, *sib, pltpu.with_memory_space_constraint(weights, pltpu.HBM))
+
+
+def input_kernel(place, dpre, weights, out_ref, w_in, sem, *, side, part, half):
     col = place[1]
-    tokens = own_ref.shape[1]
+    tokens = out_ref.shape[1]
     copies = w_in_copies(weights, w_in, sem, part, half)
     start(copies)
     wait(copies)
-    for out_ref, rows in ((sib_ref, pl.ds(tokens, tokens)), (own_ref, pl.ds(0, tokens))):
-        for k in range(8):
-            out_ref[k & 3, :, pl.ds((k >> 2) * part, part)] = lax.dot_general(
-                dpre[rows, :],
-                w_in[pl.ds(column_of(col, k, part), part), :],
-                (((1,), (1,)), ((), ())),
-                preferred_element_type=jnp.float32,
-            ).astype(jnp.bfloat16)
-
-
-def input_terms(place, dpre, weights):
-    count, half = dpre.shape
+    for k in range(8):
+        out_ref[k & 3, :, pl.ds((k >> 2) * part, part)] = lax.dot_general(
+            dpre[pl.ds(side * tokens, tokens), :],
+            w_in[pl.ds(column_of(col, k, part), part), :],
+            (((1,), (1,)), ((), ())),
+            preferred_element_type=jnp.float32,
+        ).astype(jnp.bfloat16)
+
+
+def input_terms(place, dpre, weights, side):
+    tokens, half = dpre.shape[0] // 2, dpre.shape[1]
     part = weights.shape[2]
-    out = jax.ShapeDtypeStruct((4, count // 2, 2 * part), jnp.bfloat16)
     return pl.pallas_call(
-        functools.partial(input_kernel, part=part, half=half),
-        out_shape=(out, out),
+        functools.partial(input_kernel, side=side, part=part, half=half),
+        out_shape=jax.ShapeDtypeStruct((4, tokens, 2 * part), jnp.bfloat16),
         in_specs=[smem(), vmem(), hbm()],
-        out_specs=(vmem(), vmem()),
+        out_specs=vmem(),
         scratch_shapes=[
             pltpu.VMEM((8 * part, half), jnp.bfloat16),
             pltpu.SemaphoreType.DMA((8 * (half // part),)),
         ],
-        compiler_params=pltpu.CompilerParams(vmem_limit_bytes=VMEM_LIMIT),
+        compiler_params=pltpu.CompilerParams(vmem_limit_bytes=24 * 1024 * 1024),
         cost_estimate=pl.CostEstimate(
-            flops=16 * half * count * part,
-            bytes_accessed=2 * count * half + 16 * (half + count) * part,
+            flops=16 * half * tokens * part,
+            bytes_accessed=2 * tokens * half + 16 * (half + tokens) * part,
             transcendentals=0,
         ),
-    )(place, dpre, weights)
+    )(
+        place,
+        pltpu.with_memory_space_constraint(dpre, pltpu.VMEM),
+        pltpu.with_memory_space_constraint(weights, pltpu.HBM),
+    )
 
 
 def add(*terms):
@@ -296,18 +301,17 @@
     dpre, terms = forward(place, own, sib, weights)
 
     shares = lax.psum_scatter(terms, "row", scatter_dimension=0, tiled=False)
-    theirs, ours = input_terms(place, dpre, weights)
-    joined = add(ours, swap(theirs)).astype(bf16)
+    theirs = swap(input_terms(place, dpre, weights, 1))
+    joined = add(input_terms(place, dpre, weights, 0), theirs).astype(bf16)
     moved = [lax.ppermute(joined[k], "col", along_x(k)) for k in (2, 1, 3)]
     total = add(joined[0], *moved)
     passed = lax.ppermute(total[:, part:].astype(bf16), "col", Y_LO)
     grad_input = add(total[:, :part], passed).astype(bf16)
 
     shares = after(shares, grad_input)
-    shares = add(shares, lax.ppermute(shares, "depth", Y_HI)).astype(bf16)
-    swapped = swap(shares)
-    left = jnp.where(first, shares, swapped).astype(jnp.float32)
-    right = jnp.where(first, swapped, shares).astype(jnp.float32)
+    away = lax.ppermute(shares, "depth", Y_HI)
+    here, there = add(shares, away), add(swap(shares), swap(away))
+    left, right = jnp.where(first, here, there), jnp.where(first, there, here)
     half = shares.shape[0] // 2
     grad_weight_in = jnp.concatenate([left[:half].T, right[:half].T], axis=1)
     grad_weight_out = jnp.concatenate([left[half:], right[half:]], axis=0)

time: 177 us -> 171 us (0.966)
  waiting for transfers between devices: 90.4 us -> 86.7 us
    ppermute x10 -> x11, waiting for transfers between devices: 6.3 us -> 2.25 us  [swap(): return lax.ppermute(chunk, 'depth', CORE)]
    convert_element_type x3 -> x1, other arithmetic: 3.86 us -> 0.87 us  [on_device(): joined = add(input_terms(place, dpre, weights, 0), theirs).astype(bf16)]
    unnamed x27 -> x29, local copies, waits for them, and re-layouts: 3.41 us -> 3.95 us
    ppermute x10 -> x11, starting transfers between devices: 13.5 us -> 13.8 us  [swap(): return lax.ppermute(chunk, 'depth', CORE)]
    pallas_call x1 -> x2, Pallas kernels: 7.79 us -> 7.67 us  [input_terms(): pl.pallas_call(functools.partial(input_kernel, side=side, part=part, half...]
  transfers between devices with their start and end apart: 24 -> 25, of which waited for: 12 -> 13; matrix products, arithmetic and copies ran while one was open for 2% -> 1% of each run, Pallas kernels for 4% -> 4%
where the time goes in v3:
time: 171 us
  waiting for transfers between devices  86.7 us (51%)
  starting transfers between devices  31 us (18%)
  Pallas kernels  29.4 us (17%)
  between operations  14.3 us (8%)
  other arithmetic  5.19 us (3%)
  local copies, waits for them, and re-layouts  4.26 us (2%)
    ppermute x3, waiting for transfers between devices, on_device(): moved = [lax.ppermute(joined[k], 'col', along_x(k)) for k in (2, 1, 3)]  28.1 us
    pallas_call x1, Pallas kernels, forward(): pl.pallas_call(functools.partial(forward_kernel, tokens=tokens, part=part...  19.2 us
    ppermute x11, starting transfers between devices, swap(): return lax.ppermute(chunk, 'depth', CORE)  13.8 us
    ppermute x1, waiting for transfers between devices, on_device(): away = lax.ppermute(shares, 'depth', Y_HI)  10.9 us
    ppermute x1, waiting for transfers between devices, on_device(): own[4] = lax.ppermute(mine, 'col', Y_LO)  10.9 us
    ppermute x2, waiting for transfers between devices, across(): lax.ppermute(jnp.where(first, up, down), ('depth', 'col'), by_core(along_...  10.2 us
    ppermute x1, waiting for transfers between devices, on_device(): own[7] = lax.ppermute(own[4], 'col', along_x(1))  8.62 us
    ppermute x1, waiting for transfers between devices, on_device(): passed = lax.ppermute(total[:, part:].astype(bf16), 'col', Y_LO)  7.75 us
  transfers between devices with their start and end apart: 25, of which 13 were waited for; matrix products, arithmetic and copies ran while one was open for 1% of the time, Pallas kernels for 4%

profile of v3, /device:TPU:1, one launch (start us, length us, event | category | flops | bytes accessed | tf_op | source)
XLA Modules:
  0.0 170.8 jit_solution(4275522899957285466)
XLA Ops:
  7.8 2.5 %shard_map.67 = (bf16[640,512]{1,0:T(8,128)(2,1)}, bf16[1024,256]{1,0:T(8,128)(2,1)}) custom-call(s32[3]{0:T(128)} %pad_add_fusion.place, bf16[640,256]{1,0:T(8,128)(2,1)} %activations.1, bf16[640,256]{1,0:T(8,128)(2,1)} %upstream.1, bf16[256,1024]{1,0:T(8,128)(2,1)} %weight_in.1, bf16[1024,256]{1,0:T(8,128)(2,1)} %weight_out.1), custom_call_target="tpu_custom_call" | custom-call | tf_op jit(solution)/shard_map/pallas_call | solution.py:71
  10.3 2.2 %collective-permute-start.1 = (bf16[640,512]{1,0:T(8,128)(2,1)}, bf16[640,512]{1,0:T(8,128)(2,1)S(1)}, u32[]{:S(2)}, u32[]{:S(2)}) collective-permute-start(bf16[640,512]{1,0:T(8,128)(2,1)} %get-tuple-element.15.refs_0_), channel_id=1, source_target_pairs={{0,4},{1,5},{2,6},{3,7},{4,0},{5,1},{6,2},{7,3},{8,12},{9,13},{10,... | collective-permute-start | bytes 1966088 | tf_op jit(solution)/shard_map/ppermute | solution.py:288
  13.8 1.5 collective-permute-start
  15.2 10.9 %collective-permute-done.1.refs_4_ = bf16[640,512]{1,0:T(8,128)(2,1)S(1)} collective-permute-done((bf16[640,512]{1,0:T(8,128)(2,1)}, bf16[640,512]{1,0:T(8,128)(2,1)S(1)}, u32[]{:S(2)}, u32[]{:S(2)}) %collective-permute-start.1) | collective-permute-done | bytes 655392 | tf_op jit(solution)/shard_map/ppermute | solution.py:288
  26.1 2.2 %collective-permute-start.5 = (bf16[640,512]{1,0:T(8,128)(2,1)S(1)}, bf16[640,512]{1,0:T(8,128)(2,1)S(1)}, u32[]{:S(2)}, u32[]{:S(2)}) collective-permute-start(bf16[640,512]{1,0:T(8,128)(2,1)S(1)} %collective-permute-done.1.refs_4_), channel_id=1, source_target_pairs={{0,1},{1,2},{2,3},{3,0},{4,5},{5,6},{6,7},{7,4},{8,9},{9,10},{10,1... | collective-permute-start | bytes 1966088 | tf_op jit(solution)/shard_map/ppermute | solution.py:291
  29.6 2.1 %collective-permute-start.7 = (bf16[640,512]{1,0:T(8,128)(2,1)}, bf16[640,512]{1,0:T(8,128)(2,1)}, u32[]{:S(2)}, u32[]{:S(2)}) collective-permute-start(bf16[640,512]{1,0:T(8,128)(2,1)} %get-tuple-element.15.refs_0_), channel_id=1, source_target_pairs={{0,64},{64,0},{128,192},{192,128},{1,65},{65,1},{129,193},{193,129... | collective-permute-start | bytes 1966088 | tf_op jit(solution)/shard_map/ppermute | solution.py:275
  32.0 2.2 %collective-permute-start.8 = (bf16[640,512]{1,0:T(8,128)(2,1)S(1)}, bf16[640,512]{1,0:T(8,128)(2,1)S(1)}, u32[]{:S(2)}, u32[]{:S(2)}) collective-permute-start(bf16[640,512]{1,0:T(8,128)(2,1)S(1)} %collective-permute-done.refs_1_), channel_id=1, source_target_pairs={{0,64},{64,0},{128,192},{192,128},{1,65},{65,1},{129,193},{193,129... | collective-permute-start | bytes 1966088 | tf_op jit(solution)/shard_map/ppermute | solution.py:275
  34.2 8.6 %collective-permute-done.5.refs_7_ = bf16[640,512]{1,0:T(8,128)(2,1)S(1)} collective-permute-done((bf16[640,512]{1,0:T(8,128)(2,1)S(1)}, bf16[640,512]{1,0:T(8,128)(2,1)S(1)}, u32[]{:S(2)}, u32[]{:S(2)}) %collective-permute-start.5) | collective-permute-done | bytes 655392 | tf_op jit(solution)/shard_map/ppermute | solution.py:291
  42.9 4.5 %collective-permute-start.10 = (bf16[640,512]{1,0:T(8,128)(2,1)S(1)}, bf16[640,512]{1,0:T(8,128)(2,1)S(1)}, u32[]{:S(2)}, u32[]{:S(2)}) collective-permute-start(bf16[640,512]{1,0:T(8,128)(2,1)S(1)} %collective-permute-done.2.refs_3_), channel_id=1, source_target_pairs={{0,64},{64,0},{128,192},{192,128},{1,65},{65,1},{129,193},{193,129... | collective-permute-start | bytes 1966088 | tf_op jit(solution)/shard_map/ppermute | solution.py:275
  47.7 4.3 %collective-permute-done.3.refs_2_ = bf16[640,512]{1,0:T(8,128)(2,1)S(1)} collective-permute-done((bf16[640,512]{1,0:T(8,128)(2,1)S(1)}, bf16[640,512]{1,0:T(8,128)(2,1)S(1)}, u32[]{:S(2)}, u32[]{:S(2)}) %collective-permute-start.3) | collective-permute-done | bytes 655392 | tf_op jit(solution)/shard_map/ppermute | solution.py:278
  53.1 5.9 %collective-permute-done.6.refs_6_ = bf16[640,512]{1,0:T(8,128)(2,1)S(1)} collective-permute-done((bf16[640,512]{1,0:T(8,128)(2,1)S(1)}, bf16[640,512]{1,0:T(8,128)(2,1)S(1)}, u32[]{:S(2)}, u32[]{:S(2)}) %collective-permute-start.6) | collective-permute-done | bytes 655392 | tf_op jit(solution)/shard_map/ppermute | solution.py:278
  61.6 7.4 %all-gather.3.cloned.1.call-done = bf16[8192,256]{1,0:T(8,128)(2,1)} async-done(((bf16[1024,256]{1,0:T(8,128)(2,1)}), bf16[8192,256]{1,0:T(8,128)(2,1)}) %all-gather.3.cloned.1.call-update) | async-done | bytes 4194320 | tf_op jit(solution)/shard_map/all_gather | solution.py:283
  69.1 19.2 %shard_map.68 = (bf16[1280,512]{1,0:T(8,128)(2,1)S(1)}, bf16[8,1024,256]{2,1,0:T(8,128)(2,1)}) custom-call(s32[3]{0:T(128)} %pad_add_fusion.place, bf16[640,512]{1,0:T(8,128)(2,1)} %get-tuple-element.15.refs_0_, bf16[640,512]{1,0:T(8,128)(2,1)} %copy-done.2, bf16[640,512]{1,0:T(8,128)(2,1)} %copy-done.6, bf16[640,512]{1,0:T(8,128)(2,1)} %copy-done.1, ...), custom_call_target="tpu_custom_call" | custom-call | flops 10737418240 | bytes 23068672 | tf_op jit(solution)/shard_map/pallas_call | solution.py:190
  88.9 3.8 %shard_map.70 = bf16[4,640,512]{2,1,0:T(8,128)(2,1)S(1)} custom-call(s32[3]{0:T(128)S(1)} %copy-done, bf16[1280,512]{1,0:T(8,128)(2,1)S(1)} %get-tuple-element.24.dpre, bf16[8,1024,256]{2,1,0:T(8,128)(2,1)} %bitcast.21), custom_call_target="tpu_custom_call" | custom-call | flops 1342177280 | bytes 5373952 | tf_op jit(solution)/shard_map/pallas_call | solution.py:238
  93.7 3.8 %shard_map.69 = bf16[4,640,512]{2,1,0:T(8,128)(2,1)S(1)} custom-call(s32[3]{0:T(128)S(1)} %copy-done, bf16[1280,512]{1,0:T(8,128)(2,1)S(1)} %get-tuple-element.24.dpre, bf16[8,1024,256]{2,1,0:T(8,128)(2,1)} %bitcast.22), custom_call_target="tpu_custom_call" | custom-call | flops 1342177280 | bytes 5373952 | tf_op jit(solution)/shard_map/pallas_call | solution.py:238
  99.3 2.8 %collective-permute-start.16 = (bf16[640,512]{1,0:T(8,128)(2,1)S(1)}, bf16[640,512]{1,0:T(8,128)(2,1)S(1)}, u32[]{:S(2)}, u32[]{:S(2)}) collective-permute-start(bf16[640,512]{1,0:T(8,128)(2,1)S(1)} %get-tuple-element.30), channel_id=1, source_target_pairs={{0,2},{1,3},{2,0},{3,1},{4,6},{5,7},{6,4},{7,5},{8,10},{9,11},{10,... | collective-permute-start | bytes 1966088 | tf_op jit(solution)/shard_map/ppermute | solution.py:306
  103.5 13.3 %collective-permute-done.16 = bf16[640,512]{1,0:T(8,128)(2,1)S(1)} collective-permute-done((bf16[640,512]{1,0:T(8,128)(2,1)S(1)}, bf16[640,512]{1,0:T(8,128)(2,1)S(1)}, u32[]{:S(2)}, u32[]{:S(2)}) %collective-permute-start.16) | collective-permute-done | bytes 655392 | tf_op jit(solution)/shard_map/ppermute | solution.py:306
  116.9 14.2 %collective-permute-done.18 = bf16[640,512]{1,0:T(8,128)(2,1)S(1)} collective-permute-done((bf16[640,512]{1,0:T(8,128)(2,1)S(1)}, bf16[640,512]{1,0:T(8,128)(2,1)S(1)}, u32[]{:S(2)}, u32[]{:S(2)}) %collective-permute-start.18) | collective-permute-done | bytes 655392 | tf_op jit(solution)/shard_map/ppermute | solution.py:306
  133.3 7.7 %collective-permute-done.19 = bf16[640,256]{1,0:T(8,128)(2,1)S(1)} collective-permute-done((bf16[640,256]{1,0:T(8,128)(2,1)S(1)}, bf16[640,256]{1,0:T(8,128)(2,1)S(1)}, u32[]{:S(2)}, u32[]{:S(2)}) %collective-permute-start.19) | collective-permute-done | bytes 327712 | tf_op jit(solution)/shard_map/ppermute | solution.py:308
  142.5 2.7 %collective-permute-start.20 = (bf16[1024,256]{1,0:T(8,128)(2,1)}, bf16[1024,256]{1,0:T(8,128)(2,1)S(1)}, u32[]{:S(2)}, u32[]{:S(2)}) collective-permute-start(bf16[1024,256]{1,0:T(8,128)(2,1)} %bitcast.23), channel_id=1, source_target_pairs={{0,128},{64,192},{128,0},{192,64},{1,129},{65,193},{129,1},{193,65... | collective-permute-start | bytes 1572872 | tf_op jit(solution)/shard_map/ppermute | solution.py:312
  146.1 10.9 %collective-permute-done.20 = bf16[1024,256]{1,0:T(8,128)(2,1)S(1)} collective-permute-done((bf16[1024,256]{1,0:T(8,128)(2,1)}, bf16[1024,256]{1,0:T(8,128)(2,1)S(1)}, u32[]{:S(2)}, u32[]{:S(2)}) %collective-permute-start.20) | collective-permute-done | bytes 524320 | tf_op jit(solution)/shard_map/ppermute | solution.py:312
  157.0 1.5 collective-permute-start.22
  158.5 1.5 collective-permute-done.22
  160.1 1.3 fusion.3
  (73 shorter events, 19.4 us)
Async XLA Ops:
  7.2 61.9 %all-gather.3.cloned.1.call-start = ((), (), s32[]{:S(2)}) async-start(), calls=%async_computation.2 | async-start | bytes 4718592 | tf_op jit(solution)/shard_map/all_gather | solution.py:283
  10.3 132.2 %reduce-scatter.2.cloned.1.call-start = ((), (), s32[]{:S(2)}) async-start(), calls=%async_computation.1 | async-start | bytes 4718592 | tf_op jit(solution)/shard_map/reduce_scatter | solution.py:303
  10.3 15.7 %collective-permute-start.1 = (bf16[640,512]{1,0:T(8,128)(2,1)}, bf16[640,512]{1,0:T(8,128)(2,1)S(1)}, u32[]{:S(2)}, u32[]{:S(2)}) collective-permute-start(bf16[640,512]{1,0:T(8,128)(2,1)} %get-tuple-element.15.refs_0_), channel_id=1, source_target_pairs={{0,4},{1,5},{2,6},{3,7},{4,0},{5,1},{6,2},{7,3},{8,12},{9,13},{10,... | collective-permute-start | bytes 1966088 | tf_op jit(solution)/shard_map/ppermute | solution.py:288
  12.6 19.1 %collective-permute-start.2 = (bf16[640,512]{1,0:T(8,128)(2,1)}, bf16[640,512]{1,0:T(8,128)(2,1)S(1)}, u32[]{:S(2)}, u32[]{:S(2)}) collective-permute-start(bf16[640,512]{1,0:T(8,128)(2,1)} %get-tuple-element.15.refs_0_), channel_id=1, source_target_pairs={{0,1},{1,2},{2,3},{3,0},{4,5},{5,6},{6,7},{7,4},{8,9},{9,10},{10,1... | collective-permute-start | bytes 1966088 | tf_op jit(solution)/shard_map/ppermute | solution.py:287
  13.8 17.9 %collective-permute-start = (bf16[640,512]{1,0:T(8,128)(2,1)}, bf16[640,512]{1,0:T(8,128)(2,1)S(1)}, u32[]{:S(2)}, u32[]{:S(2)}) collective-permute-start(bf16[640,512]{1,0:T(8,128)(2,1)} %get-tuple-element.15.refs_0_), channel_id=1, source_target_pairs={{0,3},{1,0},{2,1},{3,2},{4,7},{5,4},{6,5},{7,6},{8,11},{9,8},{10,9... | collective-permute-start | bytes 1966088 | tf_op jit(solution)/shard_map/ppermute | solution.py:286
  26.1 16.8 %collective-permute-start.5 = (bf16[640,512]{1,0:T(8,128)(2,1)S(1)}, bf16[640,512]{1,0:T(8,128)(2,1)S(1)}, u32[]{:S(2)}, u32[]{:S(2)}) collective-permute-start(bf16[640,512]{1,0:T(8,128)(2,1)S(1)} %collective-permute-done.1.refs_4_), channel_id=1, source_target_pairs={{0,1},{1,2},{2,3},{3,0},{4,5},{5,6},{6,7},{7,4},{8,9},{9,10},{10,1... | collective-permute-start | bytes 1966088 | tf_op jit(solution)/shard_map/ppermute | solution.py:291
  28.3 19.1 %collective-permute-start.4 = (bf16[640,512]{1,0:T(8,128)(2,1)S(1)}, bf16[640,512]{1,0:T(8,128)(2,1)S(1)}, u32[]{:S(2)}, u32[]{:S(2)}) collective-permute-start(bf16[640,512]{1,0:T(8,128)(2,1)S(1)} %collective-permute-done.1.refs_4_), channel_id=1, source_target_pairs={{0,3},{1,0},{2,1},{3,2},{4,7},{5,4},{6,5},{7,6},{8,11},{9,8},{10,9... | collective-permute-start | bytes 1966088 | tf_op jit(solution)/shard_map/ppermute | solution.py:290
  29.6 22.9 %collective-permute-start.7 = (bf16[640,512]{1,0:T(8,128)(2,1)}, bf16[640,512]{1,0:T(8,128)(2,1)}, u32[]{:S(2)}, u32[]{:S(2)}) collective-permute-start(bf16[640,512]{1,0:T(8,128)(2,1)} %get-tuple-element.15.refs_0_), channel_id=1, source_target_pairs={{0,64},{64,0},{128,192},{192,128},{1,65},{65,1},{129,193},{193,129... | collective-permute-start | bytes 1966088 | tf_op jit(solution)/shard_map/ppermute | solution.py:275
  31.8 20.2 %collective-permute-start.3 = (bf16[640,512]{1,0:T(8,128)(2,1)S(1)}, bf16[640,512]{1,0:T(8,128)(2,1)S(1)}, u32[]{:S(2)}, u32[]{:S(2)}) collective-permute-start(bf16[640,512]{1,0:T(8,128)(2,1)S(1)} %broadcast_select_fusion.1), channel_id=1, source_target_pairs={{0,3},{1,0},{2,1},{3,2},{4,7},{5,4},{6,5},{7,6},{64,65},{65,66},{6... | collective-permute-start | bytes 1966088 | tf_op jit(solution)/shard_map/ppermute | solution.py:278
  32.0 20.5 %collective-permute-start.8 = (bf16[640,512]{1,0:T(8,128)(2,1)S(1)}, bf16[640,512]{1,0:T(8,128)(2,1)S(1)}, u32[]{:S(2)}, u32[]{:S(2)}) collective-permute-start(bf16[640,512]{1,0:T(8,128)(2,1)S(1)} %collective-permute-done.refs_1_), channel_id=1, source_target_pairs={{0,64},{64,0},{128,192},{192,128},{1,65},{65,1},{129,193},{193,129... | collective-permute-start | bytes 1966088 | tf_op jit(solution)/shard_map/ppermute | solution.py:275
  42.9 10.1 %collective-permute-start.10 = (bf16[640,512]{1,0:T(8,128)(2,1)S(1)}, bf16[640,512]{1,0:T(8,128)(2,1)S(1)}, u32[]{:S(2)}, u32[]{:S(2)}) collective-permute-start(bf16[640,512]{1,0:T(8,128)(2,1)S(1)} %collective-permute-done.2.refs_3_), channel_id=1, source_target_pairs={{0,64},{64,0},{128,192},{192,128},{1,65},{65,1},{129,193},{193,129... | collective-permute-start | bytes 1966088 | tf_op jit(solution)/shard_map/ppermute | solution.py:275
  47.4 11.6 %collective-permute-start.6 = (bf16[640,512]{1,0:T(8,128)(2,1)S(1)}, bf16[640,512]{1,0:T(8,128)(2,1)S(1)}, u32[]{:S(2)}, u32[]{:S(2)}) collective-permute-start(bf16[640,512]{1,0:T(8,128)(2,1)S(1)} %broadcast_select_fusion), channel_id=1, source_target_pairs={{0,3},{1,0},{2,1},{3,2},{4,7},{5,4},{6,5},{7,6},{64,65},{65,66},{6... | collective-permute-start | bytes 1966088 | tf_op jit(solution)/shard_map/ppermute | solution.py:278
  52.0 7.5 %collective-permute-start.11 = (bf16[640,512]{1,0:T(8,128)(2,1)S(1)}, bf16[640,512]{1,0:T(8,128)(2,1)S(1)}, u32[]{:S(2)}, u32[]{:S(2)}) collective-permute-start(bf16[640,512]{1,0:T(8,128)(2,1)S(1)} %collective-permute-done.1.refs_4_), channel_id=1, source_target_pairs={{0,64},{64,0},{128,192},{192,128},{1,65},{65,1},{129,193},{193,129... | collective-permute-start | bytes 1966088 | tf_op jit(solution)/shard_map/ppermute | solution.py:275
  52.5 7.0 %collective-permute-start.12 = (bf16[640,512]{1,0:T(8,128)(2,1)S(1)}, bf16[640,512]{1,0:T(8,128)(2,1)S(1)}, u32[]{:S(2)}, u32[]{:S(2)}) collective-permute-start(bf16[640,512]{1,0:T(8,128)(2,1)S(1)} %collective-permute-done.4.refs_5_), channel_id=1, source_target_pairs={{0,64},{64,0},{128,192},{192,128},{1,65},{65,1},{129,193},{193,129... | collective-permute-start | bytes 1966088 | tf_op jit(solution)/shard_map/ppermute | solution.py:275
  52.6 6.9 %collective-permute-start.14 = (bf16[640,512]{1,0:T(8,128)(2,1)S(1)}, bf16[640,512]{1,0:T(8,128)(2,1)S(1)}, u32[]{:S(2)}, u32[]{:S(2)}) collective-permute-start(bf16[640,512]{1,0:T(8,128)(2,1)S(1)} %collective-permute-done.5.refs_7_), channel_id=1, source_target_pairs={{0,64},{64,0},{128,192},{192,128},{1,65},{65,1},{129,193},{193,129... | collective-permute-start | bytes 1966088 | tf_op jit(solution)/shard_map/ppermute | solution.py:275
  53.0 6.6 %collective-permute-start.9 = (bf16[640,512]{1,0:T(8,128)(2,1)S(1)}, bf16[640,512]{1,0:T(8,128)(2,1)S(1)}, u32[]{:S(2)}, u32[]{:S(2)}) collective-permute-start(bf16[640,512]{1,0:T(8,128)(2,1)S(1)} %collective-permute-done.3.refs_2_), channel_id=1, source_target_pairs={{0,64},{64,0},{128,192},{192,128},{1,65},{65,1},{129,193},{193,129... | collective-permute-start | bytes 1966088 | tf_op jit(solution)/shard_map/ppermute | solution.py:275
  92.7 5.5 %collective-permute-start.15 = (bf16[4,640,512]{2,1,0:T(8,128)(2,1)S(1)}, bf16[4,640,512]{2,1,0:T(8,128)(2,1)S(1)}, u32[]{:S(2)}, u32[]{:S(2)}) collective-permute-start(bf16[4,640,512]{2,1,0:T(8,128)(2,1)S(1)} %shard_map.70), channel_id=1, source_target_pairs={{0,64},{64,0},{128,192},{192,128},{1,65},{65,1},{129,193},{193,129... | collective-permute-start | bytes 7864328 | tf_op jit(solution)/shard_map/ppermute | solution.py:275
  99.3 17.6 %collective-permute-start.16 = (bf16[640,512]{1,0:T(8,128)(2,1)S(1)}, bf16[640,512]{1,0:T(8,128)(2,1)S(1)}, u32[]{:S(2)}, u32[]{:S(2)}) collective-permute-start(bf16[640,512]{1,0:T(8,128)(2,1)S(1)} %get-tuple-element.30), channel_id=1, source_target_pairs={{0,2},{1,3},{2,0},{3,1},{4,6},{5,7},{6,4},{7,5},{8,10},{9,11},{10,... | collective-permute-start | bytes 1966088 | tf_op jit(solution)/shard_map/ppermute | solution.py:306
  102.1 29.0 %collective-permute-start.18 = (bf16[640,512]{1,0:T(8,128)(2,1)S(1)}, bf16[640,512]{1,0:T(8,128)(2,1)S(1)}, u32[]{:S(2)}, u32[]{:S(2)}) collective-permute-start(bf16[640,512]{1,0:T(8,128)(2,1)S(1)} %get-tuple-element.31), channel_id=1, source_target_pairs={{0,3},{1,0},{2,1},{3,2},{4,7},{5,4},{6,5},{7,6},{8,11},{9,8},{10,9... | collective-permute-start | bytes 1966088 | tf_op jit(solution)/shard_map/ppermute | solution.py:306
  102.9 28.7 %collective-permute-start.17 = (bf16[640,512]{1,0:T(8,128)(2,1)S(1)}, bf16[640,512]{1,0:T(8,128)(2,1)S(1)}, u32[]{:S(2)}, u32[]{:S(2)}) collective-permute-start(bf16[640,512]{1,0:T(8,128)(2,1)S(1)} %get-tuple-element.32), channel_id=1, source_target_pairs={{0,1},{1,2},{2,3},{3,0},{4,5},{5,6},{6,7},{7,4},{8,9},{9,10},{10,1... | collective-permute-start | bytes 1966088 | tf_op jit(solution)/shard_map/ppermute | solution.py:306
  132.1 9.0 %collective-permute-start.19 = (bf16[640,256]{1,0:T(8,128)(2,1)S(1)}, bf16[640,256]{1,0:T(8,128)(2,1)S(1)}, u32[]{:S(2)}, u32[]{:S(2)}) collective-permute-start(bf16[640,256]{1,0:T(8,128)(2,1)S(1)} %slice.63), channel_id=1, source_target_pairs={{0,4},{1,5},{2,6},{3,7},{4,0},{5,1},{6,2},{7,3},{8,12},{9,13},{10,... | collective-permute-start | bytes 983048 | tf_op jit(solution)/shard_map/ppermute | solution.py:308
  142.5 14.5 %collective-permute-start.20 = (bf16[1024,256]{1,0:T(8,128)(2,1)}, bf16[1024,256]{1,0:T(8,128)(2,1)S(1)}, u32[]{:S(2)}, u32[]{:S(2)}) collective-permute-start(bf16[1024,256]{1,0:T(8,128)(2,1)} %bitcast.23), channel_id=1, source_target_pairs={{0,128},{64,192},{128,0},{192,64},{1,129},{65,193},{129,1},{193,65... | collective-permute-start | bytes 1572872 | tf_op jit(solution)/shard_map/ppermute | solution.py:312
  145.2 13.3 %collective-permute-start.21 = (bf16[1024,256]{1,0:T(8,128)(2,1)}, bf16[1024,256]{1,0:T(8,128)(2,1)S(1)}, u32[]{:S(2)}, u32[]{:S(2)}) collective-permute-start(bf16[1024,256]{1,0:T(8,128)(2,1)} %bitcast.24), channel_id=1, source_target_pairs={{0,64},{64,0},{128,192},{192,128},{1,65},{65,1},{129,193},{193,129... | collective-permute-start | bytes 1572872 | tf_op jit(solution)/shard_map/ppermute | solution.py:275
  157.0 3.1 %collective-permute-start.22 = (bf16[1024,256]{1,0:T(8,128)(2,1)S(1)}, bf16[1024,256]{1,0:T(8,128)(2,1)S(1)}, u32[]{:S(2)}, u32[]{:S(2)}) collective-permute-start(bf16[1024,256]{1,0:T(8,128)(2,1)S(1)} %collective-permute-done.20), channel_id=1, source_target_pairs={{0,64},{64,0},{128,192},{192,128},{1,65},{65,1},{129,193},{193,129... | collective-permute-start | bytes 1572872 | tf_op jit(solution)/shard_map/ppermute | solution.py:275
  (15 other events, 194.8 us)
Sparse Core Ops, SparseCore 0:
  10.4 58.6 all-gather.2
  88.5 53.9 reduce-scatter.1

commit v4 on v3

--- a/solution.py
+++ b/solution.py
@@ -54,30 +54,41 @@
     return pl.multiple_of(((col & 4) ^ (4 * (k >> 2)) | ((col + k) & 3)) * size, size)
 
 
-def pack_kernel(place, activations, upstream, weight_in, weight_out, mine, packed):
-    part = activations.shape[1]
+def weights_kernel(place, weight_in, weight_out, packed):
+    part = weight_in.shape[0]
     half = packed.shape[0] // 2
     at = pl.multiple_of(place[2] * half, half)
     for q in range(half // part):
         packed[pl.ds(q * part, part), :] = weight_in[:, pl.ds(pl.multiple_of(at + q * part, part), part)]
     packed[pl.ds(half, half), :] = weight_out[pl.ds(at, half), :]
+
+
+def pack_weights(place, weight_in, weight_out):
+    part, half = weight_in.shape[0], weight_in.shape[1] // 2
+    return pl.pallas_call(
+        weights_kernel,
+        out_shape=jax.ShapeDtypeStruct((2 * half, part), jnp.bfloat16),
+        in_specs=[smem(), vmem(), vmem()],
+        out_specs=vmem(),
+        compiler_params=pltpu.CompilerParams(vmem_limit_bytes=VMEM_LIMIT),
+    )(place, weight_in, weight_out)
+
+
+def tokens_kernel(activations, upstream, mine):
+    part = activations.shape[1]
     mine[:, pl.ds(0, part)] = activations[...]
     mine[:, pl.ds(part, part)] = upstream[...]
 
 
-def pack(place, activations, upstream, weight_in, weight_out):
+def pack_tokens(activations, upstream):
     tokens, part = activations.shape
-    half = weight_in.shape[1] // 2
-    return pl.pallas_call(
-        pack_kernel,
-        out_shape=(
-            jax.ShapeDtypeStruct((tokens, 2 * part), jnp.bfloat16),
-            jax.ShapeDtypeStruct((2 * half, part), jnp.bfloat16),
-        ),
-        in_specs=[smem()] + [vmem()] * 4,
-        out_specs=(vmem(), vmem()),
+    return pl.pallas_call(
+        tokens_kernel,
+        out_shape=jax.ShapeDtypeStruct((tokens, 2 * part), jnp.bfloat16),
+        in_specs=[vmem(), vmem()],
+        out_specs=vmem(),
         compiler_params=pltpu.CompilerParams(vmem_limit_bytes=VMEM_LIMIT),
-    )(place, activations, upstream, weight_in, weight_out)
+    )(activations, upstream)
 
 
 def token_copies(col, own, sib, x_all, g_all, x_sem, g_sem, tokens, part):
@@ -142,19 +153,17 @@
         for c in range(8)
     ]
     start(w_copies, x_copies[0])
-    wait(w_copies, x_copies[0])
+    wait(w_copies)
     start(v_copies, g_copies[0])
+    wait(x_copies[0])
     for side in range(2):
         rows = pl.ds(side * tokens, tokens)
-        if side:
-            wait(x_copies[1])
         pre = jnp.dot(x_all[rows, :], w_in[...], preferred_element_type=jnp.float32)
         if side == 0:
+            wait(v_copies)
             start(x_copies[1])
-            wait(v_copies, g_copies[0])
+            wait(g_copies[0])
             start(g_copies[1])
-        else:
-            wait(g_copies[1])
         back = lax.dot_general(
             g_all[rows, :], w_out[...], (((1,), (1,)), ((), ())), preferred_element_type=jnp.float32
         )
@@ -168,6 +177,8 @@
         dpre_ref[rows, :] = dpre
         both[pl.ds(0, half), rows] = dpre.T
         both[pl.ds(half, half), rows] = act.astype(jnp.bfloat16).T
+        if side == 0:
+            wait(x_copies[1], g_copies[1])
 
     outs = []
     for c in range(8):
@@ -257,6 +268,31 @@
     )
 
 
+def output_kernel(place, *refs):
+    (share, away, other_share, other_away), (in_ref, out_ref) = refs[:4], refs[4:]
+    half = share.shape[0] // 2
+    core = place[2]
+    for at, near, far in ((core, share, away), (1 - core, other_share, other_away)):
+        at = pl.ds(pl.multiple_of(at * half, half), half)
+        total = near[...].astype(jnp.float32) + far[...].astype(jnp.float32)
+        in_ref[:, at] = total[:half].T
+        out_ref[at, :] = total[half:]
+
+
+def weight_outputs(place, *shares):
+    double, part = shares[0].shape
+    return pl.pallas_call(
+        output_kernel,
+        out_shape=(
+            jax.ShapeDtypeStruct((part, double), jnp.float32),
+            jax.ShapeDtypeStruct((double, part), jnp.float32),
+        ),
+        in_specs=[smem()] + [vmem()] * 4,
+        out_specs=(vmem(), vmem()),
+        compiler_params=pltpu.CompilerParams(vmem_limit_bytes=VMEM_LIMIT),
+    )(place, *shares)
+
+
 def add(*terms):
     total = terms[0].astype(jnp.float32)
     for term in terms[1:]:
@@ -279,8 +315,9 @@
             jnp.where(first, up, down), ("depth", "col"), by_core(along_x(-1), along_x(1))
         )
 
-    mine, packed = pack(place, activations, upstream, weight_in, weight_out)
+    packed = pack_weights(place, weight_in, weight_out)
     weights = lax.all_gather(packed, "row", axis=0, tiled=False)
+    mine = pack_tokens(activations, after(upstream, packed))
 
     own = {0: mine}
     own[1] = lax.ppermute(mine, "col", along_x(-1))
@@ -310,11 +347,7 @@
 
     shares = after(shares, grad_input)
     away = lax.ppermute(shares, "depth", Y_HI)
-    here, there = add(shares, away), add(swap(shares), swap(away))
-    left, right = jnp.where(first, here, there), jnp.where(first, there, here)
-    half = shares.shape[0] // 2
-    grad_weight_in = jnp.concatenate([left[:half].T, right[:half].T], axis=1)
-    grad_weight_out = jnp.concatenate([left[half:], right[half:]], axis=0)
+    grad_weight_in, grad_weight_out = weight_outputs(place, shares, away, swap(shares), swap(away))
     return (grad_input, grad_weight_in, grad_weight_out)
 
 

time: 171 us -> 169 us (0.988)
  Pallas kernels: 29.4 us -> 32.4 us
  other arithmetic: 5.19 us -> 2.76 us
    pallas_call x1 -> x3, Pallas kernels: 2.48 us -> 7.23 us  [the longest x1 3.21 us: weight_outputs(): pl.pallas_call(output_kernel, out_shape=(jax.ShapeDtypeStruct((part, doub...]
    all_gather x1, waiting for transfers between devices: 7.43 us -> 5.46 us  [on_device(): weights = lax.all_gather(packed, 'row', axis=0, tiled=False)]
    pallas_call x1, Pallas kernels: 19.2 us -> 17.5 us  [forward(): pl.pallas_call(functools.partial(forward_kernel, tokens=tokens, part=part...]
    unnamed x29 -> x34, local copies, waits for them, and re-layouts: 3.95 us -> 3.48 us
  transfers between devices with their start and end apart: 25 -> 25, of which waited for: 13 -> 13; matrix products, arithmetic and copies ran while one was open for 1% -> 1% of each run, Pallas kernels for 4% -> 6%
where the time goes in v4:
time: 169 us
  waiting for transfers between devices  85 us (50%)
  Pallas kernels  32.4 us (19%)
  starting transfers between devices  30.8 us (18%)
  between operations  14.2 us (8%)
  local copies, waits for them, and re-layouts  3.65 us (2%)
  other arithmetic  2.76 us (2%)
    ppermute x3, waiting for transfers between devices, on_device(): moved = [lax.ppermute(joined[k], 'col', along_x(k)) for k in (2, 1, 3)]  28.1 us
    pallas_call x1, Pallas kernels, forward(): pl.pallas_call(functools.partial(forward_kernel, tokens=tokens, part=part...  17.5 us
    ppermute x11, starting transfers between devices, swap(): return lax.ppermute(chunk, 'depth', CORE)  13.6 us
    ppermute x1, waiting for transfers between devices, on_device(): own[4] = lax.ppermute(mine, 'col', Y_LO)  10.9 us
    ppermute x1, waiting for transfers between devices, on_device(): away = lax.ppermute(shares, 'depth', Y_HI)  10.8 us
    ppermute x2, waiting for transfers between devices, across(): lax.ppermute(jnp.where(first, up, down), ('depth', 'col'), by_core(along_...  10.3 us
    ppermute x1, waiting for transfers between devices, on_device(): own[7] = lax.ppermute(own[4], 'col', along_x(1))  8.82 us
    ppermute x1, waiting for transfers between devices, on_device(): passed = lax.ppermute(total[:, part:].astype(bf16), 'col', Y_LO)  7.73 us
  transfers between devices with their start and end apart: 25, of which 13 were waited for; matrix products, arithmetic and copies ran while one was open for 1% of the time, Pallas kernels for 6%

profile of v4, /device:TPU:1, one launch (start us, length us, event | category | flops | bytes accessed | tf_op | source)
XLA Modules:
  0.0 168.8 jit_solution(5153818611300750021)
XLA Ops:
  7.8 2.1 %shard_map.67 = bf16[1024,256]{1,0:T(8,128)(2,1)} custom-call(s32[3]{0:T(128)} %pad_add_fusion.place, bf16[256,1024]{1,0:T(8,128)(2,1)} %weight_in.1, bf16[1024,256]{1,0:T(8,128)(2,1)} %weight_out.1), custom_call_target="tpu_custom_call" | custom-call | tf_op jit(solution)/shard_map/pallas_call | solution.py:68
  9.9 2.0 %shard_map.68.refs_0_ = bf16[640,512]{1,0:T(8,128)(2,1)} custom-call(bf16[640,256]{1,0:T(8,128)(2,1)} %activations.1, bf16[640,256]{1,0:T(8,128)(2,1)} %upstream), custom_call_target="tpu_custom_call" | custom-call | tf_op jit(solution)/shard_map/pallas_call | solution.py:85
  11.9 2.1 %collective-permute-start.1 = (bf16[640,512]{1,0:T(8,128)(2,1)}, bf16[640,512]{1,0:T(8,128)(2,1)S(1)}, u32[]{:S(2)}, u32[]{:S(2)}) collective-permute-start(bf16[640,512]{1,0:T(8,128)(2,1)} %shard_map.68.refs_0_), channel_id=1, source_target_pairs={{0,4},{1,5},{2,6},{3,7},{4,0},{5,1},{6,2},{7,3},{8,12},{9,13},{10,... | collective-permute-start | bytes 1966088 | tf_op jit(solution)/shard_map/ppermute | solution.py:325
  16.7 10.9 %collective-permute-done.1.refs_4_ = bf16[640,512]{1,0:T(8,128)(2,1)S(1)} collective-permute-done((bf16[640,512]{1,0:T(8,128)(2,1)}, bf16[640,512]{1,0:T(8,128)(2,1)S(1)}, u32[]{:S(2)}, u32[]{:S(2)}) %collective-permute-start.1) | collective-permute-done | bytes 655392 | tf_op jit(solution)/shard_map/ppermute | solution.py:325
  27.6 2.3 %collective-permute-start.5 = (bf16[640,512]{1,0:T(8,128)(2,1)S(1)}, bf16[640,512]{1,0:T(8,128)(2,1)S(1)}, u32[]{:S(2)}, u32[]{:S(2)}) collective-permute-start(bf16[640,512]{1,0:T(8,128)(2,1)S(1)} %collective-permute-done.1.refs_4_), channel_id=1, source_target_pairs={{0,1},{1,2},{2,3},{3,0},{4,5},{5,6},{6,7},{7,4},{8,9},{9,10},{10,1... | collective-permute-start | bytes 1966088 | tf_op jit(solution)/shard_map/ppermute | solution.py:328
  31.1 2.0 %collective-permute-start.7 = (bf16[640,512]{1,0:T(8,128)(2,1)}, bf16[640,512]{1,0:T(8,128)(2,1)}, u32[]{:S(2)}, u32[]{:S(2)}) collective-permute-start(bf16[640,512]{1,0:T(8,128)(2,1)} %shard_map.68.refs_0_), channel_id=1, source_target_pairs={{0,64},{64,0},{128,192},{192,128},{1,65},{65,1},{129,193},{193,129... | collective-permute-start | bytes 1966088 | tf_op jit(solution)/shard_map/ppermute | solution.py:311
  33.5 2.2 %collective-permute-start.8 = (bf16[640,512]{1,0:T(8,128)(2,1)S(1)}, bf16[640,512]{1,0:T(8,128)(2,1)S(1)}, u32[]{:S(2)}, u32[]{:S(2)}) collective-permute-start(bf16[640,512]{1,0:T(8,128)(2,1)S(1)} %collective-permute-done.refs_1_), channel_id=1, source_target_pairs={{0,64},{64,0},{128,192},{192,128},{1,65},{65,1},{129,193},{193,129... | collective-permute-start | bytes 1966088 | tf_op jit(solution)/shard_map/ppermute | solution.py:311
  35.7 8.8 %collective-permute-done.5.refs_7_ = bf16[640,512]{1,0:T(8,128)(2,1)S(1)} collective-permute-done((bf16[640,512]{1,0:T(8,128)(2,1)S(1)}, bf16[640,512]{1,0:T(8,128)(2,1)S(1)}, u32[]{:S(2)}, u32[]{:S(2)}) %collective-permute-start.5) | collective-permute-done | bytes 655392 | tf_op jit(solution)/shard_map/ppermute | solution.py:328
  44.5 4.3 %collective-permute-start.10 = (bf16[640,512]{1,0:T(8,128)(2,1)S(1)}, bf16[640,512]{1,0:T(8,128)(2,1)S(1)}, u32[]{:S(2)}, u32[]{:S(2)}) collective-permute-start(bf16[640,512]{1,0:T(8,128)(2,1)S(1)} %collective-permute-done.2.refs_3_), channel_id=1, source_target_pairs={{0,64},{64,0},{128,192},{192,128},{1,65},{65,1},{129,193},{193,129... | collective-permute-start | bytes 1966088 | tf_op jit(solution)/shard_map/ppermute | solution.py:311
  49.1 4.4 %collective-permute-done.3.refs_2_ = bf16[640,512]{1,0:T(8,128)(2,1)S(1)} collective-permute-done((bf16[640,512]{1,0:T(8,128)(2,1)S(1)}, bf16[640,512]{1,0:T(8,128)(2,1)S(1)}, u32[]{:S(2)}, u32[]{:S(2)}) %collective-permute-start.3) | collective-permute-done | bytes 655392 | tf_op jit(solution)/shard_map/ppermute | solution.py:314
  54.7 5.9 %collective-permute-done.6.refs_6_ = bf16[640,512]{1,0:T(8,128)(2,1)S(1)} collective-permute-done((bf16[640,512]{1,0:T(8,128)(2,1)S(1)}, bf16[640,512]{1,0:T(8,128)(2,1)S(1)}, u32[]{:S(2)}, u32[]{:S(2)}) %collective-permute-start.6) | collective-permute-done | bytes 655392 | tf_op jit(solution)/shard_map/ppermute | solution.py:314
  63.2 5.5 %all-gather.3.cloned.1.call-done = bf16[8192,256]{1,0:T(8,128)(2,1)} async-done(((bf16[1024,256]{1,0:T(8,128)(2,1)}), bf16[8192,256]{1,0:T(8,128)(2,1)}) %all-gather.3.cloned.1.call-update) | async-done | bytes 4194320 | tf_op jit(solution)/shard_map/all_gather | solution.py:319
  68.7 17.5 %shard_map.69 = (bf16[1280,512]{1,0:T(8,128)(2,1)S(1)}, bf16[8,1024,256]{2,1,0:T(8,128)(2,1)}) custom-call(s32[3]{0:T(128)} %pad_add_fusion.place, bf16[640,512]{1,0:T(8,128)(2,1)} %shard_map.68.refs_0_, bf16[640,512]{1,0:T(8,128)(2,1)} %copy-done.2, bf16[640,512]{1,0:T(8,128)(2,1)} %copy-done.9, bf16[640,512]{1,0:T(8,128)(2,1)} %copy-done.1, ...), custom_call_target="tpu_custom_call" | custom-call | flops 10737418240 | bytes 23068672 | tf_op jit(solution)/shard_map/pallas_call | solution.py:201
  86.8 3.8 %shard_map.71 = bf16[4,640,512]{2,1,0:T(8,128)(2,1)S(1)} custom-call(s32[3]{0:T(128)S(1)} %copy-done, bf16[1280,512]{1,0:T(8,128)(2,1)S(1)} %get-tuple-element.24.dpre, bf16[8,1024,256]{2,1,0:T(8,128)(2,1)} %bitcast.17), custom_call_target="tpu_custom_call" | custom-call | flops 1342177280 | bytes 5373952 | tf_op jit(solution)/shard_map/pallas_call | solution.py:249
  91.6 3.8 %shard_map.70 = bf16[4,640,512]{2,1,0:T(8,128)(2,1)S(1)} custom-call(s32[3]{0:T(128)S(1)} %copy-done, bf16[1280,512]{1,0:T(8,128)(2,1)S(1)} %get-tuple-element.24.dpre, bf16[8,1024,256]{2,1,0:T(8,128)(2,1)} %bitcast.18), custom_call_target="tpu_custom_call" | custom-call | flops 1342177280 | bytes 5373952 | tf_op jit(solution)/shard_map/pallas_call | solution.py:249
  97.2 2.8 %collective-permute-start.16 = (bf16[640,512]{1,0:T(8,128)(2,1)S(1)}, bf16[640,512]{1,0:T(8,128)(2,1)S(1)}, u32[]{:S(2)}, u32[]{:S(2)}) collective-permute-start(bf16[640,512]{1,0:T(8,128)(2,1)S(1)} %get-tuple-element.29), channel_id=1, source_target_pairs={{0,2},{1,3},{2,0},{3,1},{4,6},{5,7},{6,4},{7,5},{8,10},{9,11},{10,... | collective-permute-start | bytes 1966088 | tf_op jit(solution)/shard_map/ppermute | solution.py:343
  101.4 13.3 %collective-permute-done.16 = bf16[640,512]{1,0:T(8,128)(2,1)S(1)} collective-permute-done((bf16[640,512]{1,0:T(8,128)(2,1)S(1)}, bf16[640,512]{1,0:T(8,128)(2,1)S(1)}, u32[]{:S(2)}, u32[]{:S(2)}) %collective-permute-start.16) | collective-permute-done | bytes 655392 | tf_op jit(solution)/shard_map/ppermute | solution.py:343
  114.7 14.2 %collective-permute-done.18 = bf16[640,512]{1,0:T(8,128)(2,1)S(1)} collective-permute-done((bf16[640,512]{1,0:T(8,128)(2,1)S(1)}, bf16[640,512]{1,0:T(8,128)(2,1)S(1)}, u32[]{:S(2)}, u32[]{:S(2)}) %collective-permute-start.18) | collective-permute-done | bytes 655392 | tf_op jit(solution)/shard_map/ppermute | solution.py:343
  131.2 7.7 %collective-permute-done.19 = bf16[640,256]{1,0:T(8,128)(2,1)S(1)} collective-permute-done((bf16[640,256]{1,0:T(8,128)(2,1)S(1)}, bf16[640,256]{1,0:T(8,128)(2,1)S(1)}, u32[]{:S(2)}, u32[]{:S(2)}) %collective-permute-start.19) | collective-permute-done | bytes 327712 | tf_op jit(solution)/shard_map/ppermute | solution.py:345
  140.3 2.7 %collective-permute-start.20 = (bf16[1024,256]{1,0:T(8,128)(2,1)}, bf16[1024,256]{1,0:T(8,128)(2,1)S(1)}, u32[]{:S(2)}, u32[]{:S(2)}) collective-permute-start(bf16[1024,256]{1,0:T(8,128)(2,1)} %bitcast.19), channel_id=1, source_target_pairs={{0,128},{64,192},{128,0},{192,64},{1,129},{65,193},{129,1},{193,65... | collective-permute-start | bytes 1572872 | tf_op jit(solution)/shard_map/ppermute | solution.py:349
  144.0 10.8 %collective-permute-done.20.refs_1_ = bf16[1024,256]{1,0:T(8,128)(2,1)S(1)} collective-permute-done((bf16[1024,256]{1,0:T(8,128)(2,1)}, bf16[1024,256]{1,0:T(8,128)(2,1)S(1)}, u32[]{:S(2)}, u32[]{:S(2)}) %collective-permute-start.20) | collective-permute-done | bytes 524320 | tf_op jit(solution)/shard_map/ppermute | solution.py:349
  154.8 1.5 collective-permute-start.22
  156.4 1.5 collective-permute-done.22.refs_3_
  158.7 3.2 %shard_map.72 = (f32[256,1024]{1,0:T(8,128)}, f32[1024,256]{1,0:T(8,128)}) custom-call(s32[3]{0:T(128)} %pad_add_fusion.place, bf16[1024,256]{1,0:T(8,128)(2,1)} %bitcast.21, bf16[1024,256]{1,0:T(8,128)(2,1)} %copy-done.5, bf16[1024,256]{1,0:T(8,128)(2,1)} %copy-done.6, bf16[1024,256]{1,0:T(8,128)(2,1)} %copy-done.7), custom_call_target="tpu_custom_call" | custom-call | tf_op jit(solution)/shard_map/pallas_call | solution.py:284
  (76 shorter events, 19.1 us)
Async XLA Ops:
  7.2 61.5 %all-gather.3.cloned.1.call-start = ((), (), s32[]{:S(2)}) async-start(), calls=%async_computation.2 | async-start | bytes 4718592 | tf_op jit(solution)/shard_map/all_gather | solution.py:319
  9.9 130.4 %reduce-scatter.2.cloned.1.call-start = ((), (), s32[]{:S(2)}) async-start(), calls=%async_computation.1 | async-start | bytes 4718592 | tf_op jit(solution)/shard_map/reduce_scatter | solution.py:340
  11.9 15.7 %collective-permute-start.1 = (bf16[640,512]{1,0:T(8,128)(2,1)}, bf16[640,512]{1,0:T(8,128)(2,1)S(1)}, u32[]{:S(2)}, u32[]{:S(2)}) collective-permute-start(bf16[640,512]{1,0:T(8,128)(2,1)} %shard_map.68.refs_0_), channel_id=1, source_target_pairs={{0,4},{1,5},{2,6},{3,7},{4,0},{5,1},{6,2},{7,3},{8,12},{9,13},{10,... | collective-permute-start | bytes 1966088 | tf_op jit(solution)/shard_map/ppermute | solution.py:325
  14.0 19.1 %collective-permute-start.2 = (bf16[640,512]{1,0:T(8,128)(2,1)}, bf16[640,512]{1,0:T(8,128)(2,1)S(1)}, u32[]{:S(2)}, u32[]{:S(2)}) collective-permute-start(bf16[640,512]{1,0:T(8,128)(2,1)} %shard_map.68.refs_0_), channel_id=1, source_target_pairs={{0,1},{1,2},{2,3},{3,0},{4,5},{5,6},{6,7},{7,4},{8,9},{9,10},{10,1... | collective-permute-start | bytes 1966088 | tf_op jit(solution)/shard_map/ppermute | solution.py:324
  15.2 17.9 %collective-permute-start = (bf16[640,512]{1,0:T(8,128)(2,1)}, bf16[640,512]{1,0:T(8,128)(2,1)S(1)}, u32[]{:S(2)}, u32[]{:S(2)}) collective-permute-start(bf16[640,512]{1,0:T(8,128)(2,1)} %shard_map.68.refs_0_), channel_id=1, source_target_pairs={{0,3},{1,0},{2,1},{3,2},{4,7},{5,4},{6,5},{7,6},{8,11},{9,8},{10,9... | collective-permute-start | bytes 1966088 | tf_op jit(solution)/shard_map/ppermute | solution.py:323
  27.6 17.0 %collective-permute-start.5 = (bf16[640,512]{1,0:T(8,128)(2,1)S(1)}, bf16[640,512]{1,0:T(8,128)(2,1)S(1)}, u32[]{:S(2)}, u32[]{:S(2)}) collective-permute-start(bf16[640,512]{1,0:T(8,128)(2,1)S(1)} %collective-permute-done.1.refs_4_), channel_id=1, source_target_pairs={{0,1},{1,2},{2,3},{3,0},{4,5},{5,6},{6,7},{7,4},{8,9},{9,10},{10,1... | collective-permute-start | bytes 1966088 | tf_op jit(solution)/shard_map/ppermute | solution.py:328
  29.9 18.9 %collective-permute-start.4 = (bf16[640,512]{1,0:T(8,128)(2,1)S(1)}, bf16[640,512]{1,0:T(8,128)(2,1)S(1)}, u32[]{:S(2)}, u32[]{:S(2)}) collective-permute-start(bf16[640,512]{1,0:T(8,128)(2,1)S(1)} %collective-permute-done.1.refs_4_), channel_id=1, source_target_pairs={{0,3},{1,0},{2,1},{3,2},{4,7},{5,4},{6,5},{7,6},{8,11},{9,8},{10,9... | collective-permute-start | bytes 1966088 | tf_op jit(solution)/shard_map/ppermute | solution.py:327
  31.1 22.9 %collective-permute-start.7 = (bf16[640,512]{1,0:T(8,128)(2,1)}, bf16[640,512]{1,0:T(8,128)(2,1)}, u32[]{:S(2)}, u32[]{:S(2)}) collective-permute-start(bf16[640,512]{1,0:T(8,128)(2,1)} %shard_map.68.refs_0_), channel_id=1, source_target_pairs={{0,64},{64,0},{128,192},{192,128},{1,65},{65,1},{129,193},{193,129... | collective-permute-start | bytes 1966088 | tf_op jit(solution)/shard_map/ppermute | solution.py:311
  33.3 20.3 %collective-permute-start.3 = (bf16[640,512]{1,0:T(8,128)(2,1)S(1)}, bf16[640,512]{1,0:T(8,128)(2,1)S(1)}, u32[]{:S(2)}, u32[]{:S(2)}) collective-permute-start(bf16[640,512]{1,0:T(8,128)(2,1)S(1)} %broadcast_select_fusion.1), channel_id=1, source_target_pairs={{0,3},{1,0},{2,1},{3,2},{4,7},{5,4},{6,5},{7,6},{64,65},{65,66},{6... | collective-permute-start | bytes 1966088 | tf_op jit(solution)/shard_map/ppermute | solution.py:314
  33.5 20.6 %collective-permute-start.8 = (bf16[640,512]{1,0:T(8,128)(2,1)S(1)}, bf16[640,512]{1,0:T(8,128)(2,1)S(1)}, u32[]{:S(2)}, u32[]{:S(2)}) collective-permute-start(bf16[640,512]{1,0:T(8,128)(2,1)S(1)} %collective-permute-done.refs_1_), channel_id=1, source_target_pairs={{0,64},{64,0},{128,192},{192,128},{1,65},{65,1},{129,193},{193,129... | collective-permute-start | bytes 1966088 | tf_op jit(solution)/shard_map/ppermute | solution.py:311
  44.5 10.0 %collective-permute-start.10 = (bf16[640,512]{1,0:T(8,128)(2,1)S(1)}, bf16[640,512]{1,0:T(8,128)(2,1)S(1)}, u32[]{:S(2)}, u32[]{:S(2)}) collective-permute-start(bf16[640,512]{1,0:T(8,128)(2,1)S(1)} %collective-permute-done.2.refs_3_), channel_id=1, source_target_pairs={{0,64},{64,0},{128,192},{192,128},{1,65},{65,1},{129,193},{193,129... | collective-permute-start | bytes 1966088 | tf_op jit(solution)/shard_map/ppermute | solution.py:311
  48.9 11.7 %collective-permute-start.6 = (bf16[640,512]{1,0:T(8,128)(2,1)S(1)}, bf16[640,512]{1,0:T(8,128)(2,1)S(1)}, u32[]{:S(2)}, u32[]{:S(2)}) collective-permute-start(bf16[640,512]{1,0:T(8,128)(2,1)S(1)} %broadcast_select_fusion), channel_id=1, source_target_pairs={{0,3},{1,0},{2,1},{3,2},{4,7},{5,4},{6,5},{7,6},{64,65},{65,66},{6... | collective-permute-start | bytes 1966088 | tf_op jit(solution)/shard_map/ppermute | solution.py:314
  53.6 7.5 %collective-permute-start.11 = (bf16[640,512]{1,0:T(8,128)(2,1)S(1)}, bf16[640,512]{1,0:T(8,128)(2,1)S(1)}, u32[]{:S(2)}, u32[]{:S(2)}) collective-permute-start(bf16[640,512]{1,0:T(8,128)(2,1)S(1)} %collective-permute-done.1.refs_4_), channel_id=1, source_target_pairs={{0,64},{64,0},{128,192},{192,128},{1,65},{65,1},{129,193},{193,129... | collective-permute-start | bytes 1966088 | tf_op jit(solution)/shard_map/ppermute | solution.py:311
  54.0 7.0 %collective-permute-start.12 = (bf16[640,512]{1,0:T(8,128)(2,1)S(1)}, bf16[640,512]{1,0:T(8,128)(2,1)S(1)}, u32[]{:S(2)}, u32[]{:S(2)}) collective-permute-start(bf16[640,512]{1,0:T(8,128)(2,1)S(1)} %collective-permute-done.4.refs_5_), channel_id=1, source_target_pairs={{0,64},{64,0},{128,192},{192,128},{1,65},{65,1},{129,193},{193,129... | collective-permute-start | bytes 1966088 | tf_op jit(solution)/shard_map/ppermute | solution.py:311
  54.1 6.9 %collective-permute-start.14 = (bf16[640,512]{1,0:T(8,128)(2,1)S(1)}, bf16[640,512]{1,0:T(8,128)(2,1)S(1)}, u32[]{:S(2)}, u32[]{:S(2)}) collective-permute-start(bf16[640,512]{1,0:T(8,128)(2,1)S(1)} %collective-permute-done.5.refs_7_), channel_id=1, source_target_pairs={{0,64},{64,0},{128,192},{192,128},{1,65},{65,1},{129,193},{193,129... | collective-permute-start | bytes 1966088 | tf_op jit(solution)/shard_map/ppermute | solution.py:311
  54.6 6.6 %collective-permute-start.9 = (bf16[640,512]{1,0:T(8,128)(2,1)S(1)}, bf16[640,512]{1,0:T(8,128)(2,1)S(1)}, u32[]{:S(2)}, u32[]{:S(2)}) collective-permute-start(bf16[640,512]{1,0:T(8,128)(2,1)S(1)} %collective-permute-done.3.refs_2_), channel_id=1, source_target_pairs={{0,64},{64,0},{128,192},{192,128},{1,65},{65,1},{129,193},{193,129... | collective-permute-start | bytes 1966088 | tf_op jit(solution)/shard_map/ppermute | solution.py:311
  90.6 5.5 %collective-permute-start.15 = (bf16[4,640,512]{2,1,0:T(8,128)(2,1)S(1)}, bf16[4,640,512]{2,1,0:T(8,128)(2,1)S(1)}, u32[]{:S(2)}, u32[]{:S(2)}) collective-permute-start(bf16[4,640,512]{2,1,0:T(8,128)(2,1)S(1)} %shard_map.71), channel_id=1, source_target_pairs={{0,64},{64,0},{128,192},{192,128},{1,65},{65,1},{129,193},{193,129... | collective-permute-start | bytes 7864328 | tf_op jit(solution)/shard_map/ppermute | solution.py:311
  97.2 17.6 %collective-permute-start.16 = (bf16[640,512]{1,0:T(8,128)(2,1)S(1)}, bf16[640,512]{1,0:T(8,128)(2,1)S(1)}, u32[]{:S(2)}, u32[]{:S(2)}) collective-permute-start(bf16[640,512]{1,0:T(8,128)(2,1)S(1)} %get-tuple-element.29), channel_id=1, source_target_pairs={{0,2},{1,3},{2,0},{3,1},{4,6},{5,7},{6,4},{7,5},{8,10},{9,11},{10,... | collective-permute-start | bytes 1966088 | tf_op jit(solution)/shard_map/ppermute | solution.py:343
  99.9 29.0 %collective-permute-start.18 = (bf16[640,512]{1,0:T(8,128)(2,1)S(1)}, bf16[640,512]{1,0:T(8,128)(2,1)S(1)}, u32[]{:S(2)}, u32[]{:S(2)}) collective-permute-start(bf16[640,512]{1,0:T(8,128)(2,1)S(1)} %get-tuple-element.30), channel_id=1, source_target_pairs={{0,3},{1,0},{2,1},{3,2},{4,7},{5,4},{6,5},{7,6},{8,11},{9,8},{10,9... | collective-permute-start | bytes 1966088 | tf_op jit(solution)/shard_map/ppermute | solution.py:343
  100.8 28.7 %collective-permute-start.17 = (bf16[640,512]{1,0:T(8,128)(2,1)S(1)}, bf16[640,512]{1,0:T(8,128)(2,1)S(1)}, u32[]{:S(2)}, u32[]{:S(2)}) collective-permute-start(bf16[640,512]{1,0:T(8,128)(2,1)S(1)} %get-tuple-element.31), channel_id=1, source_target_pairs={{0,1},{1,2},{2,3},{3,0},{4,5},{5,6},{6,7},{7,4},{8,9},{9,10},{10,1... | collective-permute-start | bytes 1966088 | tf_op jit(solution)/shard_map/ppermute | solution.py:343
  129.9 9.0 %collective-permute-start.19 = (bf16[640,256]{1,0:T(8,128)(2,1)S(1)}, bf16[640,256]{1,0:T(8,128)(2,1)S(1)}, u32[]{:S(2)}, u32[]{:S(2)}) collective-permute-start(bf16[640,256]{1,0:T(8,128)(2,1)S(1)} %slice.41), channel_id=1, source_target_pairs={{0,4},{1,5},{2,6},{3,7},{4,0},{5,1},{6,2},{7,3},{8,12},{9,13},{10,... | collective-permute-start | bytes 983048 | tf_op jit(solution)/shard_map/ppermute | solution.py:345
  140.3 14.5 %collective-permute-start.20 = (bf16[1024,256]{1,0:T(8,128)(2,1)}, bf16[1024,256]{1,0:T(8,128)(2,1)S(1)}, u32[]{:S(2)}, u32[]{:S(2)}) collective-permute-start(bf16[1024,256]{1,0:T(8,128)(2,1)} %bitcast.19), channel_id=1, source_target_pairs={{0,128},{64,192},{128,0},{192,64},{1,129},{65,193},{129,1},{193,65... | collective-permute-start | bytes 1572872 | tf_op jit(solution)/shard_map/ppermute | solution.py:349
  143.1 13.3 %collective-permute-start.21 = (bf16[1024,256]{1,0:T(8,128)(2,1)}, bf16[1024,256]{1,0:T(8,128)(2,1)S(1)}, u32[]{:S(2)}, u32[]{:S(2)}) collective-permute-start(bf16[1024,256]{1,0:T(8,128)(2,1)} %bitcast.20), channel_id=1, source_target_pairs={{0,64},{64,0},{128,192},{192,128},{1,65},{65,1},{129,193},{193,129... | collective-permute-start | bytes 1572872 | tf_op jit(solution)/shard_map/ppermute | solution.py:311
  154.8 3.1 %collective-permute-start.22 = (bf16[1024,256]{1,0:T(8,128)(2,1)S(1)}, bf16[1024,256]{1,0:T(8,128)(2,1)S(1)}, u32[]{:S(2)}, u32[]{:S(2)}) collective-permute-start(bf16[1024,256]{1,0:T(8,128)(2,1)S(1)} %collective-permute-done.20.refs_1_), channel_id=1, source_target_pairs={{0,64},{64,0},{128,192},{192,128},{1,65},{65,1},{129,193},{193,129... | collective-permute-start | bytes 1572872 | tf_op jit(solution)/shard_map/ppermute | solution.py:311
  (18 other events, 190.7 us)
Sparse Core Ops, SparseCore 0:
  10.0 58.6 all-gather.2
  86.3 53.9 reduce-scatter.1

commit v5 on v4

--- a/solution.py
+++ b/solution.py
@@ -268,13 +268,12 @@
     )
 
 
-def output_kernel(place, *refs):
-    (share, away, other_share, other_away), (in_ref, out_ref) = refs[:4], refs[4:]
-    half = share.shape[0] // 2
+def output_kernel(place, here, other_share, other_away, in_ref, out_ref):
+    half = here.shape[0] // 2
     core = place[2]
-    for at, near, far in ((core, share, away), (1 - core, other_share, other_away)):
+    there = other_share[...].astype(jnp.float32) + other_away[...].astype(jnp.float32)
+    for at, total in ((core, here[...]), (1 - core, there)):
         at = pl.ds(pl.multiple_of(at * half, half), half)
-        total = near[...].astype(jnp.float32) + far[...].astype(jnp.float32)
         in_ref[:, at] = total[:half].T
         out_ref[at, :] = total[half:]
 
@@ -287,10 +286,10 @@
             jax.ShapeDtypeStruct((part, double), jnp.float32),
             jax.ShapeDtypeStruct((double, part), jnp.float32),
         ),
-        in_specs=[smem()] + [vmem()] * 4,
+        in_specs=[smem()] + [vmem()] * 3,
         out_specs=(vmem(), vmem()),
-        compiler_params=pltpu.CompilerParams(vmem_limit_bytes=VMEM_LIMIT),
-    )(place, *shares)
+        compiler_params=pltpu.CompilerParams(vmem_limit_bytes=32 * 1024 * 1024),
+    )(place, *[pltpu.with_memory_space_constraint(share, pltpu.VMEM) for share in shares])
 
 
 def add(*terms):
@@ -347,7 +346,9 @@
 
     shares = after(shares, grad_input)
     away = lax.ppermute(shares, "depth", Y_HI)
-    grad_weight_in, grad_weight_out = weight_outputs(place, shares, away, swap(shares), swap(away))
+    grad_weight_in, grad_weight_out = weight_outputs(
+        place, add(shares, away), swap(shares), swap(away)
+    )
     return (grad_input, grad_weight_in, grad_weight_out)
 
 

time: 169 us -> 167 us (0.988)
    unnamed x34 -> x28, local copies, waits for them, and re-layouts: 3.48 us -> 2.7 us
  transfers between devices with their start and end apart: 25 -> 25, of which waited for: 13 -> 13; matrix products, arithmetic and copies ran while one was open for 1% -> 2% of each run, Pallas kernels for 6% -> 6%
where the time goes in v5:
time: 167 us
  waiting for transfers between devices  83.7 us (50%)
  Pallas kernels  31.4 us (19%)
  starting transfers between devices  30.8 us (18%)
  between operations  14.2 us (9%)
  other arithmetic  3.93 us (2%)
  local copies, waits for them, and re-layouts  2.88 us (2%)
    ppermute x3, waiting for transfers between devices, on_device(): moved = [lax.ppermute(joined[k], 'col', along_x(k)) for k in (2, 1, 3)]  28.1 us
    pallas_call x1, Pallas kernels, forward(): pl.pallas_call(functools.partial(forward_kernel, tokens=tokens, part=part...  17.5 us
    ppermute x11, starting transfers between devices, swap(): return lax.ppermute(chunk, 'depth', CORE)  13.6 us
    ppermute x1, waiting for transfers between devices, on_device(): own[4] = lax.ppermute(mine, 'col', Y_LO)  10.9 us
    ppermute x1, waiting for transfers between devices, on_device(): away = lax.ppermute(shares, 'depth', Y_HI)  10.8 us
    ppermute x2, waiting for transfers between devices, across(): lax.ppermute(jnp.where(first, up, down), ('depth', 'col'), by_core(along_...  10.3 us
    ppermute x1, waiting for transfers between devices, on_device(): own[7] = lax.ppermute(own[4], 'col', along_x(1))  8.82 us
    ppermute x1, waiting for transfers between devices, on_device(): passed = lax.ppermute(total[:, part:].astype(bf16), 'col', Y_LO)  7.74 us
  transfers between devices with their start and end apart: 25, of which 13 were waited for; matrix products, arithmetic and copies ran while one was open for 2% of the time, Pallas kernels for 6%

profile of v5, /device:TPU:1, one launch (start us, length us, event | category | flops | bytes accessed | tf_op | source)
XLA Modules:
  0.0 167.0 jit_solution(4589958935486850816)
XLA Ops:
  7.8 2.1 %shard_map.67 = bf16[1024,256]{1,0:T(8,128)(2,1)} custom-call(s32[3]{0:T(128)} %pad_add_fusion.place, bf16[256,1024]{1,0:T(8,128)(2,1)} %weight_in.1, bf16[1024,256]{1,0:T(8,128)(2,1)} %weight_out.1), custom_call_target="tpu_custom_call" | custom-call | tf_op jit(solution)/shard_map/pallas_call | solution.py:68
  10.0 2.0 %shard_map.68.refs_0_ = bf16[640,512]{1,0:T(8,128)(2,1)} custom-call(bf16[640,256]{1,0:T(8,128)(2,1)} %activations.1, bf16[640,256]{1,0:T(8,128)(2,1)} %upstream), custom_call_target="tpu_custom_call" | custom-call | tf_op jit(solution)/shard_map/pallas_call | solution.py:85
  11.9 2.1 %collective-permute-start.1 = (bf16[640,512]{1,0:T(8,128)(2,1)}, bf16[640,512]{1,0:T(8,128)(2,1)S(1)}, u32[]{:S(2)}, u32[]{:S(2)}) collective-permute-start(bf16[640,512]{1,0:T(8,128)(2,1)} %shard_map.68.refs_0_), channel_id=1, source_target_pairs={{0,4},{1,5},{2,6},{3,7},{4,0},{5,1},{6,2},{7,3},{8,12},{9,13},{10,... | collective-permute-start | bytes 1966088 | tf_op jit(solution)/shard_map/ppermute | solution.py:324
  15.3 1.5 collective-permute-start
  16.7 10.9 %collective-permute-done.1.refs_4_ = bf16[640,512]{1,0:T(8,128)(2,1)S(1)} collective-permute-done((bf16[640,512]{1,0:T(8,128)(2,1)}, bf16[640,512]{1,0:T(8,128)(2,1)S(1)}, u32[]{:S(2)}, u32[]{:S(2)}) %collective-permute-start.1) | collective-permute-done | bytes 655392 | tf_op jit(solution)/shard_map/ppermute | solution.py:324
  27.6 2.3 %collective-permute-start.5 = (bf16[640,512]{1,0:T(8,128)(2,1)S(1)}, bf16[640,512]{1,0:T(8,128)(2,1)S(1)}, u32[]{:S(2)}, u32[]{:S(2)}) collective-permute-start(bf16[640,512]{1,0:T(8,128)(2,1)S(1)} %collective-permute-done.1.refs_4_), channel_id=1, source_target_pairs={{0,1},{1,2},{2,3},{3,0},{4,5},{5,6},{6,7},{7,4},{8,9},{9,10},{10,1... | collective-permute-start | bytes 1966088 | tf_op jit(solution)/shard_map/ppermute | solution.py:327
  31.2 2.0 %collective-permute-start.7 = (bf16[640,512]{1,0:T(8,128)(2,1)}, bf16[640,512]{1,0:T(8,128)(2,1)}, u32[]{:S(2)}, u32[]{:S(2)}) collective-permute-start(bf16[640,512]{1,0:T(8,128)(2,1)} %shard_map.68.refs_0_), channel_id=1, source_target_pairs={{0,64},{64,0},{128,192},{192,128},{1,65},{65,1},{129,193},{193,129... | collective-permute-start | bytes 1966088 | tf_op jit(solution)/shard_map/ppermute | solution.py:310
  33.5 2.2 %collective-permute-start.8 = (bf16[640,512]{1,0:T(8,128)(2,1)S(1)}, bf16[640,512]{1,0:T(8,128)(2,1)S(1)}, u32[]{:S(2)}, u32[]{:S(2)}) collective-permute-start(bf16[640,512]{1,0:T(8,128)(2,1)S(1)} %collective-permute-done.refs_1_), channel_id=1, source_target_pairs={{0,64},{64,0},{128,192},{192,128},{1,65},{65,1},{129,193},{193,129... | collective-permute-start | bytes 1966088 | tf_op jit(solution)/shard_map/ppermute | solution.py:310
  35.7 8.8 %collective-permute-done.5.refs_7_ = bf16[640,512]{1,0:T(8,128)(2,1)S(1)} collective-permute-done((bf16[640,512]{1,0:T(8,128)(2,1)S(1)}, bf16[640,512]{1,0:T(8,128)(2,1)S(1)}, u32[]{:S(2)}, u32[]{:S(2)}) %collective-permute-start.5) | collective-permute-done | bytes 655392 | tf_op jit(solution)/shard_map/ppermute | solution.py:327
  44.6 4.3 %collective-permute-start.10 = (bf16[640,512]{1,0:T(8,128)(2,1)S(1)}, bf16[640,512]{1,0:T(8,128)(2,1)S(1)}, u32[]{:S(2)}, u32[]{:S(2)}) collective-permute-start(bf16[640,512]{1,0:T(8,128)(2,1)S(1)} %collective-permute-done.2.refs_3_), channel_id=1, source_target_pairs={{0,64},{64,0},{128,192},{192,128},{1,65},{65,1},{129,193},{193,129... | collective-permute-start | bytes 1966088 | tf_op jit(solution)/shard_map/ppermute | solution.py:310
  49.2 4.4 %collective-permute-done.3.refs_2_ = bf16[640,512]{1,0:T(8,128)(2,1)S(1)} collective-permute-done((bf16[640,512]{1,0:T(8,128)(2,1)S(1)}, bf16[640,512]{1,0:T(8,128)(2,1)S(1)}, u32[]{:S(2)}, u32[]{:S(2)}) %collective-permute-start.3) | collective-permute-done | bytes 655392 | tf_op jit(solution)/shard_map/ppermute | solution.py:313
  54.7 5.9 %collective-permute-done.6.refs_6_ = bf16[640,512]{1,0:T(8,128)(2,1)S(1)} collective-permute-done((bf16[640,512]{1,0:T(8,128)(2,1)S(1)}, bf16[640,512]{1,0:T(8,128)(2,1)S(1)}, u32[]{:S(2)}, u32[]{:S(2)}) %collective-permute-start.6) | collective-permute-done | bytes 655392 | tf_op jit(solution)/shard_map/ppermute | solution.py:313
  63.2 5.4 %all-gather.3.cloned.1.call-done = bf16[8192,256]{1,0:T(8,128)(2,1)} async-done(((bf16[1024,256]{1,0:T(8,128)(2,1)}), bf16[8192,256]{1,0:T(8,128)(2,1)}) %all-gather.3.cloned.1.call-update) | async-done | bytes 4194320 | tf_op jit(solution)/shard_map/all_gather | solution.py:318
  68.7 17.5 %shard_map.69 = (bf16[1280,512]{1,0:T(8,128)(2,1)S(1)}, bf16[8,1024,256]{2,1,0:T(8,128)(2,1)}) custom-call(s32[3]{0:T(128)} %pad_add_fusion.place, bf16[640,512]{1,0:T(8,128)(2,1)} %shard_map.68.refs_0_, bf16[640,512]{1,0:T(8,128)(2,1)} %copy-done.2, bf16[640,512]{1,0:T(8,128)(2,1)} %copy-done.6, bf16[640,512]{1,0:T(8,128)(2,1)} %copy-done.1, ...), custom_call_target="tpu_custom_call" | custom-call | flops 10737418240 | bytes 23068672 | tf_op jit(solution)/shard_map/pallas_call | solution.py:201
  86.8 3.8 %shard_map.71 = bf16[4,640,512]{2,1,0:T(8,128)(2,1)S(1)} custom-call(s32[3]{0:T(128)S(1)} %copy-done, bf16[1280,512]{1,0:T(8,128)(2,1)S(1)} %get-tuple-element.24.dpre, bf16[8,1024,256]{2,1,0:T(8,128)(2,1)} %bitcast.17), custom_call_target="tpu_custom_call" | custom-call | flops 1342177280 | bytes 5373952 | tf_op jit(solution)/shard_map/pallas_call | solution.py:249
  91.6 3.8 %shard_map.70 = bf16[4,640,512]{2,1,0:T(8,128)(2,1)S(1)} custom-call(s32[3]{0:T(128)S(1)} %copy-done, bf16[1280,512]{1,0:T(8,128)(2,1)S(1)} %get-tuple-element.24.dpre, bf16[8,1024,256]{2,1,0:T(8,128)(2,1)} %bitcast.18), custom_call_target="tpu_custom_call" | custom-call | flops 1342177280 | bytes 5373952 | tf_op jit(solution)/shard_map/pallas_call | solution.py:249
  97.2 2.8 %collective-permute-start.16 = (bf16[640,512]{1,0:T(8,128)(2,1)S(1)}, bf16[640,512]{1,0:T(8,128)(2,1)S(1)}, u32[]{:S(2)}, u32[]{:S(2)}) collective-permute-start(bf16[640,512]{1,0:T(8,128)(2,1)S(1)} %get-tuple-element.29), channel_id=1, source_target_pairs={{0,2},{1,3},{2,0},{3,1},{4,6},{5,7},{6,4},{7,5},{8,10},{9,11},{10,... | collective-permute-start | bytes 1966088 | tf_op jit(solution)/shard_map/ppermute | solution.py:342
  101.4 13.3 %collective-permute-done.16 = bf16[640,512]{1,0:T(8,128)(2,1)S(1)} collective-permute-done((bf16[640,512]{1,0:T(8,128)(2,1)S(1)}, bf16[640,512]{1,0:T(8,128)(2,1)S(1)}, u32[]{:S(2)}, u32[]{:S(2)}) %collective-permute-start.16) | collective-permute-done | bytes 655392 | tf_op jit(solution)/shard_map/ppermute | solution.py:342
  114.8 14.2 %collective-permute-done.18 = bf16[640,512]{1,0:T(8,128)(2,1)S(1)} collective-permute-done((bf16[640,512]{1,0:T(8,128)(2,1)S(1)}, bf16[640,512]{1,0:T(8,128)(2,1)S(1)}, u32[]{:S(2)}, u32[]{:S(2)}) %collective-permute-start.18) | collective-permute-done | bytes 655392 | tf_op jit(solution)/shard_map/ppermute | solution.py:342
  131.3 7.7 %collective-permute-done.19 = bf16[640,256]{1,0:T(8,128)(2,1)S(1)} collective-permute-done((bf16[640,256]{1,0:T(8,128)(2,1)S(1)}, bf16[640,256]{1,0:T(8,128)(2,1)S(1)}, u32[]{:S(2)}, u32[]{:S(2)}) %collective-permute-start.19) | collective-permute-done | bytes 327712 | tf_op jit(solution)/shard_map/ppermute | solution.py:344
  140.3 2.7 %collective-permute-start.20 = (bf16[1024,256]{1,0:T(8,128)(2,1)}, bf16[1024,256]{1,0:T(8,128)(2,1)S(1)}, u32[]{:S(2)}, u32[]{:S(2)}) collective-permute-start(bf16[1024,256]{1,0:T(8,128)(2,1)} %bitcast.19), channel_id=1, source_target_pairs={{0,128},{64,192},{128,0},{192,64},{1,129},{65,193},{129,1},{193,65... | collective-permute-start | bytes 1572872 | tf_op jit(solution)/shard_map/ppermute | solution.py:348
  144.0 10.8 %collective-permute-done.20 = bf16[1024,256]{1,0:T(8,128)(2,1)S(1)} collective-permute-done((bf16[1024,256]{1,0:T(8,128)(2,1)}, bf16[1024,256]{1,0:T(8,128)(2,1)S(1)}, u32[]{:S(2)}, u32[]{:S(2)}) %collective-permute-start.20) | collective-permute-done | bytes 524320 | tf_op jit(solution)/shard_map/ppermute | solution.py:348
  154.8 1.6 collective-permute-start.22
  157.9 2.2 %shard_map.72 = (f32[256,1024]{1,0:T(8,128)}, f32[1024,256]{1,0:T(8,128)}) custom-call(s32[3]{0:T(128)S(1)} %copy-done, f32[1024,256]{1,0:T(8,128)S(1)} %convert_add_fusion.1.here, bf16[1024,256]{1,0:T(8,128)(2,1)S(1)} %collective-permute-done.21.other_share, bf16[1024,256]{1,0:T(8,128)(2,1)S(1)} %collective-permute-done.22.other_away), custom_call_target="tpu_custom_call" | custom-call | tf_op jit(solution)/shard_map/pallas_call | solution.py:283
  (71 shorter events, 18.4 us)
Async XLA Ops:
  7.2 61.5 %all-gather.3.cloned.1.call-start = ((), (), s32[]{:S(2)}) async-start(), calls=%async_computation.2 | async-start | bytes 4718592 | tf_op jit(solution)/shard_map/all_gather | solution.py:318
  9.9 130.4 %reduce-scatter.2.cloned.1.call-start = ((), (), s32[]{:S(2)}) async-start(), calls=%async_computation.1 | async-start | bytes 4718592 | tf_op jit(solution)/shard_map/reduce_scatter | solution.py:339
  11.9 15.7 %collective-permute-start.1 = (bf16[640,512]{1,0:T(8,128)(2,1)}, bf16[640,512]{1,0:T(8,128)(2,1)S(1)}, u32[]{:S(2)}, u32[]{:S(2)}) collective-permute-start(bf16[640,512]{1,0:T(8,128)(2,1)} %shard_map.68.refs_0_), channel_id=1, source_target_pairs={{0,4},{1,5},{2,6},{3,7},{4,0},{5,1},{6,2},{7,3},{8,12},{9,13},{10,... | collective-permute-start | bytes 1966088 | tf_op jit(solution)/shard_map/ppermute | solution.py:324
  14.1 19.1 %collective-permute-start.2 = (bf16[640,512]{1,0:T(8,128)(2,1)}, bf16[640,512]{1,0:T(8,128)(2,1)S(1)}, u32[]{:S(2)}, u32[]{:S(2)}) collective-permute-start(bf16[640,512]{1,0:T(8,128)(2,1)} %shard_map.68.refs_0_), channel_id=1, source_target_pairs={{0,1},{1,2},{2,3},{3,0},{4,5},{5,6},{6,7},{7,4},{8,9},{9,10},{10,1... | collective-permute-start | bytes 1966088 | tf_op jit(solution)/shard_map/ppermute | solution.py:323
  15.3 17.9 %collective-permute-start = (bf16[640,512]{1,0:T(8,128)(2,1)}, bf16[640,512]{1,0:T(8,128)(2,1)S(1)}, u32[]{:S(2)}, u32[]{:S(2)}) collective-permute-start(bf16[640,512]{1,0:T(8,128)(2,1)} %shard_map.68.refs_0_), channel_id=1, source_target_pairs={{0,3},{1,0},{2,1},{3,2},{4,7},{5,4},{6,5},{7,6},{8,11},{9,8},{10,9... | collective-permute-start | bytes 1966088 | tf_op jit(solution)/shard_map/ppermute | solution.py:322
  27.6 17.0 %collective-permute-start.5 = (bf16[640,512]{1,0:T(8,128)(2,1)S(1)}, bf16[640,512]{1,0:T(8,128)(2,1)S(1)}, u32[]{:S(2)}, u32[]{:S(2)}) collective-permute-start(bf16[640,512]{1,0:T(8,128)(2,1)S(1)} %collective-permute-done.1.refs_4_), channel_id=1, source_target_pairs={{0,1},{1,2},{2,3},{3,0},{4,5},{5,6},{6,7},{7,4},{8,9},{9,10},{10,1... | collective-permute-start | bytes 1966088 | tf_op jit(solution)/shard_map/ppermute | solution.py:327
  29.9 18.9 %collective-permute-start.4 = (bf16[640,512]{1,0:T(8,128)(2,1)S(1)}, bf16[640,512]{1,0:T(8,128)(2,1)S(1)}, u32[]{:S(2)}, u32[]{:S(2)}) collective-permute-start(bf16[640,512]{1,0:T(8,128)(2,1)S(1)} %collective-permute-done.1.refs_4_), channel_id=1, source_target_pairs={{0,3},{1,0},{2,1},{3,2},{4,7},{5,4},{6,5},{7,6},{8,11},{9,8},{10,9... | collective-permute-start | bytes 1966088 | tf_op jit(solution)/shard_map/ppermute | solution.py:326
  31.2 22.9 %collective-permute-start.7 = (bf16[640,512]{1,0:T(8,128)(2,1)}, bf16[640,512]{1,0:T(8,128)(2,1)}, u32[]{:S(2)}, u32[]{:S(2)}) collective-permute-start(bf16[640,512]{1,0:T(8,128)(2,1)} %shard_map.68.refs_0_), channel_id=1, source_target_pairs={{0,64},{64,0},{128,192},{192,128},{1,65},{65,1},{129,193},{193,129... | collective-permute-start | bytes 1966088 | tf_op jit(solution)/shard_map/ppermute | solution.py:310
  33.3 20.3 %collective-permute-start.3 = (bf16[640,512]{1,0:T(8,128)(2,1)S(1)}, bf16[640,512]{1,0:T(8,128)(2,1)S(1)}, u32[]{:S(2)}, u32[]{:S(2)}) collective-permute-start(bf16[640,512]{1,0:T(8,128)(2,1)S(1)} %broadcast_select_fusion.1), channel_id=1, source_target_pairs={{0,3},{1,0},{2,1},{3,2},{4,7},{5,4},{6,5},{7,6},{64,65},{65,66},{6... | collective-permute-start | bytes 1966088 | tf_op jit(solution)/shard_map/ppermute | solution.py:313
  33.5 20.6 %collective-permute-start.8 = (bf16[640,512]{1,0:T(8,128)(2,1)S(1)}, bf16[640,512]{1,0:T(8,128)(2,1)S(1)}, u32[]{:S(2)}, u32[]{:S(2)}) collective-permute-start(bf16[640,512]{1,0:T(8,128)(2,1)S(1)} %collective-permute-done.refs_1_), channel_id=1, source_target_pairs={{0,64},{64,0},{128,192},{192,128},{1,65},{65,1},{129,193},{193,129... | collective-permute-start | bytes 1966088 | tf_op jit(solution)/shard_map/ppermute | solution.py:310
  44.6 10.0 %collective-permute-start.10 = (bf16[640,512]{1,0:T(8,128)(2,1)S(1)}, bf16[640,512]{1,0:T(8,128)(2,1)S(1)}, u32[]{:S(2)}, u32[]{:S(2)}) collective-permute-start(bf16[640,512]{1,0:T(8,128)(2,1)S(1)} %collective-permute-done.2.refs_3_), channel_id=1, source_target_pairs={{0,64},{64,0},{128,192},{192,128},{1,65},{65,1},{129,193},{193,129... | collective-permute-start | bytes 1966088 | tf_op jit(solution)/shard_map/ppermute | solution.py:310
  48.9 11.7 %collective-permute-start.6 = (bf16[640,512]{1,0:T(8,128)(2,1)S(1)}, bf16[640,512]{1,0:T(8,128)(2,1)S(1)}, u32[]{:S(2)}, u32[]{:S(2)}) collective-permute-start(bf16[640,512]{1,0:T(8,128)(2,1)S(1)} %broadcast_select_fusion), channel_id=1, source_target_pairs={{0,3},{1,0},{2,1},{3,2},{4,7},{5,4},{6,5},{7,6},{64,65},{65,66},{6... | collective-permute-start | bytes 1966088 | tf_op jit(solution)/shard_map/ppermute | solution.py:313
  53.6 7.5 %collective-permute-start.11 = (bf16[640,512]{1,0:T(8,128)(2,1)S(1)}, bf16[640,512]{1,0:T(8,128)(2,1)S(1)}, u32[]{:S(2)}, u32[]{:S(2)}) collective-permute-start(bf16[640,512]{1,0:T(8,128)(2,1)S(1)} %collective-permute-done.1.refs_4_), channel_id=1, source_target_pairs={{0,64},{64,0},{128,192},{192,128},{1,65},{65,1},{129,193},{193,129... | collective-permute-start | bytes 1966088 | tf_op jit(solution)/shard_map/ppermute | solution.py:310
  54.1 7.0 %collective-permute-start.12 = (bf16[640,512]{1,0:T(8,128)(2,1)S(1)}, bf16[640,512]{1,0:T(8,128)(2,1)S(1)}, u32[]{:S(2)}, u32[]{:S(2)}) collective-permute-start(bf16[640,512]{1,0:T(8,128)(2,1)S(1)} %collective-permute-done.4.refs_5_), channel_id=1, source_target_pairs={{0,64},{64,0},{128,192},{192,128},{1,65},{65,1},{129,193},{193,129... | collective-permute-start | bytes 1966088 | tf_op jit(solution)/shard_map/ppermute | solution.py:310
  54.2 6.9 %collective-permute-start.14 = (bf16[640,512]{1,0:T(8,128)(2,1)S(1)}, bf16[640,512]{1,0:T(8,128)(2,1)S(1)}, u32[]{:S(2)}, u32[]{:S(2)}) collective-permute-start(bf16[640,512]{1,0:T(8,128)(2,1)S(1)} %collective-permute-done.5.refs_7_), channel_id=1, source_target_pairs={{0,64},{64,0},{128,192},{192,128},{1,65},{65,1},{129,193},{193,129... | collective-permute-start | bytes 1966088 | tf_op jit(solution)/shard_map/ppermute | solution.py:310
  54.6 6.6 %collective-permute-start.9 = (bf16[640,512]{1,0:T(8,128)(2,1)S(1)}, bf16[640,512]{1,0:T(8,128)(2,1)S(1)}, u32[]{:S(2)}, u32[]{:S(2)}) collective-permute-start(bf16[640,512]{1,0:T(8,128)(2,1)S(1)} %collective-permute-done.3.refs_2_), channel_id=1, source_target_pairs={{0,64},{64,0},{128,192},{192,128},{1,65},{65,1},{129,193},{193,129... | collective-permute-start | bytes 1966088 | tf_op jit(solution)/shard_map/ppermute | solution.py:310
  90.7 5.5 %collective-permute-start.15 = (bf16[4,640,512]{2,1,0:T(8,128)(2,1)S(1)}, bf16[4,640,512]{2,1,0:T(8,128)(2,1)S(1)}, u32[]{:S(2)}, u32[]{:S(2)}) collective-permute-start(bf16[4,640,512]{2,1,0:T(8,128)(2,1)S(1)} %shard_map.71), channel_id=1, source_target_pairs={{0,64},{64,0},{128,192},{192,128},{1,65},{65,1},{129,193},{193,129... | collective-permute-start | bytes 7864328 | tf_op jit(solution)/shard_map/ppermute | solution.py:310
  97.2 17.6 %collective-permute-start.16 = (bf16[640,512]{1,0:T(8,128)(2,1)S(1)}, bf16[640,512]{1,0:T(8,128)(2,1)S(1)}, u32[]{:S(2)}, u32[]{:S(2)}) collective-permute-start(bf16[640,512]{1,0:T(8,128)(2,1)S(1)} %get-tuple-element.29), channel_id=1, source_target_pairs={{0,2},{1,3},{2,0},{3,1},{4,6},{5,7},{6,4},{7,5},{8,10},{9,11},{10,... | collective-permute-start | bytes 1966088 | tf_op jit(solution)/shard_map/ppermute | solution.py:342
  100.0 29.0 %collective-permute-start.18 = (bf16[640,512]{1,0:T(8,128)(2,1)S(1)}, bf16[640,512]{1,0:T(8,128)(2,1)S(1)}, u32[]{:S(2)}, u32[]{:S(2)}) collective-permute-start(bf16[640,512]{1,0:T(8,128)(2,1)S(1)} %get-tuple-element.30), channel_id=1, source_target_pairs={{0,3},{1,0},{2,1},{3,2},{4,7},{5,4},{6,5},{7,6},{8,11},{9,8},{10,9... | collective-permute-start | bytes 1966088 | tf_op jit(solution)/shard_map/ppermute | solution.py:342
  100.9 28.7 %collective-permute-start.17 = (bf16[640,512]{1,0:T(8,128)(2,1)S(1)}, bf16[640,512]{1,0:T(8,128)(2,1)S(1)}, u32[]{:S(2)}, u32[]{:S(2)}) collective-permute-start(bf16[640,512]{1,0:T(8,128)(2,1)S(1)} %get-tuple-element.31), channel_id=1, source_target_pairs={{0,1},{1,2},{2,3},{3,0},{4,5},{5,6},{6,7},{7,4},{8,9},{9,10},{10,1... | collective-permute-start | bytes 1966088 | tf_op jit(solution)/shard_map/ppermute | solution.py:342
  130.0 9.0 %collective-permute-start.19 = (bf16[640,256]{1,0:T(8,128)(2,1)S(1)}, bf16[640,256]{1,0:T(8,128)(2,1)S(1)}, u32[]{:S(2)}, u32[]{:S(2)}) collective-permute-start(bf16[640,256]{1,0:T(8,128)(2,1)S(1)} %slice.41), channel_id=1, source_target_pairs={{0,4},{1,5},{2,6},{3,7},{4,0},{5,1},{6,2},{7,3},{8,12},{9,13},{10,... | collective-permute-start | bytes 983048 | tf_op jit(solution)/shard_map/ppermute | solution.py:344
  140.3 14.5 %collective-permute-start.20 = (bf16[1024,256]{1,0:T(8,128)(2,1)}, bf16[1024,256]{1,0:T(8,128)(2,1)S(1)}, u32[]{:S(2)}, u32[]{:S(2)}) collective-permute-start(bf16[1024,256]{1,0:T(8,128)(2,1)} %bitcast.19), channel_id=1, source_target_pairs={{0,128},{64,192},{128,0},{192,64},{1,129},{65,193},{129,1},{193,65... | collective-permute-start | bytes 1572872 | tf_op jit(solution)/shard_map/ppermute | solution.py:348
  143.1 14.5 %collective-permute-start.21 = (bf16[1024,256]{1,0:T(8,128)(2,1)}, bf16[1024,256]{1,0:T(8,128)(2,1)S(1)}, u32[]{:S(2)}, u32[]{:S(2)}) collective-permute-start(bf16[1024,256]{1,0:T(8,128)(2,1)} %bitcast.20), channel_id=1, source_target_pairs={{0,64},{64,0},{128,192},{192,128},{1,65},{65,1},{129,193},{193,129... | collective-permute-start | bytes 1572872 | tf_op jit(solution)/shard_map/ppermute | solution.py:310
  154.8 3.1 %collective-permute-start.22 = (bf16[1024,256]{1,0:T(8,128)(2,1)S(1)}, bf16[1024,256]{1,0:T(8,128)(2,1)S(1)}, u32[]{:S(2)}, u32[]{:S(2)}) collective-permute-start(bf16[1024,256]{1,0:T(8,128)(2,1)S(1)} %collective-permute-done.20), channel_id=1, source_target_pairs={{0,64},{64,0},{128,192},{192,128},{1,65},{65,1},{129,193},{193,129... | collective-permute-start | bytes 1572872 | tf_op jit(solution)/shard_map/ppermute | solution.py:310
  (15 other events, 185.3 us)
Sparse Core Ops, SparseCore 0:
  10.0 58.6 all-gather.2
  86.3 53.9 reduce-scatter.1
